TPU v7x, 512 devices: a whole 4x8x8 slice. The times are simulated.
512 devices in a mesh: grp: 32 (over x, z), tp: 16 (over y, core).
Axes of the slice: x: 4, y: 8, z: 8, core: 2. Of those that a mesh axis runs over, the one named last changes fastest.
Arguments:
- acts: bfloat16 [4096, 8192], P('grp', 'tp'), may hold values from -6 to 6
- grads: bfloat16 [4096, 4096], P('grp'), may hold values from -1.5 to 1.5
- counts: int32 [32, 24], P('grp'), may hold values from 1 to 12, 128 in all within a row
- owner_slot: int32 [24], replicated, may hold values from 0 to 31, as said below
- base_weight: bfloat16 [8192, 4096], P('tp', 'grp')
- adapter_a: bfloat16 [32, 8192, 32], P('grp', 'tp'), may hold values from -0.0625 to 0.0625
- adapter_b: bfloat16 [32, 32, 4096], P('grp'), may hold values from -0.59765625 to 0.59765625
- magnitude: float32 [32, 4096], P('grp'), may hold values from 0.5 to 2
Outputs:
- row_grad: bfloat16 [4096, 8192], P('grp', 'tp')
- grad_a: float32 [32, 8192, 32], P('grp', 'tp')
- grad_b: float32 [32, 32, 4096], P('grp', None, 'tp')
- grad_gain: float32 [32, 4096], P('grp')
Inputs may be any that keep to these rules, and one draw needn't show every extreme that they name: Every tenant has one row or more on every index of grp; the largest count in each row of counts is exactly 12. `owner_slot`: distinct slots, one for each tenant; slot p lies on index p // 1 of grp; other slots are unused.
All inputs are finite; a program needn't handle non-finite values.
Results may differ from a plain program's by a relative error of at most 0.0095.
Values may be sent and summed in bfloat16 or wider, within the bound.
No kernel may reach another device: no remote copies, remote signals or barrier semaphores. Data moves between devices by JAX's collectives and lax.ppermute only.
A program may use at most 64 MiB of HBM per device.

v0:
```python
import jax
import jax.numpy as jnp
from jax import lax
from jax.sharding import PartitionSpec as P

CAP = 12


PRECISE = lax.Precision.HIGHEST
EPSILON = 1e-06


def slot_layout(count_row, owner_slot, slot_total):
    row_ends = jnp.cumsum(count_row)
    row_starts = row_ends - count_row
    slot_ids = jnp.arange(slot_total, dtype=jnp.int32)
    matches = (owner_slot[None, :] == slot_ids[:, None]).astype(jnp.int32)
    slot_start = jnp.sum(matches * row_starts[None, :], axis=1)
    slot_rows = jnp.sum(matches * count_row[None, :], axis=1)
    return (row_starts, row_ends, slot_start, slot_rows)


def pack_rows(source, slot_start, slot_rows, capacity):
    offsets = jnp.arange(capacity, dtype=jnp.int32)
    valid = offsets[None, :] < slot_rows[:, None]
    gather_at = jnp.where(valid, slot_start[:, None] + offsets[None, :], 0).reshape(-1)
    return jnp.where(valid.reshape(-1)[:, None], source[gather_at], jnp.zeros((), source.dtype))


def column_terms(square_sum, align_sum, gain):
    column_norm = jnp.sqrt(square_sum + EPSILON)
    scale = gain / column_norm
    d_gain = align_sum / column_norm
    shrink = gain * align_sum / (column_norm * column_norm * column_norm)
    return (scale, d_gain, shrink)


def split_pair(values):
    upper = values.astype(jnp.bfloat16)
    lower = (values - upper.astype(jnp.float32)).astype(jnp.bfloat16)
    return (upper, lower)


def contract_rows(left, right, precise):
    dims = (((0,), (0,)), ((), ()))
    if precise:
        return lax.dot_general(left, right, dims, precision=PRECISE)
    return lax.dot_general(left, right, dims, preferred_element_type=jnp.float32)


def contract_cols(left, right, precise):
    dims = (((1,), (1,)), ((), ()))
    if precise:
        return lax.dot_general(left, right, dims, precision=PRECISE)
    return lax.dot_general(left, right, dims, preferred_element_type=jnp.float32)


def on_device(acts, grads, counts, owner_slot, base_weight, adapter_a, adapter_b, magnitude):
    groups = lax.axis_size("grp")
    slot_local = adapter_a.shape[0]
    capacity = CAP
    in_width = acts.shape[1]
    out_width = grads.shape[1]
    row_starts, row_ends, slot_start, slot_rows = slot_layout(
        counts[0], owner_slot, groups * slot_local
    )
    weight = lax.all_gather(base_weight, "grp", axis=1, tiled=True)
    x_send = pack_rows(acts, slot_start, slot_rows, capacity).reshape(
        groups, slot_local * capacity, in_width
    )
    g_send = pack_rows(grads, slot_start, slot_rows, capacity).reshape(
        groups, slot_local * capacity, out_width
    )
    x_recv, g_recv = (
        lax.all_to_all(x_send, "grp", split_axis=0, concat_axis=0, tiled=True),
        lax.all_to_all(g_send, "grp", split_axis=0, concat_axis=0, tiled=True),
    )
    x_slots = x_recv.reshape(groups, slot_local, capacity, in_width)
    g_slots = g_recv.reshape(groups, slot_local, capacity, out_width)
    square_base = jnp.sum(jnp.square(weight.astype(jnp.float32)), axis=0)
    slot_index = 0
    rows_in = x_slots[:, slot_index].reshape(groups * capacity, in_width)
    rows_grad = g_slots[:, slot_index].reshape(groups * capacity, out_width)
    first_wide = adapter_a[slot_index].astype(jnp.float32)
    second_wide = adapter_b[slot_index].astype(jnp.float32)
    projected = jnp.dot(rows_in, weight, preferred_element_type=jnp.float32)
    align_base = jnp.sum(rows_grad.astype(jnp.float32) * projected, axis=0)
    rows_low = jnp.dot(rows_in, adapter_a[slot_index], preferred_element_type=jnp.float32)
    low_upper, low_lower = split_pair(rows_low)
    first_moment = contract_rows(low_upper, rows_grad, False) + contract_rows(
        low_lower, rows_grad, False
    )
    first_weight = contract_rows(adapter_a[slot_index], weight, False)
    gram_matrix = contract_rows(first_wide, first_wide, True)
    gram_second = jnp.dot(gram_matrix, second_wide, precision=PRECISE)
    squares = [
        square_base
        + 2.0 * jnp.sum(first_weight * second_wide, axis=0)
        + jnp.sum(second_wide * gram_second, axis=0)
    ]
    aligns = [align_base + jnp.sum(first_moment * second_wide, axis=0)]
    saved = [(rows_in, rows_grad, first_wide, second_wide, first_weight, first_moment, gram_second)]
    square_all = jnp.stack(squares)
    align_all = jnp.stack(aligns)
    square_sum, align_sum = lax.psum((square_all, align_all), "tp")
    scale, d_gain, shrink = column_terms(square_sum, align_sum, magnitude)
    slot_index = 0
    rows_in, rows_grad, first_wide, second_wide, first_weight, first_moment, gram_second = saved[
        slot_index
    ]
    col_scale = scale[slot_index]
    col_shrink = shrink[slot_index]
    hidden = (rows_grad.astype(jnp.float32) * col_scale[None, :]).astype(jnp.bfloat16)
    main_part = contract_cols(hidden, weight, False)
    inner = contract_cols(hidden, adapter_b[slot_index], False).astype(jnp.bfloat16)
    low_part = contract_cols(inner, adapter_a[slot_index], False)
    returned = [(main_part + low_part).astype(jnp.bfloat16).reshape(groups, capacity, in_width)]
    scaled_second = second_wide * col_scale[None, :]
    shrunk_second = second_wide * col_shrink[None, :]
    scaled_upper, scaled_lower = split_pair(scaled_second)
    grad_rows = contract_cols(rows_grad, scaled_upper, False) + contract_cols(
        rows_grad, scaled_lower, False
    )
    rows_upper, rows_lower = split_pair(grad_rows)
    moment_part = contract_rows(rows_in, rows_upper, False) + contract_rows(
        rows_in, rows_lower, False
    )
    shrunk_upper, shrunk_lower = split_pair(shrunk_second)
    weight_part = contract_cols(weight, shrunk_upper, False) + contract_cols(
        weight, shrunk_lower, False
    )
    small_square = contract_cols(second_wide, shrunk_second, True)
    first_grads = [moment_part - weight_part - jnp.dot(first_wide, small_square, precision=PRECISE)]
    second_grads = [
        first_moment * col_scale[None, :]
        - first_weight * col_shrink[None, :]
        - gram_second * col_shrink[None, :]
    ]
    back_send = jnp.stack(returned, axis=1).reshape(groups, slot_local * capacity, in_width)
    back_recv = lax.all_to_all(back_send, "grp", split_axis=0, concat_axis=0, tiled=True)
    flat_back = back_recv.reshape(groups * slot_local * capacity, in_width)
    local_rows = jnp.arange(acts.shape[0], dtype=jnp.int32)
    row_tenant = jnp.sum((local_rows[:, None] >= row_ends[None, :]).astype(jnp.int32), axis=1)
    one_hot = (
        row_tenant[:, None] == jnp.arange(row_ends.shape[0], dtype=jnp.int32)[None, :]
    ).astype(jnp.int32)
    row_slot = jnp.sum(one_hot * owner_slot[None, :], axis=1)
    row_first = jnp.sum(one_hot * row_starts[None, :], axis=1)
    row_grad = flat_back[row_slot * capacity + local_rows - row_first]
    grad_b = lax.psum_scatter(jnp.stack(second_grads), "tp", scatter_dimension=2, tiled=True)
    return (row_grad, jnp.stack(first_grads), grad_b, d_gain)


def solution(mesh):
    in_specs = (
        P("grp", "tp"),
        P("grp", None),
        P("grp", None),
        P(),
        P("tp", "grp"),
        P("grp", "tp", None),
        P("grp", None, None),
        P("grp", None),
    )
    out_specs = (P("grp", "tp"), P("grp", "tp", None), P("grp", None, "tp"), P("grp", None))
    return jax.shard_map(
        on_device, mesh=mesh, in_specs=in_specs, out_specs=out_specs, check_vma=False
    )
```

profile of v0, /device:TPU:1, one launch (start us, length us, event | category | flops | bytes accessed | tf_op | source)
XLA Modules:
  0.0 294.2 jit_solution(140445028690227655)
XLA Ops:
  7.2 0.0 copy-start
  7.2 0.0 all-gather.2.cloned.1.call-start
  7.2 0.7 all-gather.2.cloned.1.call-update
  7.9 0.7 copy.14
  8.7 0.1 reduce
  8.8 0.7 fusion.59
  9.5 0.8 select_reduce_fusion.3
  10.2 0.1 add_select_fusion
  10.3 0.1 select_n.48
  10.5 3.0 %gather_fusion.2 = bf16[384,512]{1,0:T(8,128)(2,1)S(1)} fusion(bf16[128,512]{1,0:T(8,128)(2,1)} %param.8, s32[1024]{0:T(1024)S(1)} %pad_clamp_fusion.1), kind=kCustom, calls=%fused_computation.2 | custom fusion | bytes 787968 | tf_op jit(solution)/shard_map/gather | solution.py:27
  13.5 0.1 gather.17
  13.6 0.1 iota_compare_fusion
  13.7 0.9 broadcast_select_fusion.1
  14.6 13.7 %all-to-all-start.2 = ((bf16[32,12,512]{2,1,0:T(8,128)(2,1)}), bf16[32,12,512]{2,1,0:T(8,128)(2,1)S(1)}, u32[]{:S(2)}, u32[]{:S(2)}) async-start(bf16[32,12,512]{2,1,0:T(8,128)(2,1)} %broadcast_select_fusion.1), calls=%async_computation.2 | async-start | bytes 1048576 | tf_op jit(solution)/shard_map/all_to_all | solution.py:75
  28.3 0.0 copy-done
  28.3 4.1 %gather_fusion = bf16[384,4096]{1,0:T(8,128)(2,1)} fusion(bf16[128,4096]{1,0:T(8,128)(2,1)S(1)} %copy-done, s32[1024]{0:T(1024)S(1)} %pad_clamp_fusion.1), kind=kCustom, calls=%fused_computation | custom fusion | bytes 6292992 | tf_op jit(solution)/shard_map/gather | solution.py:27
  32.4 5.5 %gather.14 = bf16[32,12,4096]{2,1,0:T(8,128)(2,1)} reshape(bf16[384,4096]{1,0:T(8,128)(2,1)} %gather_fusion) | data formatting | bytes 6291456 | tf_op jit(solution)/shard_map/gather | solution.py:27
  37.9 4.5 %broadcast_select_fusion = bf16[32,12,4096]{2,1,0:T(8,128)(2,1)} fusion(bf16[32,12,4096]{2,1,0:T(8,128)(2,1)} %gather.14, pred[32,12]{1,0:T(8,128)(4,1)S(1)} %iota_compare_fusion), kind=kLoop, calls=%fused_computation.10 | loop fusion | flops 1572864 | bytes 6291840 | tf_op jit(solution)/shard_map/jit(_where)/select_n | solution.py:27
  42.4 0.8 all-to-all-done.2
  43.2 8.8 %all-to-all-start = ((bf16[32,12,4096]{2,1,0:T(8,128)(2,1)}), bf16[32,12,4096]{2,1,0:T(8,128)(2,1)}, u32[]{:S(2)}, u32[]{:S(2)}) async-start(bf16[32,12,4096]{2,1,0:T(8,128)(2,1)} %broadcast_select_fusion), calls=%async_computation | async-start | bytes 8388608 | tf_op jit(solution)/shard_map/all_to_all | solution.py:76
  51.9 0.0 reduce-scatter.2.cloned.1.call-start
  52.0 0.1 convert_reduce_fusion
  52.1 0.0 copy-done.9
  52.1 0.1 select_reduce_fusion.1
  52.2 0.1 fusion.46
  52.3 0.4 fusion.31
  52.7 0.1 reshape_squeeze_reshape.7
  52.8 0.2 fusion.43
  53.0 107.6 %all-to-all-done = bf16[32,12,4096]{2,1,0:T(8,128)(2,1)} async-done(((bf16[32,12,4096]{2,1,0:T(8,128)(2,1)}), bf16[32,12,4096]{2,1,0:T(8,128)(2,1)}, u32[]{:S(2)}, u32[]{:S(2)}) %all-to-all-start) | async-done | bytes 3145760 | tf_op jit(solution)/shard_map/all_to_all | solution.py:76
  160.6 5.6 %reshape_squeeze_reshape.6 = bf16[384,4096]{1,0:T(8,128)(2,1)} reshape(bf16[32,12,4096]{2,1,0:T(8,128)(2,1)} %all-to-all-done) | data formatting | bytes 6291456 | tf_op jit(solution)/shard_map/reshape;squeeze;reshape | solution.py:83
  166.2 2.5 fusion.52
  168.7 0.0 copy-start.1
  168.8 3.2 %fusion.48 = f32[32,4096]{1,0:T(8,128)S(1)} fusion(bf16[512,4096]{1,0:T(8,128)(2,1)} %all-gather.2.cloned.1.call-done, bf16[1,512,32]{1,2,0:T(8,128)(2,1)S(1)} %copy-done.7), kind=kOutput, calls=%fused_computation.64 | convolution fusion | flops 134217728 | bytes 4751360 | tf_op jit(solution)/shard_map/dot_general | solution.py:48
  171.9 0.0 copy-done.1
  171.9 1.6 fusion.21
  173.6 1.8 fusion.1
  175.4 0.0 copy-start.8
  175.4 0.9 multiply_reduce_fusion
  176.3 51.5 %all-reduce = (f32[1,4096]{1,0:T(1,128)S(1)}, f32[1,4096]{1,0:T(1,128)S(1)}) all-reduce(f32[1,4096]{1,0:T(1,128)S(1)} %bitcast.100, f32[1,4096]{1,0:T(1,128)S(1)} %bitcast.99), channel_id=1, replica_groups=mesh['grp'=32,'tp'=16] {'tp'}, use_global_device_ids=true, to_apply=%region_6.7 | all-reduce | flops 8192 | bytes 65536 | tf_op jit(solution)/shard_map/psum | solution.py:105
  227.8 0.7 fusion.60
  228.5 2.9 fusion.25
  231.4 0.4 fusion.17
  231.8 0.0 copy-done.6
  231.9 0.9 subtract_bitcast_fusion
  232.7 0.0 reduce-scatter.2.cloned.1.call-update
  232.8 5.3 %multiply_convert_fusion = bf16[32,12,4096]{2,1,0:T(8,128)(2,1)} fusion(bf16[32,12,4096]{2,1,0:T(8,128)(2,1)} %all-to-all-done, f32[4096]{0:T(1024)S(1)} %bitcast.92), kind=kLoop, calls=%fused_computation.3 | loop fusion | flops 4718592 | bytes 6307840 | tf_op jit(solution)/shard_map/convert_element_type | solution.py:113
  238.0 5.6 %convert_element_type.88 = bf16[384,4096]{1,0:T(8,128)(2,1)} reshape(bf16[32,12,4096]{2,1,0:T(8,128)(2,1)} %multiply_convert_fusion) | data formatting | bytes 6291456 | tf_op jit(solution)/shard_map/convert_element_type | solution.py:113
  243.6 5.0 %fusion.2 = f32[384,512]{1,0:T(8,128)S(1)} fusion(bf16[512,4096]{1,0:T(8,128)(2,1)} %all-gather.2.cloned.1.call-done, bf16[384,4096]{1,0:T(8,128)(2,1)} %reshape_squeeze_reshape.6, f32[4096]{0:T(1024)S(1)} %bitcast.93), kind=kOutput, calls=%fused_computation.11 | convolution fusion | flops 1615331328 | bytes 8142848 | tf_op jit(solution)/shard_map/dot_general | solution.py:55
  248.6 3.4 %fusion.5 = bf16[384,512]{1,0:T(8,128)(2,1)S(1)} fusion(f32[384,512]{1,0:T(8,128)S(1)} %fusion.2, bf16[384,4096]{1,0:T(8,128)(2,1)} %convert_element_type.88, bf16[1,32,4096]{2,1,0:T(8,128)(2,1)S(1)} %copy-done.5, bf16[1,512,32]{1,2,0:T(8,128)(2,1)S(1)} %copy-done.7), kind=kOutput, calls=%fused_computation.14 | convolution fusion | flops 113651712 | bytes 4620288 | tf_op jit(solution)/shard_map/dot_general | solution.py:55
  252.0 0.9 reshape_stack_reshape.3
  252.9 4.2 %all-to-all-start.1 = ((bf16[32,12,512]{2,1,0:T(8,128)(2,1)}), bf16[32,12,512]{2,1,0:T(8,128)(2,1)S(1)}, u32[]{:S(2)}, u32[]{:S(2)}) async-start(bf16[32,12,512]{2,1,0:T(8,128)(2,1)} %reshape_stack_reshape.3), calls=%async_computation.1 | async-start | bytes 1048576 | tf_op jit(solution)/shard_map/all_to_all | solution.py:140
  257.1 0.0 copy-start.2
  257.1 0.0 copy-start.4
  257.1 3.7 %fusion.34 = f32[32,512]{1,0:T(8,128)S(1)} fusion(bf16[512,4096]{1,0:T(8,128)(2,1)} %all-gather.2.cloned.1.call-done, bf16[1,32,4096]{2,1,0:T(8,128)(2,1)S(1)} %copy-done.5, f32[4096]{0:T(1024)S(1)} %bitcast.97), kind=kOutput, calls=%fused_computation.51 | convolution fusion | flops 134610944 | bytes 4538368 | tf_op jit(solution)/shard_map/dot_general | solution.py:55
  260.8 0.0 copy-done.2
  260.8 1.1 convolution_add_fusion.4
  261.9 0.2 fusion.55
  262.1 1.4 fusion.9
  263.4 0.2 fusion.8
  263.6 0.8 fusion.7
  264.4 4.3 %all-to-all-done.1 = bf16[32,12,512]{2,1,0:T(8,128)(2,1)S(1)} async-done(((bf16[32,12,512]{2,1,0:T(8,128)(2,1)}), bf16[32,12,512]{2,1,0:T(8,128)(2,1)S(1)}, u32[]{:S(2)}, u32[]{:S(2)}) %all-to-all-start.1) | async-done | bytes 393248 | tf_op jit(solution)/shard_map/all_to_all | solution.py:140
  268.8 0.1 reshape.201
  268.9 1.5 gather_fusion.1
  270.4 17.0 %reduce-scatter.2.cloned.1.call-done = f32[1,32,256]{2,1,0:T(8,128)} async-done(((f32[1,32,4096]{2,1,0:T(8,128)}), f32[1,32,256]{2,1,0:T(8,128)}) %reduce-scatter.2.cloned.1.call-update) | async-done | bytes 32784 | tf_op jit(solution)/shard_map/reduce_scatter | solution.py:150
  (18 shorter events, 0.1 us)
Async XLA Ops:
  7.2 21.1 %copy-start = (bf16[128,4096]{1,0:T(8,128)(2,1)S(1)}, bf16[128,4096]{1,0:T(8,128)(2,1)}, u32[]{:S(2)}) copy-start(bf16[128,4096]{1,0:T(8,128)(2,1)} %param.9) | copy-start | bytes 3145732
  7.2 161.6 %all-gather.2.cloned.1.call-start = ((), (), s32[]{:S(2)}) async-start(), calls=%async_computation.4 | async-start | bytes 4325376 | tf_op jit(solution)/shard_map/all_gather | solution.py:67
  14.6 28.6 %all-to-all-start.2 = ((bf16[32,12,512]{2,1,0:T(8,128)(2,1)}), bf16[32,12,512]{2,1,0:T(8,128)(2,1)S(1)}, u32[]{:S(2)}, u32[]{:S(2)}) async-start(bf16[32,12,512]{2,1,0:T(8,128)(2,1)} %broadcast_select_fusion.1), calls=%async_computation.2 | async-start | bytes 1048576 | tf_op jit(solution)/shard_map/all_to_all | solution.py:75
  42.4 9.7 %copy-start.9 = (s32[24]{0:T(128)S(1)}, s32[24]{0:T(128)}, u32[]{:S(2)}) copy-start(s32[24]{0:T(128)} %param.11) | copy-start | bytes 292
  42.4 9.8 %copy-start.7 = (bf16[1,512,32]{1,2,0:T(8,128)(2,1)S(1)}, bf16[1,512,32]{1,2,0:T(8,128)(2,1)}, u32[]{:S(2)}) copy-start(bf16[1,512,32]{1,2,0:T(8,128)(2,1)} %param.13) | copy-start | bytes 98308
  42.4 9.9 %copy-start.5 = (bf16[1,32,4096]{2,1,0:T(8,128)(2,1)S(1)}, bf16[1,32,4096]{2,1,0:T(8,128)(2,1)}, u32[]{:S(2)}) copy-start(bf16[1,32,4096]{2,1,0:T(8,128)(2,1)} %param.14) | copy-start | bytes 786436
  43.2 117.5 %all-to-all-start = ((bf16[32,12,4096]{2,1,0:T(8,128)(2,1)}), bf16[32,12,4096]{2,1,0:T(8,128)(2,1)}, u32[]{:S(2)}, u32[]{:S(2)}) async-start(bf16[32,12,4096]{2,1,0:T(8,128)(2,1)} %broadcast_select_fusion), calls=%async_computation | async-start | bytes 8388608 | tf_op jit(solution)/shard_map/all_to_all | solution.py:76
  51.9 235.4 %reduce-scatter.2.cloned.1.call-start = ((), (), s32[]{:S(2)}) async-start(), calls=%async_computation.5 | async-start | bytes 557056 | tf_op jit(solution)/shard_map/reduce_scatter | solution.py:150
  168.7 3.2 %copy-start.1 = (bf16[384,4096]{1,0:T(8,128)(2,1)S(1)}, bf16[384,4096]{1,0:T(8,128)(2,1)}, u32[]{:S(2)}) copy-start(bf16[384,4096]{1,0:T(8,128)(2,1)} %reshape_squeeze_reshape.6) | copy-start | bytes 9437188
  168.8 4.8 %copy-start.3 = (bf16[512,4096]{1,0:T(8,128)(2,1)S(1)}, bf16[512,4096]{1,0:T(8,128)(2,1)}, u32[]{:S(2)}) copy-start(bf16[512,4096]{1,0:T(8,128)(2,1)} %all-gather.2.cloned.1.call-done) | copy-start | bytes 12582916
  175.4 52.5 %copy-start.8 = (f32[1,4096]{1,0:T(1,128)S(1)}, f32[1,4096]{1,0:T(1,128)}, u32[]{:S(2)}) copy-start(f32[1,4096]{1,0:T(1,128)} %param.15) | copy-start | bytes 49156
  175.4 56.5 %copy-start.6 = (f32[32,4096]{1,0:T(8,128)S(1)}, f32[32,4096]{1,0:T(8,128)}, u32[]{:S(2)}) copy-start(f32[32,4096]{1,0:T(8,128)} %get-tuple-element.16) | copy-start | bytes 1572868
  252.9 15.8 %all-to-all-start.1 = ((bf16[32,12,512]{2,1,0:T(8,128)(2,1)}), bf16[32,12,512]{2,1,0:T(8,128)(2,1)S(1)}, u32[]{:S(2)}, u32[]{:S(2)}) async-start(bf16[32,12,512]{2,1,0:T(8,128)(2,1)} %reshape_stack_reshape.3), calls=%async_computation.1 | async-start | bytes 1048576 | tf_op jit(solution)/shard_map/all_to_all | solution.py:140
  257.1 3.7 %copy-start.2 = (bf16[384,4096]{1,0:T(8,128)(2,1)S(1)}, bf16[384,4096]{1,0:T(8,128)(2,1)}, u32[]{:S(2)}) copy-start(bf16[384,4096]{1,0:T(8,128)(2,1)} %reshape_squeeze_reshape.6) | copy-start | bytes 9437188
  257.1 4.9 %copy-start.4 = (bf16[512,4096]{1,0:T(8,128)(2,1)S(1)}, bf16[512,4096]{1,0:T(8,128)(2,1)}, u32[]{:S(2)}) copy-start(bf16[512,4096]{1,0:T(8,128)(2,1)} %all-gather.2.cloned.1.call-done) | copy-start | bytes 12582916
Sparse Core Ops, SparseCore 0:
  11.1 157.2 all-gather.1
  232.9 54.4 reduce-scatter.1
where the time goes:
time: 296 us; the launch traced here: 294 us
  waiting for transfers between devices  130 us (44%)
  blocking collectives  51.5 us (17%)
  matrix products  28.8 us (10%)
  local copies, waits for them, and re-layouts  27.3 us (9%)
  starting transfers between devices  26.7 us (9%)
  other arithmetic  15.1 us (5%)
  between operations  14.3 us (5%)
    all_to_all x1, waiting for transfers between devices, on_device(): lax.all_to_all(g_send, 'grp', split_axis=0, concat_axis=0, tiled=True)  108 us
    psum x1, blocking collectives, on_device(): square_sum, align_sum = lax.psum((square_all, align_all), 'tp')  51.5 us
    dot_general x6, matrix products, contract_cols(): lax.dot_general(left, right, dims, preferred_element_type=jnp.float32)  17.4 us
    reduce_scatter x1, waiting for transfers between devices, on_device(): lax.psum_scatter(jnp.stack(second_grads), 'tp', scatter_dimension=2, tile...  17 us
    all_to_all x1, starting transfers between devices, on_device(): lax.all_to_all(x_send, 'grp', split_axis=0, concat_axis=0, tiled=True)  13.7 us
    gather x4, local copies, waits for them, and re-layouts, pack_rows(): source[gather_at]  12.7 us
    all_to_all x1, starting transfers between devices, on_device(): lax.all_to_all(g_send, 'grp', split_axis=0, concat_axis=0, tiled=True)  8.76 us
    dot_general x5, matrix products, contract_rows(): lax.dot_general(left, right, dims, preferred_element_type=jnp.float32)  7.66 us
  transfers between devices with their start and end apart: 5, of which 4 were waited for; matrix products, arithmetic and copies ran while one was open for 20% of the time, Pallas kernels for 0%

commit v1 on v0

v1 whole, which is shorter than its diff:
```python
import jax
import jax.numpy as jnp
from jax import lax
from jax.sharding import PartitionSpec as P

CAP = 12
NX = 4
EPSILON = 1e-06
HIGH = lax.Precision.HIGHEST
BF = jnp.bfloat16
F32 = jnp.float32


def dot(left, right, dims, precision=None):
    return lax.dot_general(
        left, right, (dims, ((), ())), precision=precision, preferred_element_type=F32
    )


def split_pair(values):
    upper = values.astype(BF)
    return upper, (values - upper.astype(F32)).astype(BF)


def row_targets(count_row, owner_slot, rows):
    ends = jnp.cumsum(count_row)
    starts = ends - count_row
    ids = jnp.arange(rows, dtype=jnp.int32)[None, :]
    inside = ((ids >= starts[:, None]) & (ids < ends[:, None])).astype(jnp.int32)
    shift = owner_slot * CAP - starts
    return jnp.sum(inside * shift[:, None], axis=0) + ids[0]


def on_device(acts, grads, counts, owner_slot, base_weight, adapter_a, adapter_b, magnitude):
    groups, shards = lax.axis_size("grp"), lax.axis_size("tp")
    nz = groups // NX
    quads = shards // NX
    rows, width = acts.shape
    out_width = grads.shape[1]
    rank = adapter_a.shape[2]
    x_cols, t_cols = out_width // NX, out_width // shards
    packed = groups * CAP
    z_groups = [[i * nz + j for j in range(nz)] for i in range(NX)]
    x_groups = [[i * nz + j for i in range(NX)] for j in range(nz)]
    my_x = lax.axis_index("grp") // nz
    my_t = lax.axis_index("tp")

    weight_x = lax.all_gather(
        base_weight.T, "grp", axis=0, tiled=True, axis_index_groups=z_groups
    )

    target = row_targets(counts[0], owner_slot, rows)
    place = (jnp.arange(packed, dtype=jnp.int32)[:, None] == target[None, :]).astype(BF)
    grads_t = lax.dynamic_slice(grads, (0, my_t * t_cols), (rows, t_cols))
    both = dot(place, jnp.concatenate([acts, grads_t], axis=1), ((1,), (0,))).astype(BF)
    both = lax.all_to_all(
        both.reshape(groups, CAP, width + t_cols), "grp", split_axis=0, concat_axis=0, tiled=True
    ).reshape(packed, width + t_cols)
    rows_in, rows_grad_t = both[:, :width], both[:, width:]
    rows_grad = lax.all_gather(rows_grad_t, "tp", axis=1, tiled=True)

    first, second = adapter_a[0], adapter_b[0]
    first_t = first.T
    fields = jnp.concatenate(
        [
            jnp.broadcast_to(first_t[None], (NX, rank, width)),
            second.reshape(rank, NX, x_cols).transpose(1, 0, 2),
        ],
        axis=2,
    )
    fields = lax.all_to_all(
        fields, "grp", split_axis=0, concat_axis=0, tiled=True, axis_index_groups=x_groups
    ).reshape(NX * rank, width + x_cols)
    first_all, second_all = fields[:, :width], fields[:, width:]
    second_wide = second_all.astype(F32)

    owner = jnp.arange(NX * rank, dtype=jnp.int32) // rank
    gram = jnp.where(
        owner[:, None] == owner[None, :], dot(first_all, first_all, ((1,), (1,))), 0.0
    )
    gram_second = dot(gram, second_wide, ((1,), (0,)), HIGH)
    first_weight = dot(first_all, weight_x, ((1,), (1,)))
    square_base = jnp.sum(jnp.square(weight_x.astype(F32)), axis=1)
    squares = square_base[None, :] + jnp.sum(
        (second_wide * (2.0 * first_weight + gram_second)).reshape(NX, rank, x_cols), axis=1
    )
    first_merged = first_weight + gram_second
    rows_low = dot(first_t, rows_in, ((1,), (1,)))

    def lanes(values):
        return jnp.concatenate(
            [values[:, i : i + 128] for i in range(0, values.shape[1], 128)], axis=0
        )

    pieces = first_merged.astype(BF).reshape(NX, rank, quads, t_cols)
    pieces = pieces.transpose(0, 2, 1, 3).reshape(shards, rank, t_cols)
    pieces = jnp.concatenate([pieces[:, :, i : i + 128] for i in range(0, t_cols, 128)], axis=1)
    square_upper, square_lower = split_pair(squares)
    common = jnp.concatenate(
        [lanes(square_upper), lanes(square_lower), lanes(rows_low.astype(BF))], axis=0
    )
    sums = jnp.concatenate(
        [pieces, jnp.broadcast_to(common[None], (shards,) + common.shape)], axis=1
    )
    sums = lax.all_to_all(sums, "tp", split_axis=0, concat_axis=0, tiled=True)
    sums = jnp.sum(sums.astype(F32), axis=0)

    def unlanes(values, height):
        return jnp.concatenate(
            [values[i : i + height] for i in range(0, values.shape[0], height)], axis=1
        )

    n_piece = rank * t_cols // 128
    n_square = NX * x_cols // 128
    merged_piece = unlanes(sums[:n_piece], rank)
    square_sum = unlanes(
        sums[n_piece : n_piece + n_square] + sums[n_piece + n_square : n_piece + 2 * n_square], NX
    )
    rows_low = unlanes(sums[n_piece + 2 * n_square :], rank)

    square_own = lax.all_to_all(
        square_sum.reshape(NX, 1, x_cols),
        "grp",
        split_axis=0,
        concat_axis=0,
        tiled=True,
        axis_index_groups=x_groups,
    ).reshape(1, out_width)
    swap = []
    for i in range(NX):
        for j in range(nz):
            for a in range(NX):
                for q in range(quads):
                    swap.append(
                        ((i * nz + j) * shards + a * quads + q, (a * nz + j) * shards + i * quads + q)
                    )
    merged_own = lax.ppermute(merged_piece, ("grp", "tp"), swap)
    norm = jnp.sqrt(square_own + EPSILON)
    scale = magnitude / norm

    def along_x(values, step):
        pairs = [
            (((i + step) % NX) * nz + j, i * nz + j) for i in range(NX) for j in range(nz)
        ]
        return lax.ppermute(values, "grp", pairs)

    after = along_x(weight_x, 1)
    before = along_x(weight_x, -1)
    half = x_cols // 2
    across = jnp.concatenate([along_x(after[:half], 1), along_x(before[half:], -1)], axis=0)
    weight = jnp.zeros((out_width, width), BF)
    for piece, step in ((weight_x, 0), (after, 1), (across, 2), (before, 3)):
        weight = lax.dynamic_update_slice(weight, piece, (((my_x + step) % NX) * x_cols, 0))

    hidden = (rows_grad.astype(F32) * scale).astype(BF)
    inner = dot(hidden, second, ((1,), (1,))).astype(BF)
    back = dot(hidden, weight, ((1,), (0,))) + dot(inner, first, ((1,), (1,)))
    back = lax.all_to_all(
        back.astype(BF).reshape(groups, CAP, width), "grp", split_axis=0, concat_axis=0, tiled=True
    ).reshape(packed, width)
    row_grad = dot(place, back, ((0,), (0,))).astype(BF)

    projected = dot(rows_in, weight, ((1,), (1,)))
    align = jnp.sum(rows_grad.astype(F32) * projected, axis=0)
    second_t = lax.dynamic_slice(second, (0, my_t * t_cols), (rank, t_cols)).astype(F32)
    first_moment = dot(rows_low.astype(BF), rows_grad_t, ((1,), (0,)))
    align_low = jnp.sum(first_moment * second_t, axis=0)
    align_t = lax.dynamic_slice(align, (my_t * t_cols,), (t_cols,)) + align_low
    align = lax.dynamic_update_slice(align, align_t, (my_t * t_cols,))
    align_all = lax.all_to_all(
        jnp.broadcast_to(align.reshape(1, -1, 128), (shards, out_width // 128, 128)),
        "tp",
        split_axis=0,
        concat_axis=0,
        tiled=True,
    )
    align = jnp.sum(align_all, axis=0).reshape(1, out_width)
    grad_gain = align / norm
    shrink = magnitude * align / (norm * norm * norm)

    shrunk = (second.astype(F32) * shrink).astype(BF)
    small = dot(second, shrunk, ((1,), (1,)))
    grad_a = (
        dot(rows_in, inner, ((0,), (0,)))
        - dot(weight, shrunk, ((0,), (1,)))
        - dot(first, small.astype(BF), ((1,), (0,)))
    )
    scale_t = lax.dynamic_slice(scale, (0, my_t * t_cols), (1, t_cols))
    shrink_t = lax.dynamic_slice(shrink, (0, my_t * t_cols), (1, t_cols))
    grad_b = first_moment * scale_t - merged_own * shrink_t
    return row_grad, grad_a[None], grad_b[None], grad_gain


def solution(mesh):
    in_specs = (
        P("grp", "tp"),
        P("grp", None),
        P("grp", None),
        P(),
        P("tp", "grp"),
        P("grp", "tp", None),
        P("grp", None, None),
        P("grp", None),
    )
    out_specs = (P("grp", "tp"), P("grp", "tp", None), P("grp", None, "tp"), P("grp", None))
    return jax.shard_map(
        on_device, mesh=mesh, in_specs=in_specs, out_specs=out_specs, check_vma=False
    )
```

time: 296 us -> 200 us (0.68)
  waiting for transfers between devices: 130 us -> 76.2 us
  blocking collectives: 51.5 us -> 0 us
  starting transfers between devices: 26.7 us -> 59.7 us
  other arithmetic: 15.1 us -> 6.93 us
  local copies, waits for them, and re-layouts: 27.3 us -> 19.8 us
  matrix products: 28.8 us -> 22 us
    all_to_all x3 -> x6, waiting for transfers between devices: 113 us -> 51.8 us  [the longest x1 26.8 us: on_device(): lax.all_to_all(both.reshape(groups, CAP, width + t_cols), 'grp', split_ax...]
    psum x1 -> x0, blocking collectives: 51.5 us -> none  [on_device(): square_sum, align_sum = lax.psum((square_all, align_all), 'tp')]
    all_to_all x3 -> x6, starting transfers between devices: 26.7 us -> 44.4 us  [the longest x1 11.7 us: on_device(): lax.all_to_all(both.reshape(groups, CAP, width + t_cols), 'grp', split_ax...]
    reduce_scatter x1 -> x0, waiting for transfers between devices: 17 us -> none  [on_device(): lax.psum_scatter(jnp.stack(second_grads), 'tp', scatter_dimension=2, tile...]
    ppermute x0 -> x5, starting transfers between devices: none -> 15.2 us  [the longest x4 14.5 us: along_x(): return lax.ppermute(values, 'grp', pairs)]
    gather x5 -> x0, local copies, waits for them, and re-layouts: 14.2 us -> none  [the longest x4 12.7 us: pack_rows(): source[gather_at]]
    ppermute x0 -> x5, waiting for transfers between devices: none -> 14.1 us  [the longest x4 14.1 us: along_x(): return lax.ppermute(values, 'grp', pairs)]
    all_gather x1 -> x2, waiting for transfers between devices: 0.01 us -> 9.63 us  [the longest x1 5.35 us: on_device(): rows_grad = lax.all_gather(rows_grad_t, 'tp', axis=1, tiled=True)]
  transfers between devices with their start and end apart: 5 -> 13, of which waited for: 4 -> 8; matrix products, arithmetic and copies ran while one was open for 20% -> 24% of each run, Pallas kernels for 0% -> 0%
where the time goes in v1:
time: 200 us; the launch traced here: 199 us
  waiting for transfers between devices  76.2 us (38%)
  starting transfers between devices  59.7 us (30%)
  matrix products  22 us (11%)
  local copies, waits for them, and re-layouts  19.8 us (10%)
  between operations  14.6 us (7%)
  other arithmetic  6.93 us (3%)
    all_to_all x1, waiting for transfers between devices, on_device(): lax.all_to_all(both.reshape(groups, CAP, width + t_cols), 'grp', split_ax...  26.8 us
    dot_general x14, matrix products, dot(): lax.dot_general(left, right, (dims, ((), ())), precision=precision, prefe...  22 us
    ppermute x4, starting transfers between devices, along_x(): return lax.ppermute(values, 'grp', pairs)  14.5 us
    ppermute x4, waiting for transfers between devices, along_x(): return lax.ppermute(values, 'grp', pairs)  14.1 us
    all_to_all x1, waiting for transfers between devices, on_device(): lax.all_to_all(back.astype(BF).reshape(groups, CAP, width), 'grp', split_...  11.8 us
    all_to_all x1, starting transfers between devices, on_device(): lax.all_to_all(both.reshape(groups, CAP, width + t_cols), 'grp', split_ax...  11.7 us
    all_to_all x1, starting transfers between devices, on_device(): lax.all_to_all(back.astype(BF).reshape(groups, CAP, width), 'grp', split_...  11.1 us
    all_to_all x1, waiting for transfers between devices, on_device(): lax.all_to_all(jnp.broadcast_to(align.reshape(1, -1, 128), (shards, out_w...  11 us
  transfers between devices with their start and end apart: 13, of which 8 were waited for; matrix products, arithmetic and copies ran while one was open for 24% of the time, Pallas kernels for 0%

profile of v1, /device:TPU:1, one launch (start us, length us, event | category | flops | bytes accessed | tf_op | source)
XLA Modules:
  0.0 199.2 jit_solution(3554385559575562008)
XLA Ops:
  7.2 0.7 all-gather.5.cloned.1.call-update
  7.9 1.1 reshape_squeeze.3
  9.2 0.8 broadcast_in_dim.18
  9.9 0.8 pad_maximum_fusion.1
  10.7 4.8 %all-to-all-start.1 = ((bf16[4,32,1536]{2,1,0:T(8,128)(2,1)}), bf16[4,32,1536]{2,1,0:T(8,128)(2,1)S(1)}, u32[]{:S(2)}, u32[]{:S(2)}) async-start(bf16[4,32,1536]{2,1,0:T(8,128)(2,1)} %pad_maximum_fusion.1), calls=%async_computation.1 | async-start | bytes 786432 | tf_op jit(solution)/shard_map/all_to_all | solution.py:71
  15.5 0.7 copy.21
  16.3 0.1 reduce
  16.4 0.7 multiply_subtract_fusion
  17.1 0.1 select_reduce_fusion
  17.3 1.2 convolution_convert_fusion
  18.5 1.1 reshape.168
  19.5 2.3 %all-to-all-done.1 = bf16[4,32,1536]{2,1,0:T(8,128)(2,1)S(1)} async-done(((bf16[4,32,1536]{2,1,0:T(8,128)(2,1)}), bf16[4,32,1536]{2,1,0:T(8,128)(2,1)S(1)}, u32[]{:S(2)}, u32[]{:S(2)}) %all-to-all-start.1) | async-done | bytes 393248 | tf_op jit(solution)/shard_map/all_to_all | solution.py:71
  21.8 11.7 %all-to-all-start = ((bf16[32,12,768]{2,1,0:T(8,128)(2,1)}), bf16[32,12,768]{2,1,0:T(8,128)(2,1)S(1)}, u32[]{:S(2)}, u32[]{:S(2)}) async-start(bf16[32,12,768]{2,1,0:T(8,128)(2,1)} %reshape.168), calls=%async_computation | async-start | bytes 1572864 | tf_op jit(solution)/shard_map/all_to_all | solution.py:56
  33.5 0.2 convolution_select_fusion
  33.7 26.8 %all-to-all-done = bf16[32,12,768]{2,1,0:T(8,128)(2,1)S(1)} async-done(((bf16[32,12,768]{2,1,0:T(8,128)(2,1)}), bf16[32,12,768]{2,1,0:T(8,128)(2,1)S(1)}, u32[]{:S(2)}, u32[]{:S(2)}) %all-to-all-start) | async-done | bytes 589856 | tf_op jit(solution)/shard_map/all_to_all | solution.py:56
  60.5 0.1 reshape.169
  60.6 0.7 slice.178
  61.4 0.2 fusion.17
  61.7 4.3 %all-gather.5.cloned.1.call-done = bf16[1024,512]{0,1:T(8,128)(2,1)} async-done(((bf16[128,512]{0,1:T(8,128)(2,1)}), bf16[1024,512]{0,1:T(8,128)(2,1)}) %all-gather.5.cloned.1.call-update) | async-done | bytes 1048592 | tf_op jit(solution)/shard_map/all_gather | solution.py:48
  65.9 1.6 fusion.38
  67.6 0.5 bitcast_reduce_fusion
  68.1 0.2 reshape.171
  68.4 0.2 multiply_reduce_fusion
  68.7 0.3 concatenate.27
  68.9 5.3 %collective-permute-start = (bf16[1024,512]{0,1:T(8,128)(2,1)S(1)}, bf16[1024,512]{0,1:T(8,128)(2,1)}, u32[]{:S(2)}, u32[]{:S(2)}) collective-permute-start(bf16[1024,512]{0,1:T(8,128)(2,1)S(1)} %copy-done.1), channel_id=1, source_target_pairs={{128,0},{144,16},{160,32},{176,48},{192,64},{208,80},{224,96},{240... | collective-permute-start | bytes 3145736 | tf_op jit(solution)/shard_map/ppermute | solution.py:145
  74.2 1.9 collective-permute-start.2
  76.2 0.1 broadcast_in_dim.20
  76.3 1.0 pad_maximum_fusion
  77.3 8.9 %all-to-all-start.2 = ((bf16[16,224,128]{2,1,0:T(8,128)(2,1)}), bf16[16,224,128]{2,1,0:T(8,128)(2,1)S(1)}, u32[]{:S(2)}, u32[]{:S(2)}) async-start(bf16[16,224,128]{2,1,0:T(8,128)(2,1)} %pad_maximum_fusion), calls=%async_computation.2 | async-start | bytes 1835008 | tf_op jit(solution)/shard_map/all_to_all | solution.py:105
  86.2 8.4 %collective-permute-done = bf16[1024,512]{0,1:T(8,128)(2,1)} collective-permute-done((bf16[1024,512]{0,1:T(8,128)(2,1)S(1)}, bf16[1024,512]{0,1:T(8,128)(2,1)}, u32[]{:S(2)}, u32[]{:S(2)}) %collective-permute-start) | collective-permute-done | bytes 1048608 | tf_op jit(solution)/shard_map/ppermute | solution.py:145
  94.6 1.9 slice.213
  96.5 5.4 %collective-permute-start.1 = (bf16[512,512]{0,1:T(8,128)(2,1)}, bf16[512,512]{0,1:T(8,128)(2,1)S(1)}, u32[]{:S(2)}, u32[]{:S(2)}) collective-permute-start(bf16[512,512]{0,1:T(8,128)(2,1)} %slice.213), channel_id=1, source_target_pairs={{128,0},{144,16},{160,32},{176,48},{192,64},{208,80},{224,96},{240... | collective-permute-start | bytes 1572872 | tf_op jit(solution)/shard_map/ppermute | solution.py:145
  101.9 1.9 slice.214
  103.8 1.9 collective-permute-start.3
  105.8 2.5 %broadcast_in_dim.21 = bf16[4096,512]{0,1:T(8,128)(2,1)} broadcast(bf16[]{:T(256)} %constant.83.clone.1), dimensions={} | broadcast | bytes 4194306 | tf_op jit(solution)/shard_map/broadcast_in_dim | solution.py:151
  108.3 1.1 constant_dynamic-update-slice_fusion.10
  109.4 2.4 %constant_dynamic-update-slice_fusion.9 = bf16[4096,512]{0,1:T(8,128)(2,1)} fusion(bf16[4096,512]{0,1:T(8,128)(2,1)} %constant_dynamic-update-slice_fusion.10, bf16[1024,512]{0,1:T(8,128)(2,1)} %collective-permute-done, s32[]{:T(128)S(6)} %select_n.67), kind=kLoop, calls=%fused_computation.87 | loop fusion | bytes 2097156 | tf_op jit(solution)/shard_map/dynamic_update_slice | solution.py:153
  111.8 5.7 %collective-permute-done.3 = bf16[512,512]{0,1:T(8,128)(2,1)} collective-permute-done((bf16[512,512]{0,1:T(8,128)(2,1)}, bf16[512,512]{0,1:T(8,128)(2,1)}, u32[]{:S(2)}, u32[]{:S(2)}) %collective-permute-start.3) | collective-permute-done | bytes 524320 | tf_op jit(solution)/shard_map/ppermute | solution.py:145
  117.4 2.3 %maximum_dynamic-update-slice_fusion = bf16[4096,512]{0,1:T(8,128)(2,1)} fusion(bf16[4096,512]{0,1:T(8,128)(2,1)} %constant_dynamic-update-slice_fusion.9, s32[]{:T(128)S(6)} %select_n.69, bf16[512,512]{0,1:T(8,128)(2,1)} %collective-permute-done.3, bf16[512,512]{0,1:T(8,128)(2,1)S(1)} %collective-permute-done.1), kind=kLoop, calls=%fused_computation.21 | loop fusion | flops 2097152 | bytes 2097156 | tf_op jit(solution)/shard_map/dynamic_update_slice | solution.py:153
  119.7 2.3 %constant_dynamic-update-slice_fusion.8 = bf16[4096,512]{0,1:T(8,128)(2,1)} fusion(bf16[4096,512]{0,1:T(8,128)(2,1)} %maximum_dynamic-update-slice_fusion, bf16[1024,512]{0,1:T(8,128)(2,1)} %collective-permute-done.2, s32[]{:T(128)S(6)} %select_n.71), kind=kLoop, calls=%fused_computation.86 | loop fusion | bytes 2097156 | tf_op jit(solution)/shard_map/dynamic_update_slice | solution.py:153
  122.0 0.1 convert_reduce_fusion
  122.3 0.6 copy.24
  122.9 3.3 %all-to-all-start.3 = ((f32[4,1,1024]{2,1,0:T(1,128)}), f32[4,1,1024]{2,1,0:T(1,128)S(1)}, u32[]{:S(2)}, u32[]{:S(2)}) async-start(f32[4,1,1024]{2,1,0:T(1,128)} %copy.24), calls=%async_computation.3 | async-start | bytes 32768 | tf_op jit(solution)/shard_map/all_to_all | solution.py:121
  126.2 0.2 fusion.42
  126.4 5.4 %all-gather.3.cloned.1.call-done = bf16[384,4096]{1,0:T(8,128)(2,1)} async-done(((bf16[384,256]{1,0:T(8,128)(2,1)}), bf16[384,4096]{1,0:T(8,128)(2,1)}) %all-gather.3.cloned.1.call-update) | async-done | bytes 3145744 | tf_op jit(solution)/shard_map/all_gather | solution.py:60
  131.7 5.0 %fusion.1 = f32[4096]{0:T(1024)S(1)} fusion(bf16[384,4096]{1,0:T(8,128)(2,1)} %all-gather.3.cloned.1.call-done, bf16[4096,512]{0,1:T(8,128)(2,1)} %constant_dynamic-update-slice_fusion.8, bf16[384,768]{1,0:T(8,128)(2,1)S(1)} %copy-done.4), kind=kOutput, calls=%fused_computation.3 | convolution fusion | flops 1615327232 | bytes 7749632 | tf_op jit(solution)/shard_map/dot_general | solution.py:15
  136.7 0.2 add_dynamic-update-slice_fusion
  136.9 0.7 broadcast_in_dim.23
  137.6 4.6 %all-to-all-start.5 = ((f32[16,32,128]{2,1,0:T(8,128)}), f32[16,32,128]{2,1,0:T(8,128)S(1)}, u32[]{:S(2)}, u32[]{:S(2)}) async-start(f32[16,32,128]{2,1,0:T(8,128)} %broadcast_in_dim.23), calls=%async_computation.5 | async-start | bytes 524288 | tf_op jit(solution)/shard_map/all_to_all | solution.py:170
  142.3 0.7 collective-permute-start.4
  143.0 11.0 %all-to-all-done.5 = f32[16,32,128]{2,1,0:T(8,128)S(1)} async-done(((f32[16,32,128]{2,1,0:T(8,128)}), f32[16,32,128]{2,1,0:T(8,128)S(1)}, u32[]{:S(2)}, u32[]{:S(2)}) %all-to-all-start.5) | async-done | bytes 262176 | tf_op jit(solution)/shard_map/all_to_all | solution.py:170
  154.0 0.6 fusion.62
  154.7 3.2 %fusion.14 = bf16[384,32]{0,1:T(8,128)(2,1)S(1)} fusion(bf16[384,4096]{1,0:T(8,128)(2,1)} %all-gather.3.cloned.1.call-done, f32[4096]{0:T(1024)S(1)} %bitcast.82, bf16[1,32,4096]{2,1,0:T(8,128)(2,1)S(1)} %copy-done.2), kind=kOutput, calls=%fused_computation.17 | convolution fusion | flops 105394176 | bytes 3448832 | tf_op jit(solution)/shard_map/dot_general | solution.py:15
  157.9 0.2 fusion.19
  158.1 0.3 fusion.43
  158.4 4.0 %fusion.9 = bf16[384,512]{1,0:T(8,128)(2,1)S(1)} fusion(f32[384,512]{1,0:T(8,128)S(1)} %fusion.43, bf16[4096,512]{0,1:T(8,128)(2,1)} %constant_dynamic-update-slice_fusion.8, bf16[384,4096]{1,0:T(8,128)(2,1)S(1)} %copy-done.8, f32[4096]{0:T(1024)S(1)} %bitcast.83), kind=kOutput, calls=%fused_computation.10 | convolution fusion | flops 1615724544 | bytes 8536064 | tf_op jit(solution)/shard_map/dot_general | solution.py:15
  162.4 0.9 reshape.175
  163.3 11.1 %all-to-all-start.4 = ((bf16[32,12,512]{2,1,0:T(8,128)(2,1)}), bf16[32,12,512]{2,1,0:T(8,128)(2,1)S(1)}, u32[]{:S(2)}, u32[]{:S(2)}) async-start(bf16[32,12,512]{2,1,0:T(8,128)(2,1)} %reshape.175), calls=%async_computation.4 | async-start | bytes 1048576 | tf_op jit(solution)/shard_map/all_to_all | solution.py:158
  174.4 3.5 %convolution_subtract_fusion = f32[512,32]{0,1:T(8,128)S(1)} fusion(f32[512,32]{0,1:T(8,128)S(1)} %fusion.19, bf16[4096,512]{0,1:T(8,128)(2,1)} %constant_dynamic-update-slice_fusion.8, bf16[1,32,4096]{2,1,0:T(8,128)(2,1)S(1)} %copy-done.2, f32[4096]{0:T(1024)S(1)} %bitcast.75), kind=kOutput, calls=%fused_computation.16 | convolution fusion | flops 134627328 | bytes 4603904 | tf_op jit(solution)/shard_map/dot_general | solution.py:15
  178.0 1.0 fusion.13
  178.9 0.6 subtract_bitcast_fusion
  179.6 11.8 %all-to-all-done.4 = bf16[32,12,512]{2,1,0:T(8,128)(2,1)S(1)} async-done(((bf16[32,12,512]{2,1,0:T(8,128)(2,1)}), bf16[32,12,512]{2,1,0:T(8,128)(2,1)S(1)}, u32[]{:S(2)}, u32[]{:S(2)}) %all-to-all-start.4) | async-done | bytes 393248 | tf_op jit(solution)/shard_map/all_to_all | solution.py:158
  191.3 0.1 reshape.176
  191.4 0.9 convolution_convert_fusion.1
  (53 shorter events, 0.7 us)
Async XLA Ops:
  7.2 10.1 %copy-start = (bf16[128,4096]{1,0:T(8,128)(2,1)S(1)}, bf16[128,4096]{1,0:T(8,128)(2,1)}, u32[]{:S(2)}) copy-start(bf16[128,4096]{1,0:T(8,128)(2,1)} %param.9) | copy-start | bytes 3145732
  7.2 58.8 %all-gather.5.cloned.1.call-start = ((), (), s32[]{:S(2)}) async-start(), calls=%async_computation.7 | async-start | bytes 1179648 | tf_op jit(solution)/shard_map/all_gather | solution.py:48
  9.1 52.3 %copy-start.5 = (bf16[1,512,32]{1,2,0:T(8,128)(2,1)S(1)}, bf16[1,512,32]{1,2,0:T(8,128)(2,1)}, u32[]{:S(2)}) copy-start(bf16[1,512,32]{1,2,0:T(8,128)(2,1)} %param.13) | copy-start | bytes 98308
  10.7 11.1 %all-to-all-start.1 = ((bf16[4,32,1536]{2,1,0:T(8,128)(2,1)}), bf16[4,32,1536]{2,1,0:T(8,128)(2,1)S(1)}, u32[]{:S(2)}, u32[]{:S(2)}) async-start(bf16[4,32,1536]{2,1,0:T(8,128)(2,1)} %pad_maximum_fusion.1), calls=%async_computation.1 | async-start | bytes 786432 | tf_op jit(solution)/shard_map/all_to_all | solution.py:71
  21.8 38.7 %all-to-all-start = ((bf16[32,12,768]{2,1,0:T(8,128)(2,1)}), bf16[32,12,768]{2,1,0:T(8,128)(2,1)S(1)}, u32[]{:S(2)}, u32[]{:S(2)}) async-start(bf16[32,12,768]{2,1,0:T(8,128)(2,1)} %reshape.168), calls=%async_computation | async-start | bytes 1572864 | tf_op jit(solution)/shard_map/all_to_all | solution.py:56
  33.5 98.2 %all-gather.3.cloned.1.call-start = ((), (), s32[]{:S(2)}) async-start(), calls=%async_computation.6 | async-start | bytes 3342336 | tf_op jit(solution)/shard_map/all_gather | solution.py:60
  60.6 1.1 copy-start.3
  65.9 2.4 %copy-start.1 = (bf16[1024,512]{0,1:T(8,128)(2,1)S(1)}, bf16[1024,512]{0,1:T(8,128)(2,1)}, u32[]{:S(2)}) copy-start(bf16[1024,512]{0,1:T(8,128)(2,1)} %all-gather.5.cloned.1.call-done) | copy-start | bytes 3145732
  68.9 25.7 %collective-permute-start = (bf16[1024,512]{0,1:T(8,128)(2,1)S(1)}, bf16[1024,512]{0,1:T(8,128)(2,1)}, u32[]{:S(2)}, u32[]{:S(2)}) collective-permute-start(bf16[1024,512]{0,1:T(8,128)(2,1)S(1)} %copy-done.1), channel_id=1, source_target_pairs={{128,0},{144,16},{160,32},{176,48},{192,64},{208,80},{224,96},{240... | collective-permute-start | bytes 3145736 | tf_op jit(solution)/shard_map/ppermute | solution.py:145
  74.2 27.7 %collective-permute-start.2 = (bf16[1024,512]{0,1:T(8,128)(2,1)S(1)}, bf16[1024,512]{0,1:T(8,128)(2,1)}, u32[]{:S(2)}, u32[]{:S(2)}) collective-permute-start(bf16[1024,512]{0,1:T(8,128)(2,1)S(1)} %copy-done.1), channel_id=1, source_target_pairs={{384,0},{400,16},{416,32},{432,48},{448,64},{464,80},{480,96},{496... | collective-permute-start | bytes 3145736 | tf_op jit(solution)/shard_map/ppermute | solution.py:145
  77.3 44.7 %all-to-all-start.2 = ((bf16[16,224,128]{2,1,0:T(8,128)(2,1)}), bf16[16,224,128]{2,1,0:T(8,128)(2,1)S(1)}, u32[]{:S(2)}, u32[]{:S(2)}) async-start(bf16[16,224,128]{2,1,0:T(8,128)(2,1)} %pad_maximum_fusion), calls=%async_computation.2 | async-start | bytes 1835008 | tf_op jit(solution)/shard_map/all_to_all | solution.py:105
  96.5 15.3 %collective-permute-start.1 = (bf16[512,512]{0,1:T(8,128)(2,1)}, bf16[512,512]{0,1:T(8,128)(2,1)S(1)}, u32[]{:S(2)}, u32[]{:S(2)}) collective-permute-start(bf16[512,512]{0,1:T(8,128)(2,1)} %slice.213), channel_id=1, source_target_pairs={{128,0},{144,16},{160,32},{176,48},{192,64},{208,80},{224,96},{240... | collective-permute-start | bytes 1572872 | tf_op jit(solution)/shard_map/ppermute | solution.py:145
  103.8 13.6 %collective-permute-start.3 = (bf16[512,512]{0,1:T(8,128)(2,1)}, bf16[512,512]{0,1:T(8,128)(2,1)}, u32[]{:S(2)}, u32[]{:S(2)}) collective-permute-start(bf16[512,512]{0,1:T(8,128)(2,1)} %slice.214), channel_id=1, source_target_pairs={{384,0},{400,16},{416,32},{432,48},{448,64},{464,80},{480,96},{496... | collective-permute-start | bytes 1572872 | tf_op jit(solution)/shard_map/ppermute | solution.py:145
  109.4 16.8 %copy-start.2 = (bf16[1,32,4096]{2,1,0:T(8,128)(2,1)S(1)}, bf16[1,32,4096]{2,1,0:T(8,128)(2,1)}, u32[]{:S(2)}) copy-start(bf16[1,32,4096]{2,1,0:T(8,128)(2,1)} %param.14) | copy-start | bytes 786436
  109.4 16.8 %copy-start.4 = (bf16[384,768]{1,0:T(8,128)(2,1)S(1)}, bf16[384,768]{1,0:T(8,128)(2,1)}, u32[]{:S(2)}) copy-start(bf16[384,768]{1,0:T(8,128)(2,1)} %copy-done.3) | copy-start | bytes 1769476
  122.9 14.0 %all-to-all-start.3 = ((f32[4,1,1024]{2,1,0:T(1,128)}), f32[4,1,1024]{2,1,0:T(1,128)S(1)}, u32[]{:S(2)}, u32[]{:S(2)}) async-start(f32[4,1,1024]{2,1,0:T(1,128)} %copy.24), calls=%async_computation.3 | async-start | bytes 32768 | tf_op jit(solution)/shard_map/all_to_all | solution.py:121
  126.3 27.7 %copy-start.7 = (f32[1,4096]{1,0:T(1,128)S(1)}, f32[1,4096]{1,0:T(1,128)}, u32[]{:S(2)}) copy-start(f32[1,4096]{1,0:T(1,128)} %param.15) | copy-start | bytes 49156
  136.7 21.3 %copy-start.6 = (bf16[1,512,32]{1,2,0:T(8,128)(2,1)S(1)}, bf16[1,512,32]{1,2,0:T(8,128)(2,1)}, u32[]{:S(2)}) copy-start(bf16[1,512,32]{1,2,0:T(8,128)(2,1)} %param.13) | copy-start | bytes 98308
  137.6 16.3 %all-to-all-start.5 = ((f32[16,32,128]{2,1,0:T(8,128)}), f32[16,32,128]{2,1,0:T(8,128)S(1)}, u32[]{:S(2)}, u32[]{:S(2)}) async-start(f32[16,32,128]{2,1,0:T(8,128)} %broadcast_in_dim.23), calls=%async_computation.5 | async-start | bytes 524288 | tf_op jit(solution)/shard_map/all_to_all | solution.py:170
  142.3 36.7 %collective-permute-start.4 = (f32[32,256]{1,0:T(8,128)S(1)}, f32[32,256]{1,0:T(8,128)S(1)}, u32[]{:S(2)}, u32[]{:S(2)}) collective-permute-start(f32[32,256]{1,0:T(8,128)S(1)} %pad_maximum_fusion.2), channel_id=1, source_target_pairs={{0,0},{1,1},{2,2},{3,3},{4,128},{5,129},{6,130},{7,131},{8,256},{9... | collective-permute-start | bytes 98312 | tf_op jit(solution)/shard_map/ppermute | solution.py:137
  154.0 4.4 %copy-start.8 = (bf16[384,4096]{1,0:T(8,128)(2,1)S(1)}, bf16[384,4096]{1,0:T(8,128)(2,1)}, u32[]{:S(2)}) copy-start(bf16[384,4096]{1,0:T(8,128)(2,1)} %all-gather.3.cloned.1.call-done) | copy-start | bytes 9437188
  163.3 28.0 %all-to-all-start.4 = ((bf16[32,12,512]{2,1,0:T(8,128)(2,1)}), bf16[32,12,512]{2,1,0:T(8,128)(2,1)S(1)}, u32[]{:S(2)}, u32[]{:S(2)}) async-start(bf16[32,12,512]{2,1,0:T(8,128)(2,1)} %reshape.175), calls=%async_computation.4 | async-start | bytes 1048576 | tf_op jit(solution)/shard_map/all_to_all | solution.py:158
Sparse Core Ops, SparseCore 0:
  10.0 55.8 all-gather.4
  68.0 63.6 all-gather.2

commit v2 on v1

--- a/solution.py
+++ b/solution.py
@@ -1,6 +1,8 @@
 import jax
 import jax.numpy as jnp
 from jax import lax
+from jax.experimental import pallas as pl
+from jax.experimental.pallas import tpu as pltpu
 from jax.sharding import PartitionSpec as P
 
 CAP = 12
@@ -29,6 +31,36 @@
     inside = ((ids >= starts[:, None]) & (ids < ends[:, None])).astype(jnp.int32)
     shift = owner_slot * CAP - starts
     return jnp.sum(inside * shift[:, None], axis=0) + ids[0]
+
+
+def main_kernel(place, scale, second, weight, mine, other, total, low, total_out, low_out):
+    step = pl.program_id(0)
+    t_cols = mine.shape[2]
+    near = place[2] * t_cols
+    far = t_cols - near
+
+    @pl.when(step == 0)
+    def _():
+        total_out[...] = total[...]
+        low_out[...] = low[...]
+
+    for start, rows_grad in ((near, mine), (far, other)):
+        cols = pl.ds(pl.multiple_of(start, t_cols), t_cols)
+        hidden = (rows_grad[0].astype(F32) * scale[:, cols]).astype(BF)
+        total_out[...] += jnp.dot(hidden, weight[cols, :], preferred_element_type=F32)
+        low_out[...] += dot(hidden, second[:, cols], ((1,), (1,)))
+
+
+def align_kernel(place, rows_in, weight, mine, other, align_out):
+    t_cols = mine.shape[2]
+    near = place[2] * t_cols
+    far = t_cols - near
+    for start, rows_grad in ((near, mine), (far, other)):
+        cols = pl.ds(pl.multiple_of(start, t_cols), t_cols)
+        projected = dot(rows_in[...], weight[cols, :], ((1,), (1,)))
+        align_out[:, cols] = jnp.sum(
+            rows_grad[0].astype(F32) * projected, axis=0, keepdims=True
+        )
 
 
 def on_device(acts, grads, counts, owner_slot, base_weight, adapter_a, adapter_b, magnitude):
@@ -45,6 +77,11 @@
     my_x = lax.axis_index("grp") // nz
     my_t = lax.axis_index("tp")
 
+    def to_owners(values):
+        values = values.reshape(groups, CAP, values.shape[1])
+        values = lax.all_to_all(values, "grp", split_axis=0, concat_axis=0, tiled=True)
+        return values.reshape(packed, values.shape[2])
+
     weight_x = lax.all_gather(
         base_weight.T, "grp", axis=0, tiled=True, axis_index_groups=z_groups
     )
@@ -52,12 +89,24 @@
     target = row_targets(counts[0], owner_slot, rows)
     place = (jnp.arange(packed, dtype=jnp.int32)[:, None] == target[None, :]).astype(BF)
     grads_t = lax.dynamic_slice(grads, (0, my_t * t_cols), (rows, t_cols))
-    both = dot(place, jnp.concatenate([acts, grads_t], axis=1), ((1,), (0,))).astype(BF)
-    both = lax.all_to_all(
-        both.reshape(groups, CAP, width + t_cols), "grp", split_axis=0, concat_axis=0, tiled=True
-    ).reshape(packed, width + t_cols)
-    rows_in, rows_grad_t = both[:, :width], both[:, width:]
-    rows_grad = lax.all_gather(rows_grad_t, "tp", axis=1, tiled=True)
+    grads_t = dot(place, grads_t, ((1,), (0,))).astype(BF)
+    rows_grad_t = to_owners(grads_t)
+    acts_t = dot(place, acts, ((1,), (0,))).astype(BF)
+
+    ny = shards // 2
+
+    def along_y(values, step):
+        pairs = [((i + 2 * step) % shards, i) for i in range(shards)]
+        return lax.ppermute(values, "tp", pairs)
+
+    upper, lower = [rows_grad_t], [rows_grad_t]
+    for _ in range((ny - 1) // 2):
+        upper.append(along_y(upper[-1], 1))
+        lower.append(along_y(lower[-1], -1))
+    half = packed // 2
+    last = jnp.concatenate([along_y(upper[-1][:half], 1), along_y(lower[-1][half:], -1)], axis=0)
+    mine = jnp.stack(upper + [last] + lower[:0:-1])
+    other = lax.ppermute(mine, "tp", [(i, i ^ 1) for i in range(shards)])
 
     first, second = adapter_a[0], adapter_b[0]
     first_t = first.T
@@ -68,9 +117,12 @@
         ],
         axis=2,
     )
+    fields, rows_grad_t = lax.optimization_barrier((fields, rows_grad_t))
     fields = lax.all_to_all(
         fields, "grp", split_axis=0, concat_axis=0, tiled=True, axis_index_groups=x_groups
     ).reshape(NX * rank, width + x_cols)
+    fields, acts_t = lax.optimization_barrier((fields, acts_t))
+    rows_in = to_owners(acts_t)
     first_all, second_all = fields[:, :width], fields[:, width:]
     second_wide = second_all.astype(F32)
 
@@ -148,47 +200,97 @@
     before = along_x(weight_x, -1)
     half = x_cols // 2
     across = jnp.concatenate([along_x(after[:half], 1), along_x(before[half:], -1)], axis=0)
-    weight = jnp.zeros((out_width, width), BF)
-    for piece, step in ((weight_x, 0), (after, 1), (across, 2), (before, 3)):
-        weight = lax.dynamic_update_slice(weight, piece, (((my_x + step) % NX) * x_cols, 0))
-
-    hidden = (rows_grad.astype(F32) * scale).astype(BF)
-    inner = dot(hidden, second, ((1,), (1,))).astype(BF)
-    back = dot(hidden, weight, ((1,), (0,))) + dot(inner, first, ((1,), (1,)))
-    back = lax.all_to_all(
-        back.astype(BF).reshape(groups, CAP, width), "grp", split_axis=0, concat_axis=0, tiled=True
-    ).reshape(packed, width)
+    pieces = ((weight_x, 0), (after, 1), (before, 3), (across, 2))
+    blocks = [(my_x + step) % NX for _, step in pieces]
+    weights = [piece for piece, _ in pieces]
+
+    p_chips = ny // NX
+    wide = 2 * t_cols
+
+    def chip(step, place):
+        return place[0] * p_chips + step
+
+    def ring(step, place):
+        return (chip(step, place) - place[1] + ny) % ny
+
+    grad_spec = pl.BlockSpec((1, packed, t_cols), lambda i, place: (ring(i, place), 0, 0))
+    weight_spec = pl.BlockSpec((wide, width), lambda i, place: (i, 0))
+    across_spec = pl.BlockSpec((1, wide), lambda i, place: (0, chip(i, place)))
+
+    def whole(*shape):
+        return pl.BlockSpec(shape, lambda i, place: (0,) * len(shape))
+
+    def where(block):
+        return jnp.stack([block, my_t // 2, my_t % 2]).astype(jnp.int32)
+
+    total, low = jnp.zeros((packed, width), F32), jnp.zeros((packed, rank), F32)
+    for piece, block in zip(weights, blocks):
+        total, low = pl.pallas_call(
+            main_kernel,
+            grid_spec=pltpu.PrefetchScalarGridSpec(
+                num_scalar_prefetch=1,
+                grid=(p_chips,),
+                in_specs=[
+                    across_spec,
+                    pl.BlockSpec((rank, wide), lambda i, place: (0, chip(i, place))),
+                    weight_spec,
+                    grad_spec,
+                    grad_spec,
+                    whole(packed, width),
+                    whole(packed, rank),
+                ],
+                out_specs=[whole(packed, width), whole(packed, rank)],
+            ),
+            out_shape=[
+                jax.ShapeDtypeStruct((packed, width), F32),
+                jax.ShapeDtypeStruct((packed, rank), F32),
+            ],
+            name="hidden_weight",
+        )(where(block), scale, second, piece, mine, other, total, low)
+
+    inner = low.astype(BF)
+    back = (total + dot(inner, first, ((1,), (1,)))).astype(BF)
+    back = to_owners(back)
     row_grad = dot(place, back, ((0,), (0,))).astype(BF)
 
-    projected = dot(rows_in, weight, ((1,), (1,)))
-    align = jnp.sum(rows_grad.astype(F32) * projected, axis=0)
+    align = jnp.zeros((1, out_width), F32)
+    for piece, block in zip(weights, blocks):
+        part = pl.pallas_call(
+            align_kernel,
+            grid_spec=pltpu.PrefetchScalarGridSpec(
+                num_scalar_prefetch=1,
+                grid=(p_chips,),
+                in_specs=[whole(packed, width), weight_spec, grad_spec, grad_spec],
+                out_specs=pl.BlockSpec((1, wide), lambda i, place: (0, i)),
+            ),
+            out_shape=jax.ShapeDtypeStruct((1, x_cols), F32),
+            name="align_columns",
+        )(where(block), rows_in, piece, mine, other)
+        align = lax.dynamic_update_slice(align, part, (0, block * x_cols))
     second_t = lax.dynamic_slice(second, (0, my_t * t_cols), (rank, t_cols)).astype(F32)
     first_moment = dot(rows_low.astype(BF), rows_grad_t, ((1,), (0,)))
     align_low = jnp.sum(first_moment * second_t, axis=0)
-    align_t = lax.dynamic_slice(align, (my_t * t_cols,), (t_cols,)) + align_low
-    align = lax.dynamic_update_slice(align, align_t, (my_t * t_cols,))
-    align_all = lax.all_to_all(
-        jnp.broadcast_to(align.reshape(1, -1, 128), (shards, out_width // 128, 128)),
-        "tp",
-        split_axis=0,
-        concat_axis=0,
-        tiled=True,
-    )
-    align = jnp.sum(align_all, axis=0).reshape(1, out_width)
+    align_t = lax.dynamic_slice(align, (0, my_t * t_cols), (1, t_cols)) + align_low
+    align = lax.dynamic_update_slice(align, align_t, (0, my_t * t_cols))
+    align = align.reshape(-1, 128)
+    flip = 1
+    while flip < shards:
+        align = align + lax.ppermute(align, "tp", [(i, i ^ flip) for i in range(shards)])
+        flip *= 2
+    align = align.reshape(1, out_width)
     grad_gain = align / norm
     shrink = magnitude * align / (norm * norm * norm)
 
     shrunk = (second.astype(F32) * shrink).astype(BF)
     small = dot(second, shrunk, ((1,), (1,)))
-    grad_a = (
-        dot(rows_in, inner, ((0,), (0,)))
-        - dot(weight, shrunk, ((0,), (1,)))
-        - dot(first, small.astype(BF), ((1,), (0,)))
-    )
+    grad_a = dot(inner, rows_in, ((0,), (0,))) - dot(small.astype(BF), first_t, ((0,), (0,)))
+    for piece, block in zip(weights, blocks):
+        part = lax.dynamic_slice(shrunk, (0, block * x_cols), (rank, x_cols))
+        grad_a = grad_a - dot(part, piece, ((1,), (0,)))
     scale_t = lax.dynamic_slice(scale, (0, my_t * t_cols), (1, t_cols))
     shrink_t = lax.dynamic_slice(shrink, (0, my_t * t_cols), (1, t_cols))
     grad_b = first_moment * scale_t - merged_own * shrink_t
-    return row_grad, grad_a[None], grad_b[None], grad_gain
+    return row_grad, grad_a.T[None], grad_b[None], grad_gain
 
 
 def solution(mesh):

time: 200 us -> 251 us (1.25)
  the two profiles are of different devices: /device:TPU:1 before, /device:TPU:64 now
where the time goes in v2:
time: 251 us; the launch traced here: 249 us
  starting transfers between devices  108 us (43%)
  waiting for transfers between devices  46 us (18%)
  Pallas kernels  32.1 us (13%)
  local copies, waits for them, and re-layouts  22.1 us (9%)
  matrix products  15 us (6%)
  between operations  14.9 us (6%)
  other arithmetic  10.8 us (4%)
    all_to_all x3, starting transfers between devices, to_owners(): lax.all_to_all(values, 'grp', split_axis=0, concat_axis=0, tiled=True)  29.4 us
    ppermute x8, starting transfers between devices, along_y(): return lax.ppermute(values, 'tp', pairs)  28.4 us
    ppermute x4, starting transfers between devices, on_device(): lax.ppermute(align, 'tp', [(i, i ^ flip) for i in range(shards)])  20.9 us
    all_to_all x3, waiting for transfers between devices, to_owners(): lax.all_to_all(values, 'grp', split_axis=0, concat_axis=0, tiled=True)  18.4 us
    pallas_call x4, Pallas kernels, on_device(): pl.pallas_call(main_kernel, grid_spec=pltpu.PrefetchScalarGridSpec(num_sc...  17.9 us
    ppermute x4, waiting for transfers between devices, along_x(): return lax.ppermute(values, 'grp', pairs)  15.5 us
    dot_general x15, matrix products, dot(): lax.dot_general(left, right, (dims, ((), ())), precision=precision, prefe...  15 us
    pallas_call x4, Pallas kernels, on_device(): pl.pallas_call(align_kernel, grid_spec=pltpu.PrefetchScalarGridSpec(num_s...  14.2 us
  transfers between devices with their start and end apart: 25, of which 10 were waited for; matrix products, arithmetic and copies ran while one was open for 16% of the time, Pallas kernels for 13%

profile of v2, /device:TPU:64, one launch (start us, length us, event | category | flops | bytes accessed | tf_op | source)
XLA Modules:
  0.0 249.0 jit_solution(11911139176411863830)
XLA Ops:
  9.9 12.7 %all-to-all-start = ((bf16[32,12,256]{2,1,0:T(8,128)(2,1)}), bf16[32,12,256]{2,1,0:T(8,128)(2,1)S(1)}, u32[]{:S(2)}, u32[]{:S(2)}) async-start(bf16[32,12,256]{2,1,0:T(8,128)(2,1)} %reshape.175), calls=%async_computation | async-start | bytes 524288 | tf_op jit(solution)/shard_map/all_to_all | solution.py:82
  22.7 1.7 copy.26
  25.8 9.2 %all-to-all-done = bf16[32,12,256]{2,1,0:T(8,128)(2,1)S(1)} async-done(((bf16[32,12,256]{2,1,0:T(8,128)(2,1)}), bf16[32,12,256]{2,1,0:T(8,128)(2,1)S(1)}, u32[]{:S(2)}, u32[]{:S(2)}) %all-to-all-start) | async-done | bytes 196640 | tf_op jit(solution)/shard_map/all_to_all | solution.py:82
  35.7 5.4 %collective-permute-start.4 = (bf16[384,256]{1,0:T(8,128)(2,1)}, bf16[384,256]{1,0:T(8,128)(2,1)}, u32[]{:S(2)}, u32[]{:S(2)}) collective-permute-start(bf16[384,256]{1,0:T(8,128)(2,1)} %reshape.176), channel_id=1, source_target_pairs={{2,0},{3,1},{4,2},{5,3},{6,4},{7,5},{8,6},{9,7},{10,8},{11,9},{12,... | collective-permute-start | bytes 589832 | tf_op jit(solution)/shard_map/ppermute | solution.py:100
  41.1 1.9 collective-permute-start.8
  43.0 4.1 %all-to-all-start.1 = ((bf16[4,32,1536]{2,1,0:T(8,128)(2,1)}), bf16[4,32,1536]{2,1,0:T(8,128)(2,1)}, u32[]{:S(2)}, u32[]{:S(2)}) async-start(bf16[4,32,1536]{2,1,0:T(8,128)(2,1)} %pad_maximum_fusion.1), calls=%async_computation.1 | async-start | bytes 786432 | tf_op jit(solution)/shard_map/all_to_all | solution.py:121
  47.2 5.1 %collective-permute-start.5 = (bf16[384,256]{1,0:T(8,128)(2,1)}, bf16[384,256]{1,0:T(8,128)(2,1)}, u32[]{:S(2)}, u32[]{:S(2)}) collective-permute-start(bf16[384,256]{1,0:T(8,128)(2,1)} %collective-permute-done.4), channel_id=1, source_target_pairs={{2,0},{3,1},{4,2},{5,3},{6,4},{7,5},{8,6},{9,7},{10,8},{11,9},{12,... | collective-permute-start | bytes 589832 | tf_op jit(solution)/shard_map/ppermute | solution.py:100
  52.4 1.9 collective-permute-start.9
  54.3 0.9 bitcast_dynamic-update-slice_fusion.5
  55.3 0.9 reshape.181
  56.2 6.7 %all-to-all-start.2 = ((bf16[32,12,512]{2,1,0:T(8,128)(2,1)}), bf16[32,12,512]{2,1,0:T(8,128)(2,1)}, u32[]{:S(2)}, u32[]{:S(2)}) async-start(bf16[32,12,512]{2,1,0:T(8,128)(2,1)} %reshape.181), calls=%async_computation.2 | async-start | bytes 1048576 | tf_op jit(solution)/shard_map/all_to_all | solution.py:82
  62.9 1.8 convolution_select_fusion
  64.7 5.1 %collective-permute-start.6 = (bf16[384,256]{1,0:T(8,128)(2,1)}, bf16[384,256]{1,0:T(8,128)(2,1)S(1)}, u32[]{:S(2)}, u32[]{:S(2)}) collective-permute-start(bf16[384,256]{1,0:T(8,128)(2,1)} %collective-permute-done.5), channel_id=1, source_target_pairs={{2,0},{3,1},{4,2},{5,3},{6,4},{7,5},{8,6},{9,7},{10,8},{11,9},{12,... | collective-permute-start | bytes 589832 | tf_op jit(solution)/shard_map/ppermute | solution.py:100
  69.9 1.9 collective-permute-start.10
  71.8 0.9 bitcast_dynamic-update-slice_fusion.4
  72.7 5.9 %collective-permute-done.10 = bf16[384,256]{1,0:T(8,128)(2,1)S(1)} collective-permute-done((bf16[384,256]{1,0:T(8,128)(2,1)S(1)}, bf16[384,256]{1,0:T(8,128)(2,1)S(1)}, u32[]{:S(2)}, u32[]{:S(2)}) %collective-permute-start.10) | collective-permute-done | bytes 196640 | tf_op jit(solution)/shard_map/ppermute | solution.py:100
  78.6 1.9 collective-permute-start.11
  80.6 5.1 %collective-permute-start.7 = (bf16[192,256]{1,0:T(8,128)(2,1)S(1)}, bf16[192,256]{1,0:T(8,128)(2,1)S(1)}, u32[]{:S(2)}, u32[]{:S(2)}) collective-permute-start(bf16[192,256]{1,0:T(8,128)(2,1)S(1)} %slice.211), channel_id=1, source_target_pairs={{2,0},{3,1},{4,2},{5,3},{6,4},{7,5},{8,6},{9,7},{10,8},{11,9},{12,... | collective-permute-start | bytes 294920 | tf_op jit(solution)/shard_map/ppermute | solution.py:100
  86.4 1.6 collective-permute-done.7
  88.0 0.9 bitcast_dynamic-update-slice_fusion.mine
  89.0 2.1 collective-permute-start.12
  91.0 1.1 reshape.182.rows_in
  92.5 1.8 fusion.15
  94.3 1.6 bitcast_reduce_fusion
  96.2 1.5 multiply_reduce_fusion
  97.7 4.6 %collective-permute-start = (bf16[1024,512]{1,0:T(8,128)(2,1)}, bf16[1024,512]{1,0:T(8,128)(2,1)}, u32[]{:S(2)}, u32[]{:S(2)}) collective-permute-start(bf16[1024,512]{1,0:T(8,128)(2,1)} %all-gather.2.cloned.1.call-done.weight), channel_id=1, source_target_pairs={{128,0},{144,16},{160,32},{176,48},{192,64},{208,80},{224,96},{240... | collective-permute-start | bytes 3145736 | tf_op jit(solution)/shard_map/ppermute | solution.py:197
  102.4 1.9 collective-permute-start.2
  104.7 1.1 pad_maximum_fusion
  105.7 5.2 %all-to-all-start.3 = ((bf16[16,224,128]{2,1,0:T(8,128)(2,1)}), bf16[16,224,128]{2,1,0:T(8,128)(2,1)}, u32[]{:S(2)}, u32[]{:S(2)}) async-start(bf16[16,224,128]{2,1,0:T(8,128)(2,1)} %pad_maximum_fusion), calls=%async_computation.3 | async-start | bytes 1835008 | tf_op jit(solution)/shard_map/all_to_all | solution.py:157
  112.2 13.5 %collective-permute-done.weight = bf16[1024,512]{1,0:T(8,128)(2,1)} collective-permute-done((bf16[1024,512]{1,0:T(8,128)(2,1)}, bf16[1024,512]{1,0:T(8,128)(2,1)}, u32[]{:S(2)}, u32[]{:S(2)}) %collective-permute-start) | collective-permute-done | bytes 1048608 | tf_op jit(solution)/shard_map/ppermute | solution.py:197
  125.7 1.9 slice.209
  127.6 5.6 %collective-permute-start.1 = (bf16[512,512]{1,0:T(8,128)(2,1)}, bf16[512,512]{1,0:T(8,128)(2,1)S(1)}, u32[]{:S(2)}, u32[]{:S(2)}) collective-permute-start(bf16[512,512]{1,0:T(8,128)(2,1)} %slice.209), channel_id=1, source_target_pairs={{128,0},{144,16},{160,32},{176,48},{192,64},{208,80},{224,96},{240... | collective-permute-start | bytes 1572872 | tf_op jit(solution)/shard_map/ppermute | solution.py:197
  133.8 1.9 slice.210
  135.6 1.9 collective-permute-start.3
  138.2 3.5 %align_columns.4 = f32[1,1024]{1,0:T(1,128)} custom-call(s32[3]{0:T(128)} %add_add_fusion.3.place, bf16[384,512]{1,0:T(8,128)(2,1)} %copy-done.2, bf16[1024,512]{1,0:T(8,128)(2,1)} %all-gather.2.cloned.1.call-done.weight, bf16[8,384,256]{2,1,0:T(8,128)(2,1)} %copy-done.1, bf16[8,384,256]{2,1,0:T(8,128)(2,1)} %collective-permute-done.12.other), custom_call_target="tpu_custom_call" | custom-call | tf_op jit(solution)/shard_map/align_columns/pallas_call | solution.py:258
  142.4 3.5 %align_columns.6 = f32[1,1024]{1,0:T(1,128)} custom-call(s32[3]{0:T(128)} %add_add_fusion.1.place, bf16[384,512]{1,0:T(8,128)(2,1)} %copy-done.2, bf16[1024,512]{1,0:T(8,128)(2,1)} %collective-permute-done.2.weight, bf16[8,384,256]{2,1,0:T(8,128)(2,1)} %copy-done.1, bf16[8,384,256]{2,1,0:T(8,128)(2,1)} %collective-permute-done.12.other), custom_call_target="tpu_custom_call" | custom-call | tf_op jit(solution)/shard_map/align_columns/pallas_call | solution.py:258
  145.9 3.7 %align_columns.5 = f32[1,1024]{1,0:T(1,128)} custom-call(s32[3]{0:T(128)} %add_add_fusion.2.place, bf16[384,512]{1,0:T(8,128)(2,1)} %copy-done.2, bf16[1024,512]{1,0:T(8,128)(2,1)} %collective-permute-done.weight, bf16[8,384,256]{2,1,0:T(8,128)(2,1)} %copy-done.1, bf16[8,384,256]{2,1,0:T(8,128)(2,1)} %collective-permute-done.12.other), custom_call_target="tpu_custom_call" | custom-call | tf_op jit(solution)/shard_map/align_columns/pallas_call | solution.py:258
  150.4 2.0 collective-permute-done.3
  152.3 1.1 constant_dynamic-update-slice_fusion.8.weight
  153.4 1.0 copy-done.5
  154.4 3.5 %align_columns.7 = f32[1,1024]{1,0:T(1,128)} custom-call(s32[3]{0:T(128)} %add_add_fusion.place, bf16[384,512]{1,0:T(8,128)(2,1)} %copy-done.2, bf16[1024,512]{1,0:T(8,128)(2,1)} %copy-done.5, bf16[8,384,256]{2,1,0:T(8,128)(2,1)} %copy-done.1, bf16[8,384,256]{2,1,0:T(8,128)(2,1)} %collective-permute-done.12.other), custom_call_target="tpu_custom_call" | custom-call | tf_op jit(solution)/shard_map/align_columns/pallas_call | solution.py:258
  158.6 1.4 convert_reduce_fusion
  160.1 1.1 fusion.29
  161.3 1.9 collective-permute-start.13
  163.2 1.1 collective-permute-done.13
  164.4 1.9 collective-permute-start.14
  166.9 3.3 %all-to-all-start.4 = ((f32[4,1,1024]{2,1,0:T(1,128)}), f32[4,1,1024]{2,1,0:T(1,128)S(1)}, u32[]{:S(2)}, u32[]{:S(2)}) async-start(f32[4,1,1024]{2,1,0:T(1,128)} %copy.28), calls=%async_computation.4 | async-start | bytes 32768 | tf_op jit(solution)/shard_map/all_to_all | solution.py:173
  170.2 6.2 %collective-permute-start.15 = (f32[32,128]{1,0:T(8,128)S(1)}, f32[32,128]{1,0:T(8,128)S(1)}, u32[]{:S(2)}, u32[]{:S(2)}) collective-permute-start(f32[32,128]{1,0:T(8,128)S(1)} %add.156), channel_id=1, source_target_pairs={{0,4},{1,5},{2,6},{3,7},{4,0},{5,1},{6,2},{7,3},{8,12},{9,13},{10,... | collective-permute-start | bytes 49160 | tf_op jit(solution)/shard_map/ppermute | solution.py:278
  177.1 1.2 collective-permute-done.15
  178.3 10.8 %collective-permute-start.16 = (f32[32,128]{1,0:T(8,128)S(1)}, f32[32,128]{1,0:T(8,128)S(1)}, u32[]{:S(2)}, u32[]{:S(2)}) collective-permute-start(f32[32,128]{1,0:T(8,128)S(1)} %add.157), channel_id=1, source_target_pairs={{0,8},{1,9},{2,10},{3,11},{4,12},{5,13},{6,14},{7,15},{8,0},{9,1},... | collective-permute-start | bytes 49160 | tf_op jit(solution)/shard_map/ppermute | solution.py:278
  189.2 1.6 collective-permute-done.16
  192.2 1.1 broadcast_in_dim.23.total
  194.0 4.5 %hidden_weight.4 = (f32[384,512]{1,0:T(8,128)}, f32[384,32]{1,0:T(8,128)}) custom-call(s32[3]{0:T(128)} %add_add_fusion.3.place, f32[1,4096]{1,0:T(1,128)} %get-tuple-element.44.scale, bf16[32,4096]{1,0:T(8,128)(2,1)} %bitcast.99, bf16[1024,512]{1,0:T(8,128)(2,1)} %all-gather.2.cloned.1.call-done.weight, bf16[8,384,256]{2,1,0:T(8,128)(2,1)} %copy-done.1, ...), custom_call_target="tpu_custom_call" | custom-call | tf_op jit(solution)/shard_map/hidden_weight/pallas_call | solution.py:228
  198.4 4.5 %hidden_weight.5 = (f32[384,512]{1,0:T(8,128)}, f32[384,32]{1,0:T(8,128)}) custom-call(s32[3]{0:T(128)} %add_add_fusion.2.place, f32[1,4096]{1,0:T(1,128)} %get-tuple-element.44.scale, bf16[32,4096]{1,0:T(8,128)(2,1)} %bitcast.100, bf16[1024,512]{1,0:T(8,128)(2,1)} %collective-permute-done.weight, bf16[8,384,256]{2,1,0:T(8,128)(2,1)} %copy-done.1, ...), custom_call_target="tpu_custom_call" | custom-call | tf_op jit(solution)/shard_map/hidden_weight/pallas_call | solution.py:228
  202.9 4.5 %hidden_weight.6 = (f32[384,512]{1,0:T(8,128)}, f32[384,32]{1,0:T(8,128)}) custom-call(s32[3]{0:T(128)} %add_add_fusion.1.place, f32[1,4096]{1,0:T(1,128)} %get-tuple-element.44.scale, bf16[32,4096]{1,0:T(8,128)(2,1)} %bitcast.101, bf16[1024,512]{1,0:T(8,128)(2,1)} %collective-permute-done.2.weight, bf16[8,384,256]{2,1,0:T(8,128)(2,1)} %copy-done.1, ...), custom_call_target="tpu_custom_call" | custom-call | tf_op jit(solution)/shard_map/hidden_weight/pallas_call | solution.py:228
  207.4 4.5 %hidden_weight.7 = (f32[384,512]{1,0:T(8,128)}, f32[384,32]{1,0:T(8,128)}) custom-call(s32[3]{0:T(128)} %add_add_fusion.place, f32[1,4096]{1,0:T(1,128)} %get-tuple-element.44.scale, bf16[32,4096]{1,0:T(8,128)(2,1)} %bitcast.102, bf16[1024,512]{1,0:T(8,128)(2,1)} %copy-done.5, bf16[8,384,256]{2,1,0:T(8,128)(2,1)} %copy-done.1, ...), custom_call_target="tpu_custom_call" | custom-call | tf_op jit(solution)/shard_map/hidden_weight/pallas_call | solution.py:228
  211.8 1.2 fusion.27
  213.0 1.2 add_convert_fusion
  215.1 10.0 %all-to-all-start.5 = ((bf16[32,12,512]{2,1,0:T(8,128)(2,1)}), bf16[32,12,512]{2,1,0:T(8,128)(2,1)S(1)}, u32[]{:S(2)}, u32[]{:S(2)}) async-start(bf16[32,12,512]{2,1,0:T(8,128)(2,1)} %reshape.184), calls=%async_computation.5 | async-start | bytes 1048576 | tf_op jit(solution)/shard_map/all_to_all | solution.py:82
  225.1 1.5 convolution_bitcast_fusion.2
  226.9 1.5 convolution_bitcast_fusion
  228.4 2.2 fusion.3
  231.8 9.2 %all-to-all-done.5 = bf16[32,12,512]{2,1,0:T(8,128)(2,1)S(1)} async-done(((bf16[32,12,512]{2,1,0:T(8,128)(2,1)}), bf16[32,12,512]{2,1,0:T(8,128)(2,1)S(1)}, u32[]{:S(2)}, u32[]{:S(2)}) %all-to-all-start.5) | async-done | bytes 393248 | tf_op jit(solution)/shard_map/all_to_all | solution.py:82
  241.2 0.9 convolution_convert_fusion.2
  (117 shorter events, 17.1 us)
Async XLA Ops:
  7.2 1.8 copy-start
  7.2 17.2 %copy-start.4 = (bf16[1,32,4096]{2,1,0:T(8,128)(2,1)S(1)}, bf16[1,32,4096]{2,1,0:T(8,128)(2,1)}, u32[]{:S(2)}) copy-start(bf16[1,32,4096]{2,1,0:T(8,128)(2,1)} %param.14) | copy-start | bytes 786436
  7.2 17.5 %copy-start.8 = (bf16[1,512,32]{1,2,0:T(8,128)(2,1)S(1)}, bf16[1,512,32]{1,2,0:T(8,128)(2,1)}, u32[]{:S(2)}) copy-start(bf16[1,512,32]{1,2,0:T(8,128)(2,1)} %param.13) | copy-start | bytes 98308
  9.9 15.6 %copy-start.9 = (bf16[128,512]{1,0:T(8,128)(2,1)S(1)}, bf16[128,512]{1,0:T(8,128)(2,1)}, u32[]{:S(2)}) copy-start(bf16[128,512]{1,0:T(8,128)(2,1)} %param.8) | copy-start | bytes 393220
  9.9 25.0 %all-to-all-start = ((bf16[32,12,256]{2,1,0:T(8,128)(2,1)}), bf16[32,12,256]{2,1,0:T(8,128)(2,1)S(1)}, u32[]{:S(2)}, u32[]{:S(2)}) async-start(bf16[32,12,256]{2,1,0:T(8,128)(2,1)} %reshape.175), calls=%async_computation | async-start | bytes 524288 | tf_op jit(solution)/shard_map/all_to_all | solution.py:82
  22.7 69.8 %all-gather.2.cloned.1.call-start = ((), (), s32[]{:S(2)}) async-start(), calls=%async_computation.6 | async-start | bytes 1179648 | tf_op jit(solution)/shard_map/all_gather | solution.py:85
  35.7 11.5 %collective-permute-start.4 = (bf16[384,256]{1,0:T(8,128)(2,1)}, bf16[384,256]{1,0:T(8,128)(2,1)}, u32[]{:S(2)}, u32[]{:S(2)}) collective-permute-start(bf16[384,256]{1,0:T(8,128)(2,1)} %reshape.176), channel_id=1, source_target_pairs={{2,0},{3,1},{4,2},{5,3},{6,4},{7,5},{8,6},{9,7},{10,8},{11,9},{12,... | collective-permute-start | bytes 589832 | tf_op jit(solution)/shard_map/ppermute | solution.py:100
  41.1 11.3 %collective-permute-start.8 = (bf16[384,256]{1,0:T(8,128)(2,1)}, bf16[384,256]{1,0:T(8,128)(2,1)}, u32[]{:S(2)}, u32[]{:S(2)}) collective-permute-start(bf16[384,256]{1,0:T(8,128)(2,1)} %reshape.176), channel_id=1, source_target_pairs={{14,0},{15,1},{0,2},{1,3},{2,4},{3,5},{4,6},{5,7},{6,8},{7,9},{8,1... | collective-permute-start | bytes 589832 | tf_op jit(solution)/shard_map/ppermute | solution.py:100
  43.0 12.3 %all-to-all-start.1 = ((bf16[4,32,1536]{2,1,0:T(8,128)(2,1)}), bf16[4,32,1536]{2,1,0:T(8,128)(2,1)}, u32[]{:S(2)}, u32[]{:S(2)}) async-start(bf16[4,32,1536]{2,1,0:T(8,128)(2,1)} %pad_maximum_fusion.1), calls=%async_computation.1 | async-start | bytes 786432 | tf_op jit(solution)/shard_map/all_to_all | solution.py:121
  47.2 17.5 %collective-permute-start.5 = (bf16[384,256]{1,0:T(8,128)(2,1)}, bf16[384,256]{1,0:T(8,128)(2,1)}, u32[]{:S(2)}, u32[]{:S(2)}) collective-permute-start(bf16[384,256]{1,0:T(8,128)(2,1)} %collective-permute-done.4), channel_id=1, source_target_pairs={{2,0},{3,1},{4,2},{5,3},{6,4},{7,5},{8,6},{9,7},{10,8},{11,9},{12,... | collective-permute-start | bytes 589832 | tf_op jit(solution)/shard_map/ppermute | solution.py:100
  52.4 17.5 %collective-permute-start.9 = (bf16[384,256]{1,0:T(8,128)(2,1)}, bf16[384,256]{1,0:T(8,128)(2,1)S(1)}, u32[]{:S(2)}, u32[]{:S(2)}) collective-permute-start(bf16[384,256]{1,0:T(8,128)(2,1)} %collective-permute-done.8), channel_id=1, source_target_pairs={{14,0},{15,1},{0,2},{1,3},{2,4},{3,5},{4,6},{5,7},{6,8},{7,9},{8,1... | collective-permute-start | bytes 589832 | tf_op jit(solution)/shard_map/ppermute | solution.py:100
  56.2 34.8 %all-to-all-start.2 = ((bf16[32,12,512]{2,1,0:T(8,128)(2,1)}), bf16[32,12,512]{2,1,0:T(8,128)(2,1)}, u32[]{:S(2)}, u32[]{:S(2)}) async-start(bf16[32,12,512]{2,1,0:T(8,128)(2,1)} %reshape.181), calls=%async_computation.2 | async-start | bytes 1048576 | tf_op jit(solution)/shard_map/all_to_all | solution.py:82
  64.7 15.9 %collective-permute-start.6 = (bf16[384,256]{1,0:T(8,128)(2,1)}, bf16[384,256]{1,0:T(8,128)(2,1)S(1)}, u32[]{:S(2)}, u32[]{:S(2)}) collective-permute-start(bf16[384,256]{1,0:T(8,128)(2,1)} %collective-permute-done.5), channel_id=1, source_target_pairs={{2,0},{3,1},{4,2},{5,3},{6,4},{7,5},{8,6},{9,7},{10,8},{11,9},{12,... | collective-permute-start | bytes 589832 | tf_op jit(solution)/shard_map/ppermute | solution.py:100
  69.9 8.8 %collective-permute-start.10 = (bf16[384,256]{1,0:T(8,128)(2,1)S(1)}, bf16[384,256]{1,0:T(8,128)(2,1)S(1)}, u32[]{:S(2)}, u32[]{:S(2)}) collective-permute-start(bf16[384,256]{1,0:T(8,128)(2,1)S(1)} %collective-permute-done.9), channel_id=1, source_target_pairs={{14,0},{15,1},{0,2},{1,3},{2,4},{3,5},{4,6},{5,7},{6,8},{7,9},{8,1... | collective-permute-start | bytes 589832 | tf_op jit(solution)/shard_map/ppermute | solution.py:100
  78.6 7.7 %collective-permute-start.11 = (bf16[192,256]{1,0:T(8,128)(2,1)S(1)}, bf16[192,256]{1,0:T(8,128)(2,1)S(1)}, u32[]{:S(2)}, u32[]{:S(2)}) collective-permute-start(bf16[192,256]{1,0:T(8,128)(2,1)S(1)} %slice.212), channel_id=1, source_target_pairs={{14,0},{15,1},{0,2},{1,3},{2,4},{3,5},{4,6},{5,7},{6,8},{7,9},{8,1... | collective-permute-start | bytes 294920 | tf_op jit(solution)/shard_map/ppermute | solution.py:100
  80.6 7.3 %collective-permute-start.7 = (bf16[192,256]{1,0:T(8,128)(2,1)S(1)}, bf16[192,256]{1,0:T(8,128)(2,1)S(1)}, u32[]{:S(2)}, u32[]{:S(2)}) collective-permute-start(bf16[192,256]{1,0:T(8,128)(2,1)S(1)} %slice.211), channel_id=1, source_target_pairs={{2,0},{3,1},{4,2},{5,3},{6,4},{7,5},{8,6},{9,7},{10,8},{11,9},{12,... | collective-permute-start | bytes 294920 | tf_op jit(solution)/shard_map/ppermute | solution.py:100
  88.9 6.9 %copy-start.1 = (bf16[8,384,256]{2,1,0:T(8,128)(2,1)}, bf16[8,384,256]{2,1,0:T(8,128)(2,1)S(1)}, u32[]{:S(2)}) copy-start(bf16[8,384,256]{2,1,0:T(8,128)(2,1)S(1)} %bitcast_dynamic-update-slice_fusion.mine) | copy-start | bytes 4718596
  89.0 5.3 %copy-start.10 = (f32[128,128]{1,0:T(8,128)S(1)}, f32[128,128]{1,0:T(8,128)}, u32[]{:S(2)}) copy-start(f32[128,128]{1,0:T(8,128)} %convolution_select_fusion) | copy-start | bytes 196612
  89.0 49.2 %collective-permute-start.12 = (bf16[8,384,256]{2,1,0:T(8,128)(2,1)S(1)}, bf16[8,384,256]{2,1,0:T(8,128)(2,1)}, u32[]{:S(2)}, u32[]{:S(2)}) collective-permute-start(bf16[8,384,256]{2,1,0:T(8,128)(2,1)S(1)} %bitcast_dynamic-update-slice_fusion.mine), channel_id=1, source_target_pairs={{0,1},{1,0},{2,3},{3,2},{4,5},{5,4},{6,7},{7,6},{8,9},{9,8},{10,11... | collective-permute-start | bytes 4718600 | tf_op jit(solution)/shard_map/ppermute | solution.py:109
  92.2 3.7 %copy-start.2 = (bf16[384,512]{1,0:T(8,128)(2,1)}, bf16[384,512]{1,0:T(8,128)(2,1)S(1)}, u32[]{:S(2)}) copy-start(bf16[384,512]{1,0:T(8,128)(2,1)S(1)} %reshape.182.rows_in) | copy-start | bytes 1179652
  97.7 28.0 %collective-permute-start = (bf16[1024,512]{1,0:T(8,128)(2,1)}, bf16[1024,512]{1,0:T(8,128)(2,1)}, u32[]{:S(2)}, u32[]{:S(2)}) collective-permute-start(bf16[1024,512]{1,0:T(8,128)(2,1)} %all-gather.2.cloned.1.call-done.weight), channel_id=1, source_target_pairs={{128,0},{144,16},{160,32},{176,48},{192,64},{208,80},{224,96},{240... | collective-permute-start | bytes 3145736 | tf_op jit(solution)/shard_map/ppermute | solution.py:197
  102.4 31.4 %collective-permute-start.2 = (bf16[1024,512]{1,0:T(8,128)(2,1)}, bf16[1024,512]{1,0:T(8,128)(2,1)}, u32[]{:S(2)}, u32[]{:S(2)}) collective-permute-start(bf16[1024,512]{1,0:T(8,128)(2,1)} %all-gather.2.cloned.1.call-done.weight), channel_id=1, source_target_pairs={{384,0},{400,16},{416,32},{432,48},{448,64},{464,80},{480,96},{496... | collective-permute-start | bytes 3145736 | tf_op jit(solution)/shard_map/ppermute | solution.py:197
  105.7 52.9 %all-to-all-start.3 = ((bf16[16,224,128]{2,1,0:T(8,128)(2,1)}), bf16[16,224,128]{2,1,0:T(8,128)(2,1)}, u32[]{:S(2)}, u32[]{:S(2)}) async-start(bf16[16,224,128]{2,1,0:T(8,128)(2,1)} %pad_maximum_fusion), calls=%async_computation.3 | async-start | bytes 1835008 | tf_op jit(solution)/shard_map/all_to_all | solution.py:157
  127.6 22.7 %collective-permute-start.1 = (bf16[512,512]{1,0:T(8,128)(2,1)}, bf16[512,512]{1,0:T(8,128)(2,1)S(1)}, u32[]{:S(2)}, u32[]{:S(2)}) collective-permute-start(bf16[512,512]{1,0:T(8,128)(2,1)} %slice.209), channel_id=1, source_target_pairs={{128,0},{144,16},{160,32},{176,48},{192,64},{208,80},{224,96},{240... | collective-permute-start | bytes 1572872 | tf_op jit(solution)/shard_map/ppermute | solution.py:197
  135.6 16.7 %collective-permute-start.3 = (bf16[512,512]{1,0:T(8,128)(2,1)}, bf16[512,512]{1,0:T(8,128)(2,1)}, u32[]{:S(2)}, u32[]{:S(2)}) collective-permute-start(bf16[512,512]{1,0:T(8,128)(2,1)} %slice.210), channel_id=1, source_target_pairs={{384,0},{400,16},{416,32},{432,48},{448,64},{464,80},{480,96},{496... | collective-permute-start | bytes 1572872 | tf_op jit(solution)/shard_map/ppermute | solution.py:197
  145.9 4.4 %copy-start.12 = (f32[1,1024]{1,0:T(1,128)S(1)}, f32[1,1024]{1,0:T(1,128)}, u32[]{:S(2)}) copy-start(f32[1,1024]{1,0:T(1,128)} %align_columns.6) | copy-start | bytes 12292
  153.4 1.0 copy-start.5
  157.9 32.9 %copy-start.11 = (f32[1,4096]{1,0:T(1,128)S(1)}, f32[1,4096]{1,0:T(1,128)}, u32[]{:S(2)}) copy-start(f32[1,4096]{1,0:T(1,128)} %param.15) | copy-start | bytes 49156
  158.6 33.3 %copy-start.6 = (bf16[1024,512]{1,0:T(8,128)(2,1)S(1)}, bf16[1024,512]{1,0:T(8,128)(2,1)}, u32[]{:S(2)}) copy-start(bf16[1024,512]{1,0:T(8,128)(2,1)} %copy-done.5) | copy-start | bytes 3145732
  161.3 3.1 %collective-permute-start.13 = (f32[32,128]{1,0:T(8,128)S(1)}, f32[32,128]{1,0:T(8,128)S(1)}, u32[]{:S(2)}, u32[]{:S(2)}) collective-permute-start(f32[32,128]{1,0:T(8,128)S(1)} %bitcast.109), channel_id=1, source_target_pairs={{0,1},{1,0},{2,3},{3,2},{4,5},{5,4},{6,7},{7,6},{8,9},{9,8},{10,11... | collective-permute-start | bytes 49160 | tf_op jit(solution)/shard_map/ppermute | solution.py:278
  164.4 5.8 %collective-permute-start.14 = (f32[32,128]{1,0:T(8,128)S(1)}, f32[32,128]{1,0:T(8,128)S(1)}, u32[]{:S(2)}, u32[]{:S(2)}) collective-permute-start(f32[32,128]{1,0:T(8,128)S(1)} %add.155), channel_id=1, source_target_pairs={{0,2},{1,3},{2,0},{3,1},{4,6},{5,7},{6,4},{7,5},{8,10},{9,11},{10,... | collective-permute-start | bytes 49160 | tf_op jit(solution)/shard_map/ppermute | solution.py:278
  166.9 22.2 %all-to-all-start.4 = ((f32[4,1,1024]{2,1,0:T(1,128)}), f32[4,1,1024]{2,1,0:T(1,128)S(1)}, u32[]{:S(2)}, u32[]{:S(2)}) async-start(f32[4,1,1024]{2,1,0:T(1,128)} %copy.28), calls=%async_computation.4 | async-start | bytes 32768 | tf_op jit(solution)/shard_map/all_to_all | solution.py:173
  170.2 8.1 %collective-permute-start.15 = (f32[32,128]{1,0:T(8,128)S(1)}, f32[32,128]{1,0:T(8,128)S(1)}, u32[]{:S(2)}, u32[]{:S(2)}) collective-permute-start(f32[32,128]{1,0:T(8,128)S(1)} %add.156), channel_id=1, source_target_pairs={{0,4},{1,5},{2,6},{3,7},{4,0},{5,1},{6,2},{7,3},{8,12},{9,13},{10,... | collective-permute-start | bytes 49160 | tf_op jit(solution)/shard_map/ppermute | solution.py:278
  176.4 54.8 %collective-permute-start.17 = (f32[32,256]{1,0:T(8,128)S(1)}, f32[32,256]{1,0:T(8,128)S(1)}, u32[]{:S(2)}, u32[]{:S(2)}) collective-permute-start(f32[32,256]{1,0:T(8,128)S(1)} %pad_maximum_fusion.2), channel_id=1, source_target_pairs={{0,0},{1,1},{2,2},{3,3},{4,128},{5,129},{6,130},{7,131},{8,256},{9... | collective-permute-start | bytes 98312 | tf_op jit(solution)/shard_map/ppermute | solution.py:189
  178.3 12.5 %collective-permute-start.16 = (f32[32,128]{1,0:T(8,128)S(1)}, f32[32,128]{1,0:T(8,128)S(1)}, u32[]{:S(2)}, u32[]{:S(2)}) collective-permute-start(f32[32,128]{1,0:T(8,128)S(1)} %add.157), channel_id=1, source_target_pairs={{0,8},{1,9},{2,10},{3,11},{4,12},{5,13},{6,14},{7,15},{8,0},{9,1},... | collective-permute-start | bytes 49160 | tf_op jit(solution)/shard_map/ppermute | solution.py:278
  214.2 12.4 %copy-start.3 = (bf16[384,512]{1,0:T(8,128)(2,1)S(1)}, bf16[384,512]{1,0:T(8,128)(2,1)}, u32[]{:S(2)}) copy-start(bf16[384,512]{1,0:T(8,128)(2,1)} %copy-done.2) | copy-start | bytes 1179652
  214.2 12.4 %copy-start.7 = (f32[384,32]{1,0:T(8,128)S(1)}, f32[384,32]{1,0:T(8,128)}, u32[]{:S(2)}) copy-start(f32[384,32]{1,0:T(8,128)} %get-tuple-element.26) | copy-start | bytes 147460
  215.1 25.9 %all-to-all-start.5 = ((bf16[32,12,512]{2,1,0:T(8,128)(2,1)}), bf16[32,12,512]{2,1,0:T(8,128)(2,1)S(1)}, u32[]{:S(2)}, u32[]{:S(2)}) async-start(bf16[32,12,512]{2,1,0:T(8,128)(2,1)} %reshape.184), calls=%async_computation.5 | async-start | bytes 1048576 | tf_op jit(solution)/shard_map/all_to_all | solution.py:82
Sparse Core Ops, SparseCore 0:
  26.2 45.8 all-gather.1

commit v3 on v1

v3 whole, which is shorter than its diff:
```python
import jax
import jax.numpy as jnp
from jax import lax
from jax.experimental import pallas as pl
from jax.experimental.pallas import tpu as pltpu
from jax.sharding import PartitionSpec as P

CAP = 12
NX = 4
EPSILON = 1e-06
BF = jnp.bfloat16
F32 = jnp.float32


def dot(left, right, dims, precision=None):
    return lax.dot_general(
        left, right, (dims, ((), ())), precision=precision, preferred_element_type=F32
    )


def row_targets(count_row, owner_slot, rows):
    ends = jnp.cumsum(count_row)
    starts = ends - count_row
    ids = jnp.arange(rows, dtype=jnp.int32)[None, :]
    inside = ((ids >= starts[:, None]) & (ids < ends[:, None])).astype(jnp.int32)
    shift = owner_slot * CAP - starts
    return jnp.sum(inside * shift[:, None], axis=0) + ids[0]


def align_kernel(place, rows_in, rows_low, weight, second, mine, other, joined, align, moment):
    z_cols = mine.shape[2]
    near = place[1] * z_cols
    for start, part in ((near, mine), (z_cols - near, other)):
        cols = pl.ds(pl.multiple_of(start, z_cols), z_cols)
        joined[:, cols] = part[0]
        products = dot(rows_low[...], part[0], ((0,), (0,)))
        moment[:, cols] = products
        projected = dot(rows_in[...], weight[cols, :], ((1,), (1,)))
        sums = jnp.sum(part[0].astype(F32) * projected, axis=0, keepdims=True)
        sums += jnp.sum(products * second[:, cols], axis=0, keepdims=True)
        align[:, cols] = sums


def on_device(acts, grads, counts, owner_slot, base_weight, adapter_a, adapter_b, magnitude):
    groups, shards = lax.axis_size("grp"), lax.axis_size("tp")
    nz = groups // NX
    rows, width = acts.shape
    out_width = grads.shape[1]
    rank = adapter_a.shape[2]
    t_cols, g_cols = out_width // shards, out_width // groups
    packed = groups * CAP
    z_cols = out_width // nz
    z_groups = [[i * nz + j for j in range(nz)] for i in range(NX)]
    x_groups = [[i * nz + j for i in range(NX)] for j in range(nz)]
    my_t = lax.axis_index("tp")
    my_part, my_core = my_t // 2 % (nz // 2), my_t % 2

    def exchange(values, axis, members=None):
        return lax.all_to_all(
            values, axis, split_axis=0, concat_axis=0, tiled=True, axis_index_groups=members
        )

    def to_owners(values):
        values = exchange(values.reshape(groups, CAP, values.shape[1]), "grp")
        return values.reshape(packed, values.shape[2])

    def arriving(values):
        values = values.reshape(-1, NX, nz, g_cols).transpose(0, 2, 1, 3)
        return values.reshape(-1, out_width)

    def natural(values):
        values = values.reshape(-1, nz, NX, g_cols).transpose(0, 2, 1, 3)
        return values.reshape(-1, out_width)

    shard = base_weight.T
    near = exchange(jnp.broadcast_to(shard[None], (NX,) + shard.shape), "grp", x_groups)
    weight = lax.all_gather(
        near.reshape(NX * g_cols, width), "grp", axis=0, tiled=True, axis_index_groups=z_groups
    )

    target = row_targets(counts[0], owner_slot, rows)
    place = (jnp.arange(packed, dtype=jnp.int32)[:, None] == target[None, :]).astype(BF)
    strip = lax.dynamic_slice(
        grads.reshape(rows, NX, nz, g_cols), (0, 0, my_t % nz, 0), (rows, NX, 1, g_cols)
    ).reshape(rows, z_cols)
    both = dot(place, jnp.concatenate([acts, strip], axis=1), ((1,), (0,))).astype(BF)
    both, near = lax.optimization_barrier((both, near))
    both = to_owners(both)
    rows_in, rows_grad_t = both[:, :width], both[:, width:]

    def along_y(values, step):
        pairs = [((i + 2 * step) % shards, i) for i in range(shards)]
        return lax.ppermute(values, "tp", pairs)

    n_parts, half = nz // 2, packed // 2
    above, below = along_y(rows_grad_t, 1), along_y(rows_grad_t, -1)
    far = jnp.concatenate([along_y(above[:half], 1), along_y(below[half:], -1)], axis=0)
    mine = jnp.stack([rows_grad_t, above, far, below])
    other = lax.ppermute(mine, "tp", [(i, i ^ 1) for i in range(shards)])

    first, second = adapter_a[0], arriving(adapter_b[0])
    first_t = first.T
    second_wide = second.astype(F32)
    gain = arriving(magnitude)
    gram = dot(first, first, ((0,), (0,)))
    gram_second = dot(gram, second_wide, ((1,), (0,)), lax.Precision.HIGHEST)
    rows_low = dot(rows_in, first, ((1,), (0,))).astype(BF)

    def lanes(values):
        return jnp.concatenate(
            [values[:, i : i + 128] for i in range(0, values.shape[1], 128)], axis=0
        )

    def unlanes(values, height):
        return jnp.concatenate(
            [values[i : i + height] for i in range(0, values.shape[0], height)], axis=1
        )

    def summed(values):
        return jnp.sum(exchange(values, "tp").astype(F32), axis=0)

    def to_all(values):
        return jnp.broadcast_to(values[None], (shards,) + values.shape)

    first_weight = dot(first_t, weight, ((1,), (1,)))
    square_base = jnp.sum(jnp.square(weight.astype(F32)), axis=1)
    squares = square_base[None, :] + jnp.sum(
        second_wide * (2.0 * first_weight + gram_second), axis=0, keepdims=True
    )

    wide = 2 * z_cols

    def fixed(*shape):
        return pl.BlockSpec(shape, lambda k, place: (0,) * len(shape))

    def chip(k, place):
        return lax.rem(place[0] + k, n_parts)

    block = pl.BlockSpec((1, packed, z_cols), lambda k, place: (k, 0, 0))
    rows_grad, align, first_moment = pl.pallas_call(
        align_kernel,
        grid_spec=pltpu.PrefetchScalarGridSpec(
            num_scalar_prefetch=1,
            grid=(n_parts,),
            in_specs=[
                fixed(packed, width),
                fixed(packed, rank),
                pl.BlockSpec((wide, width), lambda k, place: (chip(k, place), 0)),
                pl.BlockSpec((rank, wide), lambda k, place: (0, chip(k, place))),
                block,
                block,
            ],
            out_specs=[
                pl.BlockSpec((packed, wide), lambda k, place: (0, chip(k, place))),
                pl.BlockSpec((1, wide), lambda k, place: (0, chip(k, place))),
                pl.BlockSpec((rank, wide), lambda k, place: (0, chip(k, place))),
            ],
        ),
        out_shape=[
            jax.ShapeDtypeStruct((packed, out_width), BF),
            jax.ShapeDtypeStruct((1, out_width), F32),
            jax.ShapeDtypeStruct((rank, out_width), F32),
        ],
        compiler_params=pltpu.CompilerParams(vmem_limit_bytes=32 * 2**20),
        cost_estimate=pl.CostEstimate(
            flops=2 * packed * out_width * width,
            bytes_accessed=2 * out_width * (2 * packed + width),
            transcendentals=0,
        ),
        name="align_columns",
    )(jnp.stack([my_part, my_core]).astype(jnp.int32), rows_in, rows_low, weight, second_wide, mine, other)

    products = natural(jnp.concatenate([first_moment, first_weight + gram_second], axis=0))
    products = products.astype(BF)
    pieces = jnp.stack(
        [lanes(products[:, i : i + t_cols]) for i in range(0, out_width, t_cols)], axis=0
    )
    terms = jnp.concatenate([squares.reshape(-1, 128), align.reshape(-1, 128)], axis=0)
    n_terms = terms.shape[0]
    terms = summed(jnp.concatenate([to_all(terms.astype(BF)), pieces], axis=1))
    products = unlanes(terms[n_terms:], 2 * rank)
    moment_t, merged_t = products[:rank], products[rank:]
    terms = terms[:n_terms].reshape(2, out_width)
    norm = jnp.sqrt(terms[:1] + EPSILON)
    align = terms[1:]
    scale = gain / norm
    grad_gain = natural(align / norm)
    shrink = gain * align / (norm * norm * norm)

    hidden = (rows_grad.astype(F32) * scale).astype(BF)
    inner = dot(hidden, second, ((1,), (1,))).astype(BF)
    back = dot(hidden, weight, ((1,), (0,))) + dot(inner, first, ((1,), (1,)))
    row_grad = dot(place, to_owners(back.astype(BF)), ((0,), (0,))).astype(BF)

    shrunk = (second_wide * shrink).astype(BF)
    small = dot(second, shrunk, ((1,), (1,)))
    grad_a = (
        dot(inner, rows_in, ((0,), (0,)))
        - dot(shrunk, weight, ((1,), (0,)))
        - dot(small.astype(BF), first_t, ((0,), (0,)))
    )
    scale_t = lax.dynamic_slice(natural(scale), (0, my_t * t_cols), (1, t_cols))
    shrink_t = lax.dynamic_slice(natural(shrink), (0, my_t * t_cols), (1, t_cols))
    grad_b = moment_t * scale_t - merged_t * shrink_t
    return row_grad, grad_a.T[None], grad_b[None], grad_gain


def solution(mesh):
    in_specs = (
        P("grp", "tp"),
        P("grp", None),
        P("grp", None),
        P(),
        P("tp", "grp"),
        P("grp", "tp", None),
        P("grp", None, None),
        P("grp", None),
    )
    out_specs = (P("grp", "tp"), P("grp", "tp", None), P("grp", None, "tp"), P("grp", None))
    return jax.shard_map(
        on_device, mesh=mesh, in_specs=in_specs, out_specs=out_specs, check_vma=False
    )
```

time: 200 us -> 189 us (0.945)
  blocking collectives: 0 us -> 52.4 us
  waiting for transfers between devices: 76.2 us -> 43.3 us
  starting transfers between devices: 59.7 us -> 37.6 us
  matrix products: 22 us -> 11.2 us
  local copies, waits for them, and re-layouts: 19.8 us -> 12 us
  Pallas kernels: 0 us -> 5.54 us
  other arithmetic: 6.93 us -> 11.3 us
    all_to_all x0 -> x2, blocking collectives: none -> 52.4 us  [exchange(): lax.all_to_all(values, axis, split_axis=0, concat_axis=0, tiled=True, axi...]
    all_to_all x6 -> x2, starting transfers between devices: 44.4 us -> 9.49 us  [exchange(): lax.all_to_all(values, axis, split_axis=0, concat_axis=0, tiled=True, axi...]
    all_to_all x6 -> x2, waiting for transfers between devices: 51.8 us -> 32.2 us  [exchange(): lax.all_to_all(values, axis, split_axis=0, concat_axis=0, tiled=True, axi...]
    ppermute x5, starting transfers between devices: 15.2 us -> 28 us  [the longest x4 14.9 us: along_y(): return lax.ppermute(values, 'tp', pairs)]
    dot_general x14 -> x12, matrix products: 22 us -> 11.2 us  [dot(): lax.dot_general(left, right, (dims, ((), ())), precision=precision, prefe...]
    all_gather x2 -> x1, waiting for transfers between devices: 9.63 us -> 0.02 us  [on_device(): lax.all_gather(near.reshape(NX * g_cols, width), 'grp', axis=0, tiled=Tru...]
    dynamic_update_slice x3 -> x0, local copies, waits for them, and re-layouts: 5.77 us -> none  [on_device(): lax.dynamic_update_slice(weight, piece, ((my_x + step) % NX * x_cols, 0))]
    pallas_call x0 -> x1, Pallas kernels: none -> 5.54 us  [on_device(): pl.pallas_call(align_kernel, grid_spec=pltpu.PrefetchScalarGridSpec(num_s...]
  transfers between devices with their start and end apart: 13 -> 8, of which waited for: 8 -> 5; matrix products, arithmetic and copies ran while one was open for 24% -> 6% of each run, Pallas kernels for 0% -> 0%
where the time goes in v3:
time: 189 us; the launch traced here: 188 us
  blocking collectives  52.4 us (28%)
  waiting for transfers between devices  43.3 us (23%)
  starting transfers between devices  37.6 us (20%)
  between operations  14.7 us (8%)
  local copies, waits for them, and re-layouts  12 us (6%)
  other arithmetic  11.3 us (6%)
  matrix products  11.2 us (6%)
  Pallas kernels  5.54 us (3%)
    all_to_all x2, blocking collectives, exchange(): lax.all_to_all(values, axis, split_axis=0, concat_axis=0, tiled=True, axi...  52.4 us
    all_to_all x2, waiting for transfers between devices, exchange(): lax.all_to_all(values, axis, split_axis=0, concat_axis=0, tiled=True, axi...  32.2 us
    ppermute x4, starting transfers between devices, along_y(): return lax.ppermute(values, 'tp', pairs)  14.9 us
    ppermute x1, starting transfers between devices, on_device(): other = lax.ppermute(mine, 'tp', [(i, i ^ 1) for i in range(shards)])  13.1 us
    dot_general x12, matrix products, dot(): lax.dot_general(left, right, (dims, ((), ())), precision=precision, prefe...  11.2 us
    ppermute x4, waiting for transfers between devices, along_y(): return lax.ppermute(values, 'tp', pairs)  11 us
    all_to_all x2, starting transfers between devices, exchange(): lax.all_to_all(values, axis, split_axis=0, concat_axis=0, tiled=True, axi...  9.49 us
    pallas_call x1, Pallas kernels, on_device(): pl.pallas_call(align_kernel, grid_spec=pltpu.PrefetchScalarGridSpec(num_s...  5.54 us
  transfers between devices with their start and end apart: 8, of which 5 were waited for; matrix products, arithmetic and copies ran while one was open for 6% of the time, Pallas kernels for 0%

profile of v3, /device:TPU:1, one launch (start us, length us, event | category | flops | bytes accessed | tf_op | source)
XLA Modules:
  0.0 188.0 jit_solution(2828717273387597233)
XLA Ops:
  7.3 1.1 copy.79
  8.4 11.7 %all_to_all.20 = bf16[4,128,512]{2,1,0:T(8,128)(2,1)} all-to-all(bf16[4,128,512]{2,1,0:T(8,128)(2,1)S(1)} %broadcast_in_dim.8), channel_id=1, replica_groups={{0,128,256,384},{16,144,272,400},{32,160,288,416},{48,176,304,432},{64,..., dimensions={0} | all-to-all | bytes 1048576 | tf_op jit(solution)/shard_map/all_to_all | solution.py:59
  20.1 0.7 copy.77
  20.8 0.1 copy.76
  21.0 0.1 reduce
  21.1 0.1 copy.78
  21.3 0.1 select_reduce_fusion
  21.4 0.5 copy-done.13
  21.9 0.4 convolution_convert_fusion
  22.2 0.2 reshape.230
  22.4 40.7 %all_to_all.21 = bf16[32,12,1024]{2,1,0:T(8,128)(2,1)S(1)} all-to-all(bf16[32,12,1024]{2,1,0:T(8,128)(2,1)S(1)} %reshape.230), channel_id=1, replica_groups=mesh['grp'=32,'tp'=16] {'grp'}, dimensions={0} | all-to-all | bytes 1572864 | tf_op jit(solution)/shard_map/all_to_all | solution.py:59
  63.2 0.2 reshape.231
  63.4 0.1 slice_bitcast_fusion
  63.4 5.6 %collective-permute-start = (bf16[384,512]{1,0:T(8,128)(2,1)S(1)}, bf16[384,512]{1,0:T(8,128)(2,1)S(1)}, u32[]{:S(2)}, u32[]{:S(2)}) collective-permute-start(bf16[384,512]{1,0:T(8,128)(2,1)S(1)} %get-tuple-element.17), channel_id=1, source_target_pairs={{2,0},{3,1},{4,2},{5,3},{6,4},{7,5},{8,6},{9,7},{10,8},{11,9},{12,... | collective-permute-start | bytes 1179656 | tf_op jit(solution)/shard_map/ppermute | solution.py:93
  69.1 1.9 %collective-permute-start.2 = (bf16[384,512]{1,0:T(8,128)(2,1)S(1)}, bf16[384,512]{1,0:T(8,128)(2,1)S(1)}, u32[]{:S(2)}, u32[]{:S(2)}) collective-permute-start(bf16[384,512]{1,0:T(8,128)(2,1)S(1)} %get-tuple-element.17), channel_id=1, source_target_pairs={{14,0},{15,1},{0,2},{1,3},{2,4},{3,5},{4,6},{5,7},{6,8},{7,9},{8,1... | collective-permute-start | bytes 1179656 | tf_op jit(solution)/shard_map/ppermute | solution.py:93
  71.0 2.8 %collective-permute-done = bf16[384,512]{1,0:T(8,128)(2,1)S(1)} collective-permute-done((bf16[384,512]{1,0:T(8,128)(2,1)S(1)}, bf16[384,512]{1,0:T(8,128)(2,1)S(1)}, u32[]{:S(2)}, u32[]{:S(2)}) %collective-permute-start) | collective-permute-done | bytes 393248 | tf_op jit(solution)/shard_map/ppermute | solution.py:93
  73.8 5.4 %collective-permute-start.1 = (bf16[192,512]{1,0:T(8,128)(2,1)S(1)}, bf16[192,512]{1,0:T(8,128)(2,1)S(1)}, u32[]{:S(2)}, u32[]{:S(2)}) collective-permute-start(bf16[192,512]{1,0:T(8,128)(2,1)S(1)} %slice.235), channel_id=1, source_target_pairs={{2,0},{3,1},{4,2},{5,3},{6,4},{7,5},{8,6},{9,7},{10,8},{11,9},{12,... | collective-permute-start | bytes 589832 | tf_op jit(solution)/shard_map/ppermute | solution.py:93
  79.2 1.9 %collective-permute-start.3 = (bf16[192,512]{1,0:T(8,128)(2,1)S(1)}, bf16[192,512]{1,0:T(8,128)(2,1)S(1)}, u32[]{:S(2)}, u32[]{:S(2)}) collective-permute-start(bf16[192,512]{1,0:T(8,128)(2,1)S(1)} %slice.236), channel_id=1, source_target_pairs={{14,0},{15,1},{0,2},{1,3},{2,4},{3,5},{4,6},{5,7},{6,8},{7,9},{8,1... | collective-permute-start | bytes 589832 | tf_op jit(solution)/shard_map/ppermute | solution.py:93
  81.2 2.7 %collective-permute-done.1 = bf16[192,512]{1,0:T(8,128)(2,1)S(1)} collective-permute-done((bf16[192,512]{1,0:T(8,128)(2,1)S(1)}, bf16[192,512]{1,0:T(8,128)(2,1)S(1)}, u32[]{:S(2)}, u32[]{:S(2)}) %collective-permute-start.1) | collective-permute-done | bytes 196640 | tf_op jit(solution)/shard_map/ppermute | solution.py:93
  83.9 5.5 %collective-permute-done.3 = bf16[192,512]{1,0:T(8,128)(2,1)S(1)} collective-permute-done((bf16[192,512]{1,0:T(8,128)(2,1)S(1)}, bf16[192,512]{1,0:T(8,128)(2,1)S(1)}, u32[]{:S(2)}, u32[]{:S(2)}) %collective-permute-start.3) | collective-permute-done | bytes 196640 | tf_op jit(solution)/shard_map/ppermute | solution.py:93
  89.4 0.2 pad_maximum_fusion.mine
  89.6 13.1 %collective-permute-start.4 = (bf16[4,384,512]{2,1,0:T(8,128)(2,1)S(1)}, bf16[4,384,512]{2,1,0:T(8,128)(2,1)}, u32[]{:S(2)}, u32[]{:S(2)}) collective-permute-start(bf16[4,384,512]{2,1,0:T(8,128)(2,1)S(1)} %pad_maximum_fusion.mine), channel_id=1, source_target_pairs={{0,1},{1,0},{2,3},{3,2},{4,5},{5,4},{6,7},{7,6},{8,9},{9,8},{10,11... | collective-permute-start | bytes 4718600 | tf_op jit(solution)/shard_map/ppermute | solution.py:99
  102.9 0.7 copy-done.9
  103.6 0.1 copy.81
  103.7 0.9 reshape.233
  104.6 1.0 convert_element_type.61.second
  105.6 0.1 pad_add_fusion.place
  105.6 0.1 fusion.29
  105.8 0.2 convolution_convert_fusion.2
  106.0 0.2 copy.82.rows_low
  106.2 2.2 %copy-done.1 = bf16[4096,512]{1,0:T(8,128)(2,1)S(1)} copy-done((bf16[4096,512]{1,0:T(8,128)(2,1)S(1)}, bf16[4096,512]{1,0:T(8,128)(2,1)}, u32[]{:S(2)}) %copy-start.1) | copy-done | bytes 4194328
  108.4 5.5 %align_columns.1 = (bf16[384,4096]{1,0:T(8,128)(2,1)S(1)}, f32[1,4096]{1,0:T(1,128)S(1)}, f32[32,4096]{1,0:T(8,128)S(1)}) custom-call(s32[2]{0:T(128)S(1)} %pad_add_fusion.place, bf16[384,512]{1,0:T(8,128)(2,1)S(1)} %get-tuple-element.18.rows_in, bf16[384,32]{1,0:T(8,128)(2,1)S(1)} %copy.82.rows_low, bf16[4096,512]{1,0:T(8,128)(2,1)S(1)} %copy-done.1, ...), custom_call_target="tpu_custom_call" | custom-call | flops 1610612736 | bytes 10485760 | tf_op jit(solution)/shard_map/align_columns/pallas_call | solution.py:140
  114.0 1.3 fusion.31
  115.3 0.5 multiply_reduce_fusion.1
  115.9 0.4 convert_element_type.64
  116.2 0.1 copy.84
  116.3 0.2 copy.117
  116.6 0.1 fusion.44
  116.7 0.1 convert_reduce_fusion.1
  116.7 3.1 %multiply_reduce_fusion = f32[4096]{0:T(1024)S(1)} fusion(bf16[4096,512]{1,0:T(8,128)(2,1)} %all-gather.2.cloned.1.call-done.weight), kind=kLoop, calls=%fused_computation | loop fusion | flops 6287360 | bytes 4210688 | tf_op jit(solution)/shard_map/reduce_sum | solution.py:126
  120.1 1.0 pad_maximum_fusion.1
  121.1 4.2 %all-to-all-start.2 = ((bf16[16,192,128]{2,1,0:T(8,128)(2,1)}), bf16[16,192,128]{2,1,0:T(8,128)(2,1)}, u32[]{:S(2)}, u32[]{:S(2)}) async-start(bf16[16,192,128]{2,1,0:T(8,128)(2,1)} %pad_maximum_fusion.1), calls=%async_computation.2 | async-start | bytes 1572864 | tf_op jit(solution)/shard_map/all_to_all | solution.py:59
  125.3 0.6 copy.83
  125.9 22.1 %all-to-all-done.2 = bf16[16,192,128]{2,1,0:T(8,128)(2,1)} async-done(((bf16[16,192,128]{2,1,0:T(8,128)(2,1)}), bf16[16,192,128]{2,1,0:T(8,128)(2,1)}, u32[]{:S(2)}, u32[]{:S(2)}) %all-to-all-start.2) | async-done | bytes 786464 | tf_op jit(solution)/shard_map/all_to_all | solution.py:59
  148.0 1.2 convert_reduce_fusion
  149.2 0.6 fusion.38
  149.9 0.7 fusion.34
  150.6 1.0 fusion.6
  151.7 0.3 fusion.27
  152.0 0.8 copy-done.2
  152.8 0.8 convolution_bitcast_fusion.1
  153.6 0.8 convolution_subtract_fusion
  154.5 2.6 %fusion.3 = bf16[384,512]{1,0:T(8,128)(2,1)} fusion(f32[384,512]{1,0:T(8,128)S(1)} %fusion.27, bf16[4096,512]{1,0:T(8,128)(2,1)S(1)} %copy-done.2, bf16[384,4096]{1,0:T(8,128)(2,1)S(1)} %copy-done.4, f32[4096]{0:T(1024)S(1)} %get-tuple-element.52), kind=kOutput, calls=%fused_computation.8 | convolution fusion | flops 1615724544 | bytes 8536064 | tf_op jit(solution)/shard_map/dot_general | solution.py:16
  157.0 1.9 %reshape.236 = bf16[32,12,512]{2,1,0:T(8,128)(2,1)} reshape(bf16[384,512]{1,0:T(8,128)(2,1)} %fusion.3) | data formatting | bytes 786432 | tf_op jit(solution)/shard_map/reshape | solution.py:64
  158.9 5.3 %all-to-all-start.3 = ((bf16[32,12,512]{2,1,0:T(8,128)(2,1)}), bf16[32,12,512]{2,1,0:T(8,128)(2,1)S(1)}, u32[]{:S(2)}, u32[]{:S(2)}) async-start(bf16[32,12,512]{2,1,0:T(8,128)(2,1)} %reshape.236), calls=%async_computation.3 | async-start | bytes 1048576 | tf_op jit(solution)/shard_map/all_to_all | solution.py:59
  164.2 0.8 copy_multiply_fusion.1
  165.0 0.7 fusion.35
  165.7 0.7 multiply_bitcast_fusion
  166.5 0.6 copy.95
  167.1 2.2 %fusion.5 = f32[1,512,32]{1,2,0:T(8,128)} fusion(f32[512,32]{0,1:T(8,128)} %convolution_subtract_fusion, bf16[32,4,8,128]{3,2,1,0:T(8,128)(2,1)} %bitcast.177, f32[8,4,128]{2,1,0:T(4,128)S(1)} %copy.89, bf16[1,512,32]{1,2,0:T(8,128)(2,1)S(1)} %copy-done), kind=kOutput, calls=%fused_computation.12 | convolution fusion | flops 9847808 | bytes 442368 | tf_op jit(solution)/shard_map/dot_general | solution.py:16
  169.3 0.6 fusion.24
  169.9 10.2 %all-to-all-done.3 = bf16[32,12,512]{2,1,0:T(8,128)(2,1)S(1)} async-done(((bf16[32,12,512]{2,1,0:T(8,128)(2,1)}), bf16[32,12,512]{2,1,0:T(8,128)(2,1)S(1)}, u32[]{:S(2)}, u32[]{:S(2)}) %all-to-all-start.3) | async-done | bytes 393248 | tf_op jit(solution)/shard_map/all_to_all | solution.py:59
  180.1 0.1 reshape.237
  180.2 0.9 convolution_convert_fusion.1
  (69 shorter events, 0.7 us)
Async XLA Ops:
  7.2 98.5 %copy-start = (bf16[1,512,32]{1,2,0:T(8,128)(2,1)S(1)}, bf16[1,512,32]{1,2,0:T(8,128)(2,1)}, u32[]{:S(2)}) copy-start(bf16[1,512,32]{1,2,0:T(8,128)(2,1)} %param.13) | copy-start | bytes 98308
  7.2 12.9 %copy-start.8 = (bf16[128,4096]{1,0:T(8,128)(2,1)S(1)}, bf16[128,4096]{1,0:T(8,128)(2,1)}, u32[]{:S(2)}) copy-start(bf16[128,4096]{1,0:T(8,128)(2,1)} %param.9) | copy-start | bytes 3145732
  7.2 13.6 %copy-start.15 = (s32[1,24]{1,0:T(1,128)S(1)}, s32[1,24]{1,0:T(1,128)}, u32[]{:S(2)}) copy-start(s32[1,24]{1,0:T(1,128)} %param.10) | copy-start | bytes 292
  7.2 13.9 %copy-start.12 = (bf16[128,512]{1,0:T(8,128)(2,1)S(1)}, bf16[128,512]{1,0:T(8,128)(2,1)}, u32[]{:S(2)}) copy-start(bf16[128,512]{1,0:T(8,128)(2,1)} %param.8) | copy-start | bytes 393220
  7.2 14.0 %copy-start.16 = (s32[24]{0:T(128)S(1)}, s32[24]{0:T(128)}, u32[]{:S(2)}) copy-start(s32[24]{0:T(128)} %param.11) | copy-start | bytes 292
  7.2 99.0 %all-gather.2.cloned.1.call-start = ((), (), s32[]{:S(2)}) async-start(), calls=%async_computation.4 | async-start | bytes 4718592 | tf_op jit(solution)/shard_map/all_gather | solution.py:77
  21.4 0.5 copy-start.13
  63.3 42.4 %copy-start.5 = (bf16[384,1024]{1,0:T(8,128)(2,1)}, bf16[384,1024]{1,0:T(8,128)(2,1)S(1)}, u32[]{:S(2)}) copy-start(bf16[384,1024]{1,0:T(8,128)(2,1)S(1)} %reshape.231) | copy-start | bytes 2359300
  63.3 39.4 %copy-start.10 = (bf16[1,32,4096]{2,1,0:T(8,128)(2,1)S(1)}, bf16[1,32,4096]{2,1,0:T(8,128)(2,1)}, u32[]{:S(2)}) copy-start(bf16[1,32,4096]{2,1,0:T(8,128)(2,1)} %param.14) | copy-start | bytes 786436
  63.4 10.3 %collective-permute-start = (bf16[384,512]{1,0:T(8,128)(2,1)S(1)}, bf16[384,512]{1,0:T(8,128)(2,1)S(1)}, u32[]{:S(2)}, u32[]{:S(2)}) collective-permute-start(bf16[384,512]{1,0:T(8,128)(2,1)S(1)} %get-tuple-element.17), channel_id=1, source_target_pairs={{2,0},{3,1},{4,2},{5,3},{6,4},{7,5},{8,6},{9,7},{10,8},{11,9},{12,... | collective-permute-start | bytes 1179656 | tf_op jit(solution)/shard_map/ppermute | solution.py:93
  69.1 10.2 %collective-permute-start.2 = (bf16[384,512]{1,0:T(8,128)(2,1)S(1)}, bf16[384,512]{1,0:T(8,128)(2,1)S(1)}, u32[]{:S(2)}, u32[]{:S(2)}) collective-permute-start(bf16[384,512]{1,0:T(8,128)(2,1)S(1)} %get-tuple-element.17), channel_id=1, source_target_pairs={{14,0},{15,1},{0,2},{1,3},{2,4},{3,5},{4,6},{5,7},{6,8},{7,9},{8,1... | collective-permute-start | bytes 1179656 | tf_op jit(solution)/shard_map/ppermute | solution.py:93
  73.8 10.1 %collective-permute-start.1 = (bf16[192,512]{1,0:T(8,128)(2,1)S(1)}, bf16[192,512]{1,0:T(8,128)(2,1)S(1)}, u32[]{:S(2)}, u32[]{:S(2)}) collective-permute-start(bf16[192,512]{1,0:T(8,128)(2,1)S(1)} %slice.235), channel_id=1, source_target_pairs={{2,0},{3,1},{4,2},{5,3},{6,4},{7,5},{8,6},{9,7},{10,8},{11,9},{12,... | collective-permute-start | bytes 589832 | tf_op jit(solution)/shard_map/ppermute | solution.py:93
  79.2 10.1 %collective-permute-start.3 = (bf16[192,512]{1,0:T(8,128)(2,1)S(1)}, bf16[192,512]{1,0:T(8,128)(2,1)S(1)}, u32[]{:S(2)}, u32[]{:S(2)}) collective-permute-start(bf16[192,512]{1,0:T(8,128)(2,1)S(1)} %slice.236), channel_id=1, source_target_pairs={{14,0},{15,1},{0,2},{1,3},{2,4},{3,5},{4,6},{5,7},{6,8},{7,9},{8,1... | collective-permute-start | bytes 589832 | tf_op jit(solution)/shard_map/ppermute | solution.py:93
  89.6 16.6 %collective-permute-start.4 = (bf16[4,384,512]{2,1,0:T(8,128)(2,1)S(1)}, bf16[4,384,512]{2,1,0:T(8,128)(2,1)}, u32[]{:S(2)}, u32[]{:S(2)}) collective-permute-start(bf16[4,384,512]{2,1,0:T(8,128)(2,1)S(1)} %pad_maximum_fusion.mine), channel_id=1, source_target_pairs={{0,1},{1,0},{2,3},{3,2},{4,5},{5,4},{6,7},{7,6},{8,9},{9,8},{10,11... | collective-permute-start | bytes 4718600 | tf_op jit(solution)/shard_map/ppermute | solution.py:99
  102.8 0.7 copy-start.9
  106.2 2.2 %copy-start.1 = (bf16[4096,512]{1,0:T(8,128)(2,1)S(1)}, bf16[4096,512]{1,0:T(8,128)(2,1)}, u32[]{:S(2)}) copy-start(bf16[4096,512]{1,0:T(8,128)(2,1)} %all-gather.2.cloned.1.call-done.weight) | copy-start | bytes 12582916
  113.9 1.9 copy-start.3
  114.0 1.4 copy-start.7
  119.8 5.5 %copy-start.11 = (f32[1,4096]{1,0:T(1,128)S(1)}, f32[1,4096]{1,0:T(1,128)}, u32[]{:S(2)}) copy-start(f32[1,4096]{1,0:T(1,128)} %param.15) | copy-start | bytes 49156
  119.8 30.8 %copy-start.4 = (bf16[384,4096]{1,0:T(8,128)(2,1)S(1)}, bf16[384,4096]{1,0:T(8,128)(2,1)}, u32[]{:S(2)}) copy-start(bf16[384,4096]{1,0:T(8,128)(2,1)} %copy-done.3) | copy-start | bytes 9437188
  121.1 26.9 %all-to-all-start.2 = ((bf16[16,192,128]{2,1,0:T(8,128)(2,1)}), bf16[16,192,128]{2,1,0:T(8,128)(2,1)}, u32[]{:S(2)}, u32[]{:S(2)}) async-start(bf16[16,192,128]{2,1,0:T(8,128)(2,1)} %pad_maximum_fusion.1), calls=%async_computation.2 | async-start | bytes 1572864 | tf_op jit(solution)/shard_map/all_to_all | solution.py:59
  150.6 2.2 %copy-start.2 = (bf16[4096,512]{1,0:T(8,128)(2,1)S(1)}, bf16[4096,512]{1,0:T(8,128)(2,1)}, u32[]{:S(2)}) copy-start(bf16[4096,512]{1,0:T(8,128)(2,1)} %all-gather.2.cloned.1.call-done.weight) | copy-start | bytes 12582916
  151.7 2.0 %copy-start.6 = (bf16[384,1024]{1,0:T(8,128)(2,1)S(1)}, bf16[384,1024]{1,0:T(8,128)(2,1)}, u32[]{:S(2)}) copy-start(bf16[384,1024]{1,0:T(8,128)(2,1)} %copy-done.5) | copy-start | bytes 2359300
  157.0 23.1 %copy-start.14 = (s32[128]{0:T(128)S(1)}, s32[128]{0:T(128)}, u32[]{:S(2)}) copy-start(s32[128]{0:T(128)} %copy-done.13) | copy-start | bytes 1540
  158.9 21.2 %all-to-all-start.3 = ((bf16[32,12,512]{2,1,0:T(8,128)(2,1)}), bf16[32,12,512]{2,1,0:T(8,128)(2,1)S(1)}, u32[]{:S(2)}, u32[]{:S(2)}) async-start(bf16[32,12,512]{2,1,0:T(8,128)(2,1)} %reshape.236), calls=%async_computation.3 | async-start | bytes 1048576 | tf_op jit(solution)/shard_map/all_to_all | solution.py:59
Sparse Core Ops, SparseCore 0:
  20.2 80.7 all-gather.1

commit v4 on v3

--- a/solution.py
+++ b/solution.py
@@ -27,18 +27,15 @@
     return jnp.sum(inside * shift[:, None], axis=0) + ids[0]
 
 
-def align_kernel(place, rows_in, rows_low, weight, second, mine, other, joined, align, moment):
+def align_kernel(place, rows_in, rows_low, weight, second, mine, other, joined, align):
     z_cols = mine.shape[2]
     near = place[1] * z_cols
     for start, part in ((near, mine), (z_cols - near, other)):
         cols = pl.ds(pl.multiple_of(start, z_cols), z_cols)
         joined[:, cols] = part[0]
-        products = dot(rows_low[...], part[0], ((0,), (0,)))
-        moment[:, cols] = products
         projected = dot(rows_in[...], weight[cols, :], ((1,), (1,)))
-        sums = jnp.sum(part[0].astype(F32) * projected, axis=0, keepdims=True)
-        sums += jnp.sum(products * second[:, cols], axis=0, keepdims=True)
-        align[:, cols] = sums
+        projected += jnp.dot(rows_low[...], second[:, cols], preferred_element_type=F32)
+        align[:, cols] = jnp.sum(part[0].astype(F32) * projected, axis=0, keepdims=True)
 
 
 def on_device(acts, grads, counts, owner_slot, base_weight, adapter_a, adapter_b, magnitude):
@@ -94,14 +91,14 @@
 
     n_parts, half = nz // 2, packed // 2
     above, below = along_y(rows_grad_t, 1), along_y(rows_grad_t, -1)
-    far = jnp.concatenate([along_y(above[:half], 1), along_y(below[half:], -1)], axis=0)
+    far = jnp.concatenate([along_y(rows_grad_t[:half], 2), along_y(rows_grad_t[half:], -2)], axis=0)
     mine = jnp.stack([rows_grad_t, above, far, below])
     other = lax.ppermute(mine, "tp", [(i, i ^ 1) for i in range(shards)])
 
     first, second = adapter_a[0], arriving(adapter_b[0])
     first_t = first.T
     second_wide = second.astype(F32)
-    gain = arriving(magnitude)
+    gain = magnitude.reshape(NX, nz, g_cols).transpose(1, 0, 2).reshape(-1, g_cols)
     gram = dot(first, first, ((0,), (0,)))
     gram_second = dot(gram, second_wide, ((1,), (0,)), lax.Precision.HIGHEST)
     rows_low = dot(rows_in, first, ((1,), (0,))).astype(BF)
@@ -122,6 +119,8 @@
     def to_all(values):
         return jnp.broadcast_to(values[None], (shards,) + values.shape)
 
+    low_t = dot(first_t, rows_in, ((1,), (1,))).astype(BF)
+    low_t = unlanes(summed(to_all(lanes(low_t))), rank).astype(BF)
     first_weight = dot(first_t, weight, ((1,), (1,)))
     square_base = jnp.sum(jnp.square(weight.astype(F32)), axis=1)
     squares = square_base[None, :] + jnp.sum(
@@ -137,7 +136,7 @@
         return lax.rem(place[0] + k, n_parts)
 
     block = pl.BlockSpec((1, packed, z_cols), lambda k, place: (k, 0, 0))
-    rows_grad, align, first_moment = pl.pallas_call(
+    rows_grad, align = pl.pallas_call(
         align_kernel,
         grid_spec=pltpu.PrefetchScalarGridSpec(
             num_scalar_prefetch=1,
@@ -153,13 +152,11 @@
             out_specs=[
                 pl.BlockSpec((packed, wide), lambda k, place: (0, chip(k, place))),
                 pl.BlockSpec((1, wide), lambda k, place: (0, chip(k, place))),
-                pl.BlockSpec((rank, wide), lambda k, place: (0, chip(k, place))),
             ],
         ),
         out_shape=[
             jax.ShapeDtypeStruct((packed, out_width), BF),
             jax.ShapeDtypeStruct((1, out_width), F32),
-            jax.ShapeDtypeStruct((rank, out_width), F32),
         ],
         compiler_params=pltpu.CompilerParams(vmem_limit_bytes=32 * 2**20),
         cost_estimate=pl.CostEstimate(
@@ -168,9 +165,9 @@
             transcendentals=0,
         ),
         name="align_columns",
-    )(jnp.stack([my_part, my_core]).astype(jnp.int32), rows_in, rows_low, weight, second_wide, mine, other)
-
-    products = natural(jnp.concatenate([first_moment, first_weight + gram_second], axis=0))
+    )(jnp.stack([my_part, my_core]).astype(jnp.int32), rows_in, rows_low, weight, second, mine, other)
+
+    products = natural(first_weight + gram_second)
     products = products.astype(BF)
     pieces = jnp.stack(
         [lanes(products[:, i : i + t_cols]) for i in range(0, out_width, t_cols)], axis=0
@@ -178,30 +175,43 @@
     terms = jnp.concatenate([squares.reshape(-1, 128), align.reshape(-1, 128)], axis=0)
     n_terms = terms.shape[0]
     terms = summed(jnp.concatenate([to_all(terms.astype(BF)), pieces], axis=1))
-    products = unlanes(terms[n_terms:], 2 * rank)
-    moment_t, merged_t = products[:rank], products[rank:]
-    terms = terms[:n_terms].reshape(2, out_width)
-    norm = jnp.sqrt(terms[:1] + EPSILON)
-    align = terms[1:]
+    merged_t = unlanes(terms[n_terms:], rank)
+    squares, align = terms[: n_terms // 2], terms[n_terms // 2 : n_terms]
+    norm = jnp.sqrt(squares + EPSILON)
     scale = gain / norm
-    grad_gain = natural(align / norm)
     shrink = gain * align / (norm * norm * norm)
 
-    hidden = (rows_grad.astype(F32) * scale).astype(BF)
+    def in_order(values):
+        values = values.reshape(nz, NX, g_cols).transpose(1, 0, 2)
+        return values.reshape(groups, g_cols)
+
+    grad_gain = in_order(align / norm).reshape(1, out_width)
+
+    def along_tp(values):
+        strips = t_cols // g_cols
+        values = lax.dynamic_slice(in_order(values), (my_t * strips, 0), (strips, g_cols))
+        return values.reshape(1, t_cols)
+
+    hidden = (rows_grad.astype(F32) * scale.reshape(1, out_width)).astype(BF)
     inner = dot(hidden, second, ((1,), (1,))).astype(BF)
     back = dot(hidden, weight, ((1,), (0,))) + dot(inner, first, ((1,), (1,)))
-    row_grad = dot(place, to_owners(back.astype(BF)), ((0,), (0,))).astype(BF)
-
-    shrunk = (second_wide * shrink).astype(BF)
+    back, inner = lax.optimization_barrier((back.astype(BF), inner))
+    row_grad = dot(place, to_owners(back), ((0,), (0,))).astype(BF)
+
+    shrunk = (second_wide * shrink.reshape(1, out_width)).astype(BF)
     small = dot(second, shrunk, ((1,), (1,)))
     grad_a = (
         dot(inner, rows_in, ((0,), (0,)))
         - dot(shrunk, weight, ((1,), (0,)))
         - dot(small.astype(BF), first_t, ((0,), (0,)))
     )
-    scale_t = lax.dynamic_slice(natural(scale), (0, my_t * t_cols), (1, t_cols))
-    shrink_t = lax.dynamic_slice(natural(shrink), (0, my_t * t_cols), (1, t_cols))
-    grad_b = moment_t * scale_t - merged_t * shrink_t
+    strips = []
+    for i in range(t_cols // g_cols):
+        block = my_t * (t_cols // g_cols) + i
+        start = (block % nz * NX + block // nz) * g_cols
+        strips.append(lax.dynamic_slice(rows_grad, (0, start), (packed, g_cols)))
+    moment_t = dot(low_t, jnp.concatenate(strips, axis=1), ((1,), (0,)))
+    grad_b = moment_t * along_tp(scale) - merged_t * along_tp(shrink)
     return row_grad, grad_a.T[None], grad_b[None], grad_gain
 
 

time: 189 us -> 186 us (0.984)
  blocking collectives: 52.4 us -> 11.7 us
  starting transfers between devices: 37.6 us -> 58.5 us
  waiting for transfers between devices: 43.3 us -> 61.1 us
  other arithmetic: 11.3 us -> 4.85 us
  matrix products: 11.2 us -> 15.5 us
    all_to_all x2 -> x1, blocking collectives: 52.4 us -> 11.7 us  [exchange(): lax.all_to_all(values, axis, split_axis=0, concat_axis=0, tiled=True, axi...]
    all_to_all x2 -> x4, starting transfers between devices: 9.49 us -> 32.6 us  [exchange(): lax.all_to_all(values, axis, split_axis=0, concat_axis=0, tiled=True, axi...]
    all_to_all x2 -> x4, waiting for transfers between devices: 32.2 us -> 52.5 us  [exchange(): lax.all_to_all(values, axis, split_axis=0, concat_axis=0, tiled=True, axi...]
    dot_general x12 -> x13, matrix products: 11.2 us -> 15.5 us  [dot(): lax.dot_general(left, right, (dims, ((), ())), precision=precision, prefe...]
    ppermute x4, waiting for transfers between devices: 11 us -> 8.56 us  [along_y(): return lax.ppermute(values, 'tp', pairs)]
    div x3 -> x1, other arithmetic: 2.24 us -> 0.02 us  [on_device(): grad_gain = in_order(align / norm).reshape(1, out_width)]
    reduce_sum x1, other arithmetic: 3.08 us -> 0.9 us  [on_device(): square_base = jnp.sum(jnp.square(weight.astype(F32)), axis=1)]
    ppermute x1, starting transfers between devices: 13.1 us -> 11 us  [on_device(): other = lax.ppermute(mine, 'tp', [(i, i ^ 1) for i in range(shards)])]
  transfers between devices with their start and end apart: 8 -> 10, of which waited for: 5 -> 5; matrix products, arithmetic and copies ran while one was open for 6% -> 11% of each run, Pallas kernels for 0% -> 3%
where the time goes in v4:
time: 186 us; the launch traced here: 185 us
  waiting for transfers between devices  61.1 us (33%)
  starting transfers between devices  58.5 us (31%)
  matrix products  15.5 us (8%)
  between operations  14.7 us (8%)
  local copies, waits for them, and re-layouts  13.6 us (7%)
  blocking collectives  11.7 us (6%)
  Pallas kernels  5.35 us (3%)
  other arithmetic  4.85 us (3%)
    all_to_all x4, waiting for transfers between devices, exchange(): lax.all_to_all(values, axis, split_axis=0, concat_axis=0, tiled=True, axi...  52.5 us
    all_to_all x4, starting transfers between devices, exchange(): lax.all_to_all(values, axis, split_axis=0, concat_axis=0, tiled=True, axi...  32.6 us
    dot_general x13, matrix products, dot(): lax.dot_general(left, right, (dims, ((), ())), precision=precision, prefe...  15.5 us
    ppermute x4, starting transfers between devices, along_y(): return lax.ppermute(values, 'tp', pairs)  14.9 us
    all_to_all x1, blocking collectives, exchange(): lax.all_to_all(values, axis, split_axis=0, concat_axis=0, tiled=True, axi...  11.7 us
    ppermute x1, starting transfers between devices, on_device(): other = lax.ppermute(mine, 'tp', [(i, i ^ 1) for i in range(shards)])  11 us
    ppermute x4, waiting for transfers between devices, along_y(): return lax.ppermute(values, 'tp', pairs)  8.56 us
    unnamed x38, local copies, waits for them, and re-layouts  5.44 us
  transfers between devices with their start and end apart: 10, of which 5 were waited for; matrix products, arithmetic and copies ran while one was open for 11% of the time, Pallas kernels for 3%

profile of v4, /device:TPU:1, one launch (start us, length us, event | category | flops | bytes accessed | tf_op | source)
XLA Modules:
  0.0 185.2 jit_solution(13510341036013816474)
XLA Ops:
  7.2 0.0 all-gather.2.cloned.1.call-start
  7.3 1.1 copy.46
  8.4 11.7 %all_to_all.25 = bf16[4,128,512]{2,1,0:T(8,128)(2,1)} all-to-all(bf16[4,128,512]{2,1,0:T(8,128)(2,1)S(1)} %broadcast_in_dim.10), channel_id=1, replica_groups={{0,128,256,384},{16,144,272,400},{32,160,288,416},{48,176,304,432},{64,..., dimensions={0} | all-to-all | bytes 1048576 | tf_op jit(solution)/shard_map/all_to_all | solution.py:56
  20.1 0.0 all-gather.2.cloned.1.call-update
  20.1 0.7 copy.44
  20.8 0.1 copy.45
  21.0 0.1 copy.43
  21.1 0.1 reduce.1
  21.3 0.1 select_reduce_fusion
  21.4 0.4 convolution_convert_fusion
  21.8 1.1 reshape.138
  22.9 12.7 %all-to-all-start.1 = ((bf16[32,12,1024]{2,1,0:T(8,128)(2,1)}), bf16[32,12,1024]{2,1,0:T(8,128)(2,1)S(1)}, u32[]{:S(2)}, u32[]{:S(2)}) async-start(bf16[32,12,1024]{2,1,0:T(8,128)(2,1)} %reshape.138), calls=%async_computation.1 | async-start | bytes 2097152 | tf_op jit(solution)/shard_map/all_to_all | solution.py:56
  35.7 0.7 copy-done.8
  36.4 0.1 copy.49
  36.5 0.2 reshape.141.second
  36.7 0.1 pad_add_fusion.place
  36.8 27.6 %all-to-all-done.1 = bf16[32,12,1024]{2,1,0:T(8,128)(2,1)S(1)} async-done(((bf16[32,12,1024]{2,1,0:T(8,128)(2,1)}), bf16[32,12,1024]{2,1,0:T(8,128)(2,1)S(1)}, u32[]{:S(2)}, u32[]{:S(2)}) %all-to-all-start.1) | async-done | bytes 786464 | tf_op jit(solution)/shard_map/all_to_all | solution.py:56
  64.3 0.2 reshape.139
  64.5 0.1 slice_bitcast_fusion
  64.6 3.3 %collective-permute-start.3 = (bf16[384,512]{1,0:T(8,128)(2,1)S(1)}, bf16[384,512]{1,0:T(8,128)(2,1)S(1)}, u32[]{:S(2)}, u32[]{:S(2)}) collective-permute-start(bf16[384,512]{1,0:T(8,128)(2,1)S(1)} %get-tuple-element.21), channel_id=1, source_target_pairs={{14,0},{15,1},{0,2},{1,3},{2,4},{3,5},{4,6},{5,7},{6,8},{7,9},{8,1... | collective-permute-start | bytes 1179656 | tf_op jit(solution)/shard_map/ppermute | solution.py:90
  67.9 4.2 %collective-permute-start = (bf16[384,512]{1,0:T(8,128)(2,1)S(1)}, bf16[384,512]{1,0:T(8,128)(2,1)S(1)}, u32[]{:S(2)}, u32[]{:S(2)}) collective-permute-start(bf16[384,512]{1,0:T(8,128)(2,1)S(1)} %get-tuple-element.21), channel_id=1, source_target_pairs={{2,0},{3,1},{4,2},{5,3},{6,4},{7,5},{8,6},{9,7},{10,8},{11,9},{12,... | collective-permute-start | bytes 1179656 | tf_op jit(solution)/shard_map/ppermute | solution.py:90
  72.1 2.1 %collective-permute-start.2 = (bf16[192,512]{1,0:T(8,128)(2,1)S(1)}, bf16[192,512]{1,0:T(8,128)(2,1)S(1)}, u32[]{:S(2)}, u32[]{:S(2)}) collective-permute-start(bf16[192,512]{1,0:T(8,128)(2,1)S(1)} %get-tuple-element.24), channel_id=1, source_target_pairs={{12,0},{13,1},{14,2},{15,3},{0,4},{1,5},{2,6},{3,7},{4,8},{5,9},{6... | collective-permute-start | bytes 589832 | tf_op jit(solution)/shard_map/ppermute | solution.py:90
  74.3 5.3 %collective-permute-start.1 = (bf16[192,512]{1,0:T(8,128)(2,1)S(1)}, bf16[192,512]{1,0:T(8,128)(2,1)S(1)}, u32[]{:S(2)}, u32[]{:S(2)}) collective-permute-start(bf16[192,512]{1,0:T(8,128)(2,1)S(1)} %get-tuple-element.23), channel_id=1, source_target_pairs={{4,0},{5,1},{6,2},{7,3},{8,4},{9,5},{10,6},{11,7},{12,8},{13,9},{1... | collective-permute-start | bytes 589832 | tf_op jit(solution)/shard_map/ppermute | solution.py:90
  79.6 0.1 fusion.31
  79.7 3.3 %collective-permute-done.2 = bf16[192,512]{1,0:T(8,128)(2,1)S(1)} collective-permute-done((bf16[192,512]{1,0:T(8,128)(2,1)S(1)}, bf16[192,512]{1,0:T(8,128)(2,1)S(1)}, u32[]{:S(2)}, u32[]{:S(2)}) %collective-permute-start.2) | collective-permute-done | bytes 196640 | tf_op jit(solution)/shard_map/ppermute | solution.py:90
  83.0 5.3 %collective-permute-done.1 = bf16[192,512]{1,0:T(8,128)(2,1)S(1)} collective-permute-done((bf16[192,512]{1,0:T(8,128)(2,1)S(1)}, bf16[192,512]{1,0:T(8,128)(2,1)S(1)}, u32[]{:S(2)}, u32[]{:S(2)}) %collective-permute-start.1) | collective-permute-done | bytes 196640 | tf_op jit(solution)/shard_map/ppermute | solution.py:90
  88.3 0.2 pad_maximum_fusion.mine
  88.5 11.0 %collective-permute-start.4 = (bf16[4,384,512]{2,1,0:T(8,128)(2,1)S(1)}, bf16[4,384,512]{2,1,0:T(8,128)(2,1)}, u32[]{:S(2)}, u32[]{:S(2)}) collective-permute-start(bf16[4,384,512]{2,1,0:T(8,128)(2,1)S(1)} %pad_maximum_fusion.mine), channel_id=1, source_target_pairs={{0,1},{1,0},{2,3},{3,2},{4,5},{5,4},{6,7},{7,6},{8,9},{9,8},{10,11... | collective-permute-start | bytes 4718600 | tf_op jit(solution)/shard_map/ppermute | solution.py:96
  99.5 0.2 convolution_convert_fusion.2.rows_low
  99.8 0.1 pad_maximum_fusion.2
  99.9 0.1 copy.52
  100.0 0.9 broadcast_in_dim.13
  100.8 4.9 %all-to-all-start.4 = ((bf16[16,96,128]{2,1,0:T(8,128)(2,1)}), bf16[16,96,128]{2,1,0:T(8,128)(2,1)}, u32[]{:S(2)}, u32[]{:S(2)}) async-start(bf16[16,96,128]{2,1,0:T(8,128)(2,1)} %broadcast_in_dim.13), calls=%async_computation.4 | async-start | bytes 786432 | tf_op jit(solution)/shard_map/all_to_all | solution.py:56
  105.8 3.5 %fusion.33 = f32[32,4096]{1,0:T(8,128)S(1)} fusion(bf16[4096,512]{1,0:T(8,128)(2,1)} %all-gather.2.cloned.1.call-done.weight, bf16[1,512,32]{1,2,0:T(8,128)(2,1)S(1)} %copy-done), kind=kOutput, calls=%fused_computation.67 | convolution fusion | flops 134217728 | bytes 4751360 | tf_op jit(solution)/shard_map/dot_general | solution.py:16
  109.3 0.5 fusion.10
  109.7 0.2 convert_element_type.76
  110.0 0.1 copy.71
  110.2 2.2 %copy-done.1 = bf16[4096,512]{1,0:T(8,128)(2,1)S(1)} copy-done((bf16[4096,512]{1,0:T(8,128)(2,1)S(1)}, bf16[4096,512]{1,0:T(8,128)(2,1)}, u32[]{:S(2)}) %copy-start.1) | copy-done | bytes 4194328
  112.3 5.3 %align_columns.1 = (bf16[384,4096]{1,0:T(8,128)(2,1)S(1)}, f32[1,4096]{1,0:T(1,128)S(1)}) custom-call(s32[2]{0:T(128)S(1)} %pad_add_fusion.place, bf16[384,512]{1,0:T(8,128)(2,1)S(1)} %get-tuple-element.22.rows_in, bf16[384,32]{1,0:T(8,128)(2,1)S(1)} %convolution_convert_fusion.2.rows_low, bf16[4096,512]{1,0:T(8,128)(2,1)S(1)} %copy-done.1, ...), custom_call_target="tpu_custom_call" | custom-call | flops 1610612736 | bytes 10485760 | tf_op jit(solution)/shard_map/align_columns/pallas_call | solution.py:139
  117.7 0.1 convert_reduce_fusion.1
  117.8 0.9 multiply_reduce_fusion
  118.7 0.7 copy-done.3
  119.7 0.9 pad_maximum_fusion.1
  120.5 7.2 %all-to-all-start.2 = ((bf16[16,128,128]{2,1,0:T(8,128)(2,1)}), bf16[16,128,128]{2,1,0:T(8,128)(2,1)}, u32[]{:S(2)}, u32[]{:S(2)}) async-start(bf16[16,128,128]{2,1,0:T(8,128)(2,1)} %pad_maximum_fusion.1), calls=%async_computation.2 | async-start | bytes 1048576 | tf_op jit(solution)/shard_map/all_to_all | solution.py:56
  127.8 1.1 reduce
  128.9 0.6 fusion.56
  129.5 0.7 constant_dynamic-slice_fusion.3
  130.2 15.0 %all-to-all-done.2 = bf16[16,128,128]{2,1,0:T(8,128)(2,1)} async-done(((bf16[16,128,128]{2,1,0:T(8,128)(2,1)}), bf16[16,128,128]{2,1,0:T(8,128)(2,1)}, u32[]{:S(2)}, u32[]{:S(2)}) %all-to-all-start.2) | async-done | bytes 524320 | tf_op jit(solution)/shard_map/all_to_all | solution.py:56
  145.2 1.1 convert_reduce_fusion
  146.4 1.0 fusion.6
  147.4 0.3 fusion.29
  147.7 0.8 copy-done.2
  148.5 2.6 %fusion.3 = bf16[384,512]{1,0:T(8,128)(2,1)} fusion(f32[384,512]{1,0:T(8,128)S(1)} %fusion.29, bf16[4096,512]{1,0:T(8,128)(2,1)S(1)} %copy-done.2, bf16[384,4096]{1,0:T(8,128)(2,1)S(1)} %copy-done.4, f32[4096]{0:T(1024)S(1)} %bitcast.187), kind=kOutput, calls=%fused_computation.7 | convolution fusion | flops 1615724544 | bytes 8536064 | tf_op jit(solution)/shard_map/dot_general | solution.py:16
  151.1 1.9 %reshape.144 = bf16[32,12,512]{2,1,0:T(8,128)(2,1)} reshape(bf16[384,512]{1,0:T(8,128)(2,1)} %fusion.3) | data formatting | bytes 786432 | tf_op jit(solution)/shard_map/reshape | solution.py:61
  153.0 7.8 %all-to-all-start.3 = ((bf16[32,12,512]{2,1,0:T(8,128)(2,1)}), bf16[32,12,512]{2,1,0:T(8,128)(2,1)S(1)}, u32[]{:S(2)}, u32[]{:S(2)}) async-start(bf16[32,12,512]{2,1,0:T(8,128)(2,1)} %reshape.144), calls=%async_computation.3 | async-start | bytes 1048576 | tf_op jit(solution)/shard_map/all_to_all | solution.py:56
  160.9 1.8 fusion.8
  162.6 0.6 copy.55
  163.2 3.0 %convolution_bitcast_fusion.1 = f32[512,32]{0,1:T(8,128)S(1)} fusion(bf16[4096,512]{1,0:T(8,128)(2,1)} %all-gather.2.cloned.1.call-done.weight, bf16[32,4096]{1,0:T(8,128)(2,1)S(1)} %reshape.141.second, f32[4096]{0:T(1024)S(1)} %bitcast.181), kind=kOutput, calls=%fused_computation.14 | convolution fusion | flops 134610944 | bytes 4538368 | tf_op jit(solution)/shard_map/dot_general | solution.py:16
  166.2 0.2 convolution_subtract_fusion
  166.4 0.0 copy-done.9
  166.4 1.1 fusion.5
  167.5 9.9 %all-to-all-done.3 = bf16[32,12,512]{2,1,0:T(8,128)(2,1)S(1)} async-done(((bf16[32,12,512]{2,1,0:T(8,128)(2,1)}), bf16[32,12,512]{2,1,0:T(8,128)(2,1)S(1)}, u32[]{:S(2)}, u32[]{:S(2)}) %all-to-all-start.3) | async-done | bytes 393248 | tf_op jit(solution)/shard_map/all_to_all | solution.py:56
  177.4 0.1 reshape.145
  177.5 0.9 convolution_convert_fusion.1
  (70 shorter events, 0.7 us)
Async XLA Ops:
  7.2 72.4 %copy-start = (bf16[1,512,32]{1,2,0:T(8,128)(2,1)S(1)}, bf16[1,512,32]{1,2,0:T(8,128)(2,1)}, u32[]{:S(2)}) copy-start(bf16[1,512,32]{1,2,0:T(8,128)(2,1)} %param.13) | copy-start | bytes 98308
  7.2 12.9 %copy-start.7 = (bf16[128,4096]{1,0:T(8,128)(2,1)S(1)}, bf16[128,4096]{1,0:T(8,128)(2,1)}, u32[]{:S(2)}) copy-start(bf16[128,4096]{1,0:T(8,128)(2,1)} %param.9) | copy-start | bytes 3145732
  7.2 13.6 %copy-start.11 = (bf16[128,512]{1,0:T(8,128)(2,1)S(1)}, bf16[128,512]{1,0:T(8,128)(2,1)}, u32[]{:S(2)}) copy-start(bf16[128,512]{1,0:T(8,128)(2,1)} %param.8) | copy-start | bytes 393220
  7.2 13.8 %copy-start.15 = (s32[1,24]{1,0:T(1,128)S(1)}, s32[1,24]{1,0:T(1,128)}, u32[]{:S(2)}) copy-start(s32[1,24]{1,0:T(1,128)} %param.10) | copy-start | bytes 292
  7.2 14.0 %copy-start.16 = (s32[24]{0:T(128)S(1)}, s32[24]{0:T(128)}, u32[]{:S(2)}) copy-start(s32[24]{0:T(128)} %param.11) | copy-start | bytes 292
  7.2 98.5 %all-gather.2.cloned.1.call-start = ((), (), s32[]{:S(2)}) async-start(), calls=%async_computation.5 | async-start | bytes 4718592 | tf_op jit(solution)/shard_map/all_gather | solution.py:74
  20.8 14.8 %copy-start.10 = (bf16[1,32,4096]{2,1,0:T(8,128)(2,1)S(1)}, bf16[1,32,4096]{2,1,0:T(8,128)(2,1)}, u32[]{:S(2)}) copy-start(bf16[1,32,4096]{2,1,0:T(8,128)(2,1)} %param.14) | copy-start | bytes 786436
  21.4 1.5 copy-start.13
  22.9 41.4 %all-to-all-start.1 = ((bf16[32,12,1024]{2,1,0:T(8,128)(2,1)}), bf16[32,12,1024]{2,1,0:T(8,128)(2,1)S(1)}, u32[]{:S(2)}, u32[]{:S(2)}) async-start(bf16[32,12,1024]{2,1,0:T(8,128)(2,1)} %reshape.138), calls=%async_computation.1 | async-start | bytes 2097152 | tf_op jit(solution)/shard_map/all_to_all | solution.py:56
  35.7 0.7 copy-start.8
  64.5 35.0 %copy-start.5 = (bf16[384,1024]{1,0:T(8,128)(2,1)}, bf16[384,1024]{1,0:T(8,128)(2,1)S(1)}, u32[]{:S(2)}) copy-start(bf16[384,1024]{1,0:T(8,128)(2,1)S(1)} %reshape.139) | copy-start | bytes 2359300
  64.6 23.7 %collective-permute-start.3 = (bf16[384,512]{1,0:T(8,128)(2,1)S(1)}, bf16[384,512]{1,0:T(8,128)(2,1)S(1)}, u32[]{:S(2)}, u32[]{:S(2)}) collective-permute-start(bf16[384,512]{1,0:T(8,128)(2,1)S(1)} %get-tuple-element.21), channel_id=1, source_target_pairs={{14,0},{15,1},{0,2},{1,3},{2,4},{3,5},{4,6},{5,7},{6,8},{7,9},{8,1... | collective-permute-start | bytes 1179656 | tf_op jit(solution)/shard_map/ppermute | solution.py:90
  67.9 20.4 %collective-permute-start = (bf16[384,512]{1,0:T(8,128)(2,1)S(1)}, bf16[384,512]{1,0:T(8,128)(2,1)S(1)}, u32[]{:S(2)}, u32[]{:S(2)}) collective-permute-start(bf16[384,512]{1,0:T(8,128)(2,1)S(1)} %get-tuple-element.21), channel_id=1, source_target_pairs={{2,0},{3,1},{4,2},{5,3},{6,4},{7,5},{8,6},{9,7},{10,8},{11,9},{12,... | collective-permute-start | bytes 1179656 | tf_op jit(solution)/shard_map/ppermute | solution.py:90
  72.1 10.8 %collective-permute-start.2 = (bf16[192,512]{1,0:T(8,128)(2,1)S(1)}, bf16[192,512]{1,0:T(8,128)(2,1)S(1)}, u32[]{:S(2)}, u32[]{:S(2)}) collective-permute-start(bf16[192,512]{1,0:T(8,128)(2,1)S(1)} %get-tuple-element.24), channel_id=1, source_target_pairs={{12,0},{13,1},{14,2},{15,3},{0,4},{1,5},{2,6},{3,7},{4,8},{5,9},{6... | collective-permute-start | bytes 589832 | tf_op jit(solution)/shard_map/ppermute | solution.py:90
  74.3 14.0 %collective-permute-start.1 = (bf16[192,512]{1,0:T(8,128)(2,1)S(1)}, bf16[192,512]{1,0:T(8,128)(2,1)S(1)}, u32[]{:S(2)}, u32[]{:S(2)}) collective-permute-start(bf16[192,512]{1,0:T(8,128)(2,1)S(1)} %get-tuple-element.23), channel_id=1, source_target_pairs={{4,0},{5,1},{6,2},{7,3},{8,4},{9,5},{10,6},{11,7},{12,8},{13,9},{1... | collective-permute-start | bytes 589832 | tf_op jit(solution)/shard_map/ppermute | solution.py:90
  88.5 21.6 %collective-permute-start.4 = (bf16[4,384,512]{2,1,0:T(8,128)(2,1)S(1)}, bf16[4,384,512]{2,1,0:T(8,128)(2,1)}, u32[]{:S(2)}, u32[]{:S(2)}) collective-permute-start(bf16[4,384,512]{2,1,0:T(8,128)(2,1)S(1)} %pad_maximum_fusion.mine), channel_id=1, source_target_pairs={{0,1},{1,0},{2,3},{3,2},{4,5},{5,4},{6,7},{7,6},{8,9},{9,8},{10,11... | collective-permute-start | bytes 4718600 | tf_op jit(solution)/shard_map/ppermute | solution.py:96
  100.8 19.7 %all-to-all-start.4 = ((bf16[16,96,128]{2,1,0:T(8,128)(2,1)}), bf16[16,96,128]{2,1,0:T(8,128)(2,1)}, u32[]{:S(2)}, u32[]{:S(2)}) async-start(bf16[16,96,128]{2,1,0:T(8,128)(2,1)} %broadcast_in_dim.13), calls=%async_computation.4 | async-start | bytes 786432 | tf_op jit(solution)/shard_map/all_to_all | solution.py:56
  110.2 2.2 %copy-start.1 = (bf16[4096,512]{1,0:T(8,128)(2,1)S(1)}, bf16[4096,512]{1,0:T(8,128)(2,1)}, u32[]{:S(2)}) copy-start(bf16[4096,512]{1,0:T(8,128)(2,1)} %all-gather.2.cloned.1.call-done.weight) | copy-start | bytes 12582916
  117.7 1.7 copy-start.3
  117.8 10.0 %copy-start.12 = (f32[1,4096]{1,0:T(1,128)S(1)}, f32[1,4096]{1,0:T(1,128)}, u32[]{:S(2)}) copy-start(f32[1,4096]{1,0:T(1,128)} %param.15) | copy-start | bytes 49156
  119.4 10.1 %copy-start.4 = (bf16[384,4096]{1,0:T(8,128)(2,1)S(1)}, bf16[384,4096]{1,0:T(8,128)(2,1)}, u32[]{:S(2)}) copy-start(bf16[384,4096]{1,0:T(8,128)(2,1)} %copy-done.3) | copy-start | bytes 9437188
  120.5 24.7 %all-to-all-start.2 = ((bf16[16,128,128]{2,1,0:T(8,128)(2,1)}), bf16[16,128,128]{2,1,0:T(8,128)(2,1)}, u32[]{:S(2)}, u32[]{:S(2)}) async-start(bf16[16,128,128]{2,1,0:T(8,128)(2,1)} %pad_maximum_fusion.1), calls=%async_computation.2 | async-start | bytes 1048576 | tf_op jit(solution)/shard_map/all_to_all | solution.py:56
  146.3 2.2 %copy-start.2 = (bf16[4096,512]{1,0:T(8,128)(2,1)S(1)}, bf16[4096,512]{1,0:T(8,128)(2,1)}, u32[]{:S(2)}) copy-start(bf16[4096,512]{1,0:T(8,128)(2,1)} %all-gather.2.cloned.1.call-done.weight) | copy-start | bytes 12582916
  153.0 13.2 %copy-start.6 = (bf16[384,1024]{1,0:T(8,128)(2,1)S(1)}, bf16[384,1024]{1,0:T(8,128)(2,1)}, u32[]{:S(2)}) copy-start(bf16[384,1024]{1,0:T(8,128)(2,1)} %copy-done.5) | copy-start | bytes 2359300
  153.0 13.4 %copy-start.9 = (bf16[4,8,32,128]{3,2,1,0:T(8,128)(2,1)S(1)}, bf16[4,8,32,128]{3,2,1,0:T(8,128)(2,1)}, u32[]{:S(2)}) copy-start(bf16[4,8,32,128]{3,2,1,0:T(8,128)(2,1)} %copy-done.8) | copy-start | bytes 786436
  153.0 24.4 %all-to-all-start.3 = ((bf16[32,12,512]{2,1,0:T(8,128)(2,1)}), bf16[32,12,512]{2,1,0:T(8,128)(2,1)S(1)}, u32[]{:S(2)}, u32[]{:S(2)}) async-start(bf16[32,12,512]{2,1,0:T(8,128)(2,1)} %reshape.144), calls=%async_computation.3 | async-start | bytes 1048576 | tf_op jit(solution)/shard_map/all_to_all | solution.py:56
  163.2 14.2 %copy-start.14 = (s32[128]{0:T(128)S(1)}, s32[128]{0:T(128)}, u32[]{:S(2)}) copy-start(s32[128]{0:T(128)} %copy-done.13) | copy-start | bytes 1540
Sparse Core Ops, SparseCore 0:
  20.2 81.4 all-gather.1

commit v5 on v4

--- a/solution.py
+++ b/solution.py
@@ -27,15 +27,38 @@
     return jnp.sum(inside * shift[:, None], axis=0) + ids[0]
 
 
-def align_kernel(place, rows_in, rows_low, weight, second, mine, other, joined, align):
-    z_cols = mine.shape[2]
+def columns_kernel(
+    place, left, rows_low, weight, narrow, gram_second, mine, other, joined, terms, pieces
+):
+    packed, z_cols = mine.shape[1:]
+    n_x, rank, g_cols = pieces.shape[0], rows_low.shape[1], pieces.shape[3]
     near = place[1] * z_cols
+    ones = jnp.ones((8, weight.shape[1]), BF)
     for start, part in ((near, mine), (z_cols - near, other)):
         cols = pl.ds(pl.multiple_of(start, z_cols), z_cols)
-        joined[:, cols] = part[0]
-        projected = dot(rows_in[...], weight[cols, :], ((1,), (1,)))
-        projected += jnp.dot(rows_low[...], second[:, cols], preferred_element_type=F32)
-        align[:, cols] = jnp.sum(part[0].astype(F32) * projected, axis=0, keepdims=True)
+        grads = part[0]
+        joined[:, cols] = grads
+        values = weight[cols, :]
+        products = dot(left[...], values, ((1,), (1,)))
+        first_weight = products[packed:]
+        projected = products[:packed] + jnp.dot(
+            rows_low[...], narrow[:, cols], preferred_element_type=F32
+        )
+        wide = values.astype(F32)
+        wide = wide * wide
+        upper = wide.astype(BF)
+        lower = (wide - upper.astype(F32)).astype(BF)
+        base = (dot(ones, upper, ((1,), (1,))) + dot(ones, lower, ((1,), (1,))))[:1]
+        factor, extra = narrow[:, cols].astype(F32), gram_second[:, cols]
+        terms[0:1, cols] = base + jnp.sum(
+            factor * (2.0 * first_weight + extra), axis=0, keepdims=True
+        )
+        terms[1:2, cols] = jnp.sum(grads.astype(F32) * projected, axis=0, keepdims=True)
+        merged = (first_weight + extra).astype(BF)
+        strip = pl.multiple_of(start // z_cols * rank, rank)
+        for i in range(n_x):
+            strips = slice(i * g_cols, (i + 1) * g_cols)
+            pieces[i, 0, pl.ds(strip, rank), :] = merged[:, strips]
 
 
 def on_device(acts, grads, counts, owner_slot, base_weight, adapter_a, adapter_b, magnitude):
@@ -93,8 +116,6 @@
     above, below = along_y(rows_grad_t, 1), along_y(rows_grad_t, -1)
     far = jnp.concatenate([along_y(rows_grad_t[:half], 2), along_y(rows_grad_t[half:], -2)], axis=0)
     mine = jnp.stack([rows_grad_t, above, far, below])
-    other = lax.ppermute(mine, "tp", [(i, i ^ 1) for i in range(shards)])
-
     first, second = adapter_a[0], arriving(adapter_b[0])
     first_t = first.T
     second_wide = second.astype(F32)
@@ -103,6 +124,12 @@
     gram_second = dot(gram, second_wide, ((1,), (0,)), lax.Precision.HIGHEST)
     rows_low = dot(rows_in, first, ((1,), (0,))).astype(BF)
 
+    left = jnp.concatenate([rows_in, first_t], axis=0)
+    mine, left, rows_low, gram_second = lax.optimization_barrier(
+        (mine, left, rows_low, gram_second)
+    )
+    other = lax.ppermute(mine, "tp", [(i, i ^ 1) for i in range(shards)])
+
     def lanes(values):
         return jnp.concatenate(
             [values[:, i : i + 128] for i in range(0, values.shape[1], 128)], axis=0
@@ -121,62 +148,69 @@
 
     low_t = dot(first_t, rows_in, ((1,), (1,))).astype(BF)
     low_t = unlanes(summed(to_all(lanes(low_t))), rank).astype(BF)
-    first_weight = dot(first_t, weight, ((1,), (1,)))
-    square_base = jnp.sum(jnp.square(weight.astype(F32)), axis=1)
-    squares = square_base[None, :] + jnp.sum(
-        second_wide * (2.0 * first_weight + gram_second), axis=0, keepdims=True
-    )
-
     wide = 2 * z_cols
+
+    def chip(k, place):
+        return lax.rem(place[0] + k, n_parts)
 
     def fixed(*shape):
         return pl.BlockSpec(shape, lambda k, place: (0,) * len(shape))
 
-    def chip(k, place):
-        return lax.rem(place[0] + k, n_parts)
+    def across(height):
+        return pl.BlockSpec((height, wide), lambda k, place: (0, chip(k, place)))
 
     block = pl.BlockSpec((1, packed, z_cols), lambda k, place: (k, 0, 0))
-    rows_grad, align = pl.pallas_call(
-        align_kernel,
+    rows_grad, terms, pieces = pl.pallas_call(
+        columns_kernel,
         grid_spec=pltpu.PrefetchScalarGridSpec(
             num_scalar_prefetch=1,
             grid=(n_parts,),
             in_specs=[
-                fixed(packed, width),
+                fixed(packed + rank, width),
                 fixed(packed, rank),
                 pl.BlockSpec((wide, width), lambda k, place: (chip(k, place), 0)),
-                pl.BlockSpec((rank, wide), lambda k, place: (0, chip(k, place))),
+                across(rank),
+                across(rank),
                 block,
                 block,
             ],
             out_specs=[
-                pl.BlockSpec((packed, wide), lambda k, place: (0, chip(k, place))),
-                pl.BlockSpec((1, wide), lambda k, place: (0, chip(k, place))),
+                across(packed),
+                across(2),
+                pl.BlockSpec(
+                    (NX, 1, 2 * rank, g_cols), lambda k, place: (0, chip(k, place), 0, 0)
+                ),
             ],
         ),
         out_shape=[
             jax.ShapeDtypeStruct((packed, out_width), BF),
-            jax.ShapeDtypeStruct((1, out_width), F32),
+            jax.ShapeDtypeStruct((2, out_width), F32),
+            jax.ShapeDtypeStruct((NX, n_parts, 2 * rank, g_cols), BF),
         ],
-        compiler_params=pltpu.CompilerParams(vmem_limit_bytes=32 * 2**20),
+        compiler_params=pltpu.CompilerParams(vmem_limit_bytes=40 * 2**20),
         cost_estimate=pl.CostEstimate(
             flops=2 * packed * out_width * width,
             bytes_accessed=2 * out_width * (2 * packed + width),
             transcendentals=0,
         ),
-        name="align_columns",
-    )(jnp.stack([my_part, my_core]).astype(jnp.int32), rows_in, rows_low, weight, second, mine, other)
-
-    products = natural(first_weight + gram_second)
-    products = products.astype(BF)
-    pieces = jnp.stack(
-        [lanes(products[:, i : i + t_cols]) for i in range(0, out_width, t_cols)], axis=0
-    )
-    terms = jnp.concatenate([squares.reshape(-1, 128), align.reshape(-1, 128)], axis=0)
+        name="columns_sums",
+    )(
+        jnp.stack([my_part, my_core]).astype(jnp.int32),
+        left,
+        rows_low,
+        weight,
+        second,
+        gram_second,
+        mine,
+        other,
+    )
+
+    terms = terms.astype(BF).reshape(-1, g_cols)
     n_terms = terms.shape[0]
-    terms = summed(jnp.concatenate([to_all(terms.astype(BF)), pieces], axis=1))
+    pieces = pieces.reshape(shards, 2 * rank, g_cols)
+    terms = summed(jnp.concatenate([to_all(terms), pieces], axis=1))
+    squares, align = terms[: n_terms // 2], terms[n_terms // 2 : n_terms]
     merged_t = unlanes(terms[n_terms:], rank)
-    squares, align = terms[: n_terms // 2], terms[n_terms // 2 : n_terms]
     norm = jnp.sqrt(squares + EPSILON)
     scale = gain / norm
     shrink = gain * align / (norm * norm * norm)

time: 186 us -> 186 us (level)
  starting transfers between devices: 58.5 us -> 55.2 us
  Pallas kernels: 5.35 us -> 7.68 us
  waiting for transfers between devices: 61.1 us -> 63.1 us
    all_to_all x4, starting transfers between devices: 32.6 us -> 29.9 us  [exchange(): lax.all_to_all(values, axis, split_axis=0, concat_axis=0, tiled=True, axi...]
    pallas_call x1, Pallas kernels: 5.35 us -> 7.68 us  [on_device(): pl.pallas_call(columns_kernel, grid_spec=pltpu.PrefetchScalarGridSpec(num...]
    dot_general x13 -> x12, matrix products: 15.5 us -> 13.9 us  [dot(): lax.dot_general(left, right, (dims, ((), ())), precision=precision, prefe...]
    unnamed x38 -> x39, local copies, waits for them, and re-layouts: 5.44 us -> 5.48 us
  transfers between devices with their start and end apart: 10 -> 10, of which waited for: 5 -> 6; matrix products, arithmetic and copies ran while one was open for 11% -> 9% of each run, Pallas kernels for 3% -> 4%
where the time goes in v5:
time: 186 us; the launch traced here: 185 us
  waiting for transfers between devices  63.1 us (34%)
  starting transfers between devices  55.2 us (30%)
  local copies, waits for them, and re-layouts  15.2 us (8%)
  between operations  14.5 us (8%)
  matrix products  13.9 us (7%)
  blocking collectives  11.7 us (6%)
  Pallas kernels  7.68 us (4%)
  other arithmetic  3.36 us (2%)
    all_to_all x4, waiting for transfers between devices, exchange(): lax.all_to_all(values, axis, split_axis=0, concat_axis=0, tiled=True, axi...  53.4 us
    all_to_all x4, starting transfers between devices, exchange(): lax.all_to_all(values, axis, split_axis=0, concat_axis=0, tiled=True, axi...  29.9 us
    dot_general x12, matrix products, dot(): lax.dot_general(left, right, (dims, ((), ())), precision=precision, prefe...  13.9 us
    ppermute x4, starting transfers between devices, along_y(): return lax.ppermute(values, 'tp', pairs)  13.7 us
    all_to_all x1, blocking collectives, exchange(): lax.all_to_all(values, axis, split_axis=0, concat_axis=0, tiled=True, axi...  11.7 us
    ppermute x1, starting transfers between devices, on_device(): other = lax.ppermute(mine, 'tp', [(i, i ^ 1) for i in range(shards)])  11.6 us
    ppermute x4, waiting for transfers between devices, along_y(): return lax.ppermute(values, 'tp', pairs)  9.72 us
    pallas_call x1, Pallas kernels, on_device(): pl.pallas_call(columns_kernel, grid_spec=pltpu.PrefetchScalarGridSpec(num...  7.68 us
  transfers between devices with their start and end apart: 10, of which 6 were waited for; matrix products, arithmetic and copies ran while one was open for 9% of the time, Pallas kernels for 4%

profile of v5, /device:TPU:1, one launch (start us, length us, event | category | flops | bytes accessed | tf_op | source)
XLA Modules:
  0.0 184.6 jit_solution(13770810300087996239)
XLA Ops:
  7.2 0.0 all-gather.2.cloned.1.call-start
  7.3 1.1 copy.44
  8.4 11.7 %all_to_all.25 = bf16[4,128,512]{2,1,0:T(8,128)(2,1)} all-to-all(bf16[4,128,512]{2,1,0:T(8,128)(2,1)S(1)} %broadcast_in_dim.12), channel_id=1, replica_groups={{0,128,256,384},{16,144,272,400},{32,160,288,416},{48,176,304,432},{64,..., dimensions={0} | all-to-all | bytes 1048576 | tf_op jit(solution)/shard_map/all_to_all | solution.py:79
  20.1 0.0 all-gather.2.cloned.1.call-update
  20.1 0.7 copy.42
  20.8 0.0 copy-start.12
  20.8 0.1 copy.41
  20.9 0.1 reduce.1
  21.1 0.1 copy.43
  21.2 0.1 select_reduce_fusion
  21.4 0.4 convolution_convert_fusion
  21.7 1.2 reshape.110
  22.9 12.7 %all-to-all-start.1 = ((bf16[32,12,1024]{2,1,0:T(8,128)(2,1)}), bf16[32,12,1024]{2,1,0:T(8,128)(2,1)S(1)}, u32[]{:S(2)}, u32[]{:S(2)}) async-start(bf16[32,12,1024]{2,1,0:T(8,128)(2,1)} %reshape.110), calls=%async_computation.1 | async-start | bytes 2097152 | tf_op jit(solution)/shard_map/all_to_all | solution.py:79
  35.7 0.7 copy-done.7
  36.4 0.1 copy.47
  36.5 0.2 reshape.112.narrow
  36.7 0.0 copy-start.10
  36.7 0.1 fusion.27
  36.8 0.4 fusion.50.gram_second
  37.2 27.2 %all-to-all-done.1 = bf16[32,12,1024]{2,1,0:T(8,128)(2,1)S(1)} async-done(((bf16[32,12,1024]{2,1,0:T(8,128)(2,1)}), bf16[32,12,1024]{2,1,0:T(8,128)(2,1)S(1)}, u32[]{:S(2)}, u32[]{:S(2)}) %all-to-all-start.1) | async-done | bytes 786464 | tf_op jit(solution)/shard_map/all_to_all | solution.py:79
  64.4 0.2 reshape.111
  64.6 0.1 fusion.46
  64.7 3.2 %collective-permute-start.3 = (bf16[384,512]{1,0:T(8,128)(2,1)S(1)}, bf16[384,512]{1,0:T(8,128)(2,1)S(1)}, u32[]{:S(2)}, u32[]{:S(2)}) collective-permute-start(bf16[384,512]{1,0:T(8,128)(2,1)S(1)} %get-tuple-element.30), channel_id=1, source_target_pairs={{14,0},{15,1},{0,2},{1,3},{2,4},{3,5},{4,6},{5,7},{6,8},{7,9},{8,1... | collective-permute-start | bytes 1179656 | tf_op jit(solution)/shard_map/ppermute | solution.py:113
  67.9 4.3 %collective-permute-start = (bf16[384,512]{1,0:T(8,128)(2,1)S(1)}, bf16[384,512]{1,0:T(8,128)(2,1)S(1)}, u32[]{:S(2)}, u32[]{:S(2)}) collective-permute-start(bf16[384,512]{1,0:T(8,128)(2,1)S(1)} %get-tuple-element.30), channel_id=1, source_target_pairs={{2,0},{3,1},{4,2},{5,3},{6,4},{7,5},{8,6},{9,7},{10,8},{11,9},{12,... | collective-permute-start | bytes 1179656 | tf_op jit(solution)/shard_map/ppermute | solution.py:113
  72.2 3.9 %collective-permute-start.1 = (bf16[192,512]{1,0:T(8,128)(2,1)S(1)}, bf16[192,512]{1,0:T(8,128)(2,1)S(1)}, u32[]{:S(2)}, u32[]{:S(2)}) collective-permute-start(bf16[192,512]{1,0:T(8,128)(2,1)S(1)} %get-tuple-element.31), channel_id=1, source_target_pairs={{4,0},{5,1},{6,2},{7,3},{8,4},{9,5},{10,6},{11,7},{12,8},{13,9},{1... | collective-permute-start | bytes 589832 | tf_op jit(solution)/shard_map/ppermute | solution.py:113
  76.2 2.3 %collective-permute-start.2 = (bf16[192,512]{1,0:T(8,128)(2,1)S(1)}, bf16[192,512]{1,0:T(8,128)(2,1)S(1)}, u32[]{:S(2)}, u32[]{:S(2)}) collective-permute-start(bf16[192,512]{1,0:T(8,128)(2,1)S(1)} %get-tuple-element.32), channel_id=1, source_target_pairs={{12,0},{13,1},{14,2},{15,3},{0,4},{1,5},{2,6},{3,7},{4,8},{5,9},{6... | collective-permute-start | bytes 589832 | tf_op jit(solution)/shard_map/ppermute | solution.py:113
  78.5 0.2 convolution_convert_fusion.2.rows_low
  78.7 1.3 collective-permute-done.1
  80.1 8.4 %collective-permute-done.2 = bf16[192,512]{1,0:T(8,128)(2,1)S(1)} collective-permute-done((bf16[192,512]{1,0:T(8,128)(2,1)S(1)}, bf16[192,512]{1,0:T(8,128)(2,1)S(1)}, u32[]{:S(2)}, u32[]{:S(2)}) %collective-permute-start.2) | collective-permute-done | bytes 196640 | tf_op jit(solution)/shard_map/ppermute | solution.py:113
  88.5 0.2 pad_maximum_fusion.mine
  88.7 11.6 %collective-permute-start.4 = (bf16[4,384,512]{2,1,0:T(8,128)(2,1)S(1)}, bf16[4,384,512]{2,1,0:T(8,128)(2,1)}, u32[]{:S(2)}, u32[]{:S(2)}) collective-permute-start(bf16[4,384,512]{2,1,0:T(8,128)(2,1)S(1)} %pad_maximum_fusion.mine), channel_id=1, source_target_pairs={{0,1},{1,0},{2,3},{3,2},{4,5},{5,4},{6,7},{7,6},{8,9},{9,8},{10,11... | collective-permute-start | bytes 4718600 | tf_op jit(solution)/shard_map/ppermute | solution.py:131
  100.3 0.1 pad_maximum_fusion.3
  100.4 0.1 copy.49
  100.5 0.8 broadcast_in_dim.16
  101.3 4.6 %all-to-all-start.4 = ((bf16[16,96,128]{2,1,0:T(8,128)(2,1)}), bf16[16,96,128]{2,1,0:T(8,128)(2,1)S(1)}, u32[]{:S(2)}, u32[]{:S(2)}) async-start(bf16[16,96,128]{2,1,0:T(8,128)(2,1)} %broadcast_in_dim.16), calls=%async_computation.4 | async-start | bytes 786432 | tf_op jit(solution)/shard_map/all_to_all | solution.py:79
  106.0 0.1 pad_add_fusion.place
  106.0 2.2 %copy-done = bf16[4096,512]{1,0:T(8,128)(2,1)S(1)} copy-done((bf16[4096,512]{1,0:T(8,128)(2,1)S(1)}, bf16[4096,512]{1,0:T(8,128)(2,1)}, u32[]{:S(2)}) %copy-start) | copy-done | bytes 4194328
  108.2 7.7 %columns_sums.1 = (bf16[384,4096]{1,0:T(8,128)(2,1)S(1)}, f32[2,4096]{1,0:T(2,128)S(1)}, bf16[4,4,64,128]{3,2,1,0:T(8,128)(2,1)S(1)}) custom-call(s32[2]{0:T(128)S(1)} %pad_add_fusion.place, bf16[416,512]{1,0:T(8,128)(2,1)S(1)} %pad_maximum_fusion.2.left, bf16[384,32]{1,0:T(8,128)(2,1)S(1)} %convolution_convert_fusion.2.rows_low, ...), custom_call_target="tpu_custom_call" | custom-call | flops 1610612736 | bytes 10485760 | tf_op jit(solution)/shard_map/columns_sums/pallas_call | solution.py:163
  115.9 1.7 copy-done.2
  117.7 0.9 pad_maximum_fusion.1
  118.5 2.0 %all-to-all-done.4 = bf16[16,96,128]{2,1,0:T(8,128)(2,1)S(1)} async-done(((bf16[16,96,128]{2,1,0:T(8,128)(2,1)}), bf16[16,96,128]{2,1,0:T(8,128)(2,1)S(1)}, u32[]{:S(2)}, u32[]{:S(2)}) %all-to-all-start.4) | async-done | bytes 393248 | tf_op jit(solution)/shard_map/all_to_all | solution.py:79
  120.5 5.3 %all-to-all-start.2 = ((bf16[16,128,128]{2,1,0:T(8,128)(2,1)}), bf16[16,128,128]{2,1,0:T(8,128)(2,1)}, u32[]{:S(2)}, u32[]{:S(2)}) async-start(bf16[16,128,128]{2,1,0:T(8,128)(2,1)} %pad_maximum_fusion.1), calls=%async_computation.2 | async-start | bytes 1048576 | tf_op jit(solution)/shard_map/all_to_all | solution.py:79
  125.8 0.7 copy.48
  126.5 0.1 reduce
  126.6 0.6 fusion.49
  127.2 1.8 constant_dynamic-slice_fusion.3
  128.9 14.3 %all-to-all-done.2 = bf16[16,128,128]{2,1,0:T(8,128)(2,1)} async-done(((bf16[16,128,128]{2,1,0:T(8,128)(2,1)}), bf16[16,128,128]{2,1,0:T(8,128)(2,1)}, u32[]{:S(2)}, u32[]{:S(2)}) %all-to-all-start.2) | async-done | bytes 524320 | tf_op jit(solution)/shard_map/all_to_all | solution.py:79
  143.2 1.1 convert_reduce_fusion
  144.3 0.6 slice_divide_fusion
  144.9 3.1 %fusion.6 = bf16[384,32]{0,1:T(8,128)(2,1)S(1)} fusion(bf16[32,4096]{1,0:T(8,128)(2,1)S(1)} %reshape.112.narrow, bf16[384,4096]{1,0:T(8,128)(2,1)} %copy-done.2, f32[4096]{0:T(1024)S(1)} %bitcast.113), kind=kOutput, calls=%fused_computation.14 | convolution fusion | flops 105394176 | bytes 3448832 | tf_op jit(solution)/shard_map/dot_general | solution.py:16
  148.0 0.0 copy-done.11
  148.0 0.3 fusion.25
  148.3 2.6 %fusion.3 = bf16[384,512]{1,0:T(8,128)(2,1)} fusion(f32[384,512]{1,0:T(8,128)S(1)} %fusion.25, bf16[4096,512]{1,0:T(8,128)(2,1)S(1)} %copy-done.1, bf16[384,4096]{1,0:T(8,128)(2,1)S(1)} %copy-done.3, f32[4096]{0:T(1024)S(1)} %bitcast.114), kind=kOutput, calls=%fused_computation.6 | convolution fusion | flops 1615724544 | bytes 8536064 | tf_op jit(solution)/shard_map/dot_general | solution.py:16
  150.9 1.9 %reshape.117 = bf16[32,12,512]{2,1,0:T(8,128)(2,1)} reshape(bf16[384,512]{1,0:T(8,128)(2,1)} %fusion.3) | data formatting | bytes 786432 | tf_op jit(solution)/shard_map/reshape | solution.py:84
  152.8 7.4 %all-to-all-start.3 = ((bf16[32,12,512]{2,1,0:T(8,128)(2,1)}), bf16[32,12,512]{2,1,0:T(8,128)(2,1)S(1)}, u32[]{:S(2)}, u32[]{:S(2)}) async-start(bf16[32,12,512]{2,1,0:T(8,128)(2,1)} %reshape.117), calls=%async_computation.3 | async-start | bytes 1048576 | tf_op jit(solution)/shard_map/all_to_all | solution.py:79
  160.2 1.8 fusion.8
  162.0 0.6 copy.52
  162.6 3.0 %convolution_bitcast_fusion.1 = f32[512,32]{0,1:T(8,128)S(1)} fusion(bf16[4096,512]{1,0:T(8,128)(2,1)} %all-gather.2.cloned.1.call-done.weight, bf16[32,4096]{1,0:T(8,128)(2,1)S(1)} %reshape.112.narrow, f32[4096]{0:T(1024)S(1)} %bitcast.107), kind=kOutput, calls=%fused_computation.13 | convolution fusion | flops 134610944 | bytes 4538368 | tf_op jit(solution)/shard_map/dot_general | solution.py:16
  165.6 0.2 convolution_subtract_fusion
  165.8 0.0 copy-done.8
  165.8 1.1 fusion.5
  166.8 9.9 %all-to-all-done.3 = bf16[32,12,512]{2,1,0:T(8,128)(2,1)S(1)} async-done(((bf16[32,12,512]{2,1,0:T(8,128)(2,1)}), bf16[32,12,512]{2,1,0:T(8,128)(2,1)S(1)}, u32[]{:S(2)}, u32[]{:S(2)}) %all-to-all-start.3) | async-done | bytes 393248 | tf_op jit(solution)/shard_map/all_to_all | solution.py:79
  176.7 0.1 reshape.118
  176.8 0.9 convolution_convert_fusion.1
  (49 shorter events, 0.4 us)
Async XLA Ops:
  7.2 12.9 %copy-start.6 = (bf16[128,4096]{1,0:T(8,128)(2,1)S(1)}, bf16[128,4096]{1,0:T(8,128)(2,1)}, u32[]{:S(2)}) copy-start(bf16[128,4096]{1,0:T(8,128)(2,1)} %param.9) | copy-start | bytes 3145732
  7.2 13.6 %copy-start.16 = (s32[1,24]{1,0:T(1,128)S(1)}, s32[1,24]{1,0:T(1,128)}, u32[]{:S(2)}) copy-start(s32[1,24]{1,0:T(1,128)} %param.10) | copy-start | bytes 292
  7.2 13.9 %copy-start.13 = (bf16[128,512]{1,0:T(8,128)(2,1)S(1)}, bf16[128,512]{1,0:T(8,128)(2,1)}, u32[]{:S(2)}) copy-start(bf16[128,512]{1,0:T(8,128)(2,1)} %param.8) | copy-start | bytes 393220
  7.2 14.0 %copy-start.17 = (s32[24]{0:T(128)S(1)}, s32[24]{0:T(128)}, u32[]{:S(2)}) copy-start(s32[24]{0:T(128)} %param.11) | copy-start | bytes 292
  7.2 98.8 %all-gather.2.cloned.1.call-start = ((), (), s32[]{:S(2)}) async-start(), calls=%async_computation.5 | async-start | bytes 4718592 | tf_op jit(solution)/shard_map/all_gather | solution.py:97
  20.8 14.8 %copy-start.12 = (bf16[1,32,4096]{2,1,0:T(8,128)(2,1)S(1)}, bf16[1,32,4096]{2,1,0:T(8,128)(2,1)}, u32[]{:S(2)}) copy-start(bf16[1,32,4096]{2,1,0:T(8,128)(2,1)} %param.14) | copy-start | bytes 786436
  21.3 15.3 %copy-start.14 = (s32[128]{0:T(128)}, s32[128]{0:T(128)S(1)}, u32[]{:S(2)}) copy-start(s32[128]{0:T(128)S(1)} %iota_add_fusion) | copy-start | bytes 1540
  21.4 15.3 %copy-start.9 = (bf16[1,512,32]{1,2,0:T(8,128)(2,1)S(1)}, bf16[1,512,32]{1,2,0:T(8,128)(2,1)}, u32[]{:S(2)}) copy-start(bf16[1,512,32]{1,2,0:T(8,128)(2,1)} %param.13) | copy-start | bytes 98308
  22.9 41.5 %all-to-all-start.1 = ((bf16[32,12,1024]{2,1,0:T(8,128)(2,1)}), bf16[32,12,1024]{2,1,0:T(8,128)(2,1)S(1)}, u32[]{:S(2)}, u32[]{:S(2)}) async-start(bf16[32,12,1024]{2,1,0:T(8,128)(2,1)} %reshape.110), calls=%async_computation.1 | async-start | bytes 2097152 | tf_op jit(solution)/shard_map/all_to_all | solution.py:79
  35.7 0.7 copy-start.7
  36.7 41.8 %copy-start.10 = (bf16[1,512,32]{1,2,0:T(8,128)(2,1)S(1)}, bf16[1,512,32]{1,2,0:T(8,128)(2,1)}, u32[]{:S(2)}) copy-start(bf16[1,512,32]{1,2,0:T(8,128)(2,1)} %param.13) | copy-start | bytes 98308
  64.6 23.9 %copy-start.4 = (bf16[384,1024]{1,0:T(8,128)(2,1)}, bf16[384,1024]{1,0:T(8,128)(2,1)S(1)}, u32[]{:S(2)}) copy-start(bf16[384,1024]{1,0:T(8,128)(2,1)S(1)} %reshape.111) | copy-start | bytes 2359300
  64.7 23.8 %collective-permute-start.3 = (bf16[384,512]{1,0:T(8,128)(2,1)S(1)}, bf16[384,512]{1,0:T(8,128)(2,1)S(1)}, u32[]{:S(2)}, u32[]{:S(2)}) collective-permute-start(bf16[384,512]{1,0:T(8,128)(2,1)S(1)} %get-tuple-element.30), channel_id=1, source_target_pairs={{14,0},{15,1},{0,2},{1,3},{2,4},{3,5},{4,6},{5,7},{6,8},{7,9},{8,1... | collective-permute-start | bytes 1179656 | tf_op jit(solution)/shard_map/ppermute | solution.py:113
  67.9 20.6 %collective-permute-start = (bf16[384,512]{1,0:T(8,128)(2,1)S(1)}, bf16[384,512]{1,0:T(8,128)(2,1)S(1)}, u32[]{:S(2)}, u32[]{:S(2)}) collective-permute-start(bf16[384,512]{1,0:T(8,128)(2,1)S(1)} %get-tuple-element.30), channel_id=1, source_target_pairs={{2,0},{3,1},{4,2},{5,3},{6,4},{7,5},{8,6},{9,7},{10,8},{11,9},{12,... | collective-permute-start | bytes 1179656 | tf_op jit(solution)/shard_map/ppermute | solution.py:113
  72.2 7.8 %collective-permute-start.1 = (bf16[192,512]{1,0:T(8,128)(2,1)S(1)}, bf16[192,512]{1,0:T(8,128)(2,1)S(1)}, u32[]{:S(2)}, u32[]{:S(2)}) collective-permute-start(bf16[192,512]{1,0:T(8,128)(2,1)S(1)} %get-tuple-element.31), channel_id=1, source_target_pairs={{4,0},{5,1},{6,2},{7,3},{8,4},{9,5},{10,6},{11,7},{12,8},{13,9},{1... | collective-permute-start | bytes 589832 | tf_op jit(solution)/shard_map/ppermute | solution.py:113
  76.2 12.3 %collective-permute-start.2 = (bf16[192,512]{1,0:T(8,128)(2,1)S(1)}, bf16[192,512]{1,0:T(8,128)(2,1)S(1)}, u32[]{:S(2)}, u32[]{:S(2)}) collective-permute-start(bf16[192,512]{1,0:T(8,128)(2,1)S(1)} %get-tuple-element.32), channel_id=1, source_target_pairs={{12,0},{13,1},{14,2},{15,3},{0,4},{1,5},{2,6},{3,7},{4,8},{5,9},{6... | collective-permute-start | bytes 589832 | tf_op jit(solution)/shard_map/ppermute | solution.py:113
  88.7 17.3 %collective-permute-start.4 = (bf16[4,384,512]{2,1,0:T(8,128)(2,1)S(1)}, bf16[4,384,512]{2,1,0:T(8,128)(2,1)}, u32[]{:S(2)}, u32[]{:S(2)}) collective-permute-start(bf16[4,384,512]{2,1,0:T(8,128)(2,1)S(1)} %pad_maximum_fusion.mine), channel_id=1, source_target_pairs={{0,1},{1,0},{2,3},{3,2},{4,5},{5,4},{6,7},{7,6},{8,9},{9,8},{10,11... | collective-permute-start | bytes 4718600 | tf_op jit(solution)/shard_map/ppermute | solution.py:131
  101.3 19.2 %all-to-all-start.4 = ((bf16[16,96,128]{2,1,0:T(8,128)(2,1)}), bf16[16,96,128]{2,1,0:T(8,128)(2,1)S(1)}, u32[]{:S(2)}, u32[]{:S(2)}) async-start(bf16[16,96,128]{2,1,0:T(8,128)(2,1)} %broadcast_in_dim.16), calls=%async_computation.4 | async-start | bytes 786432 | tf_op jit(solution)/shard_map/all_to_all | solution.py:79
  106.0 2.2 %copy-start = (bf16[4096,512]{1,0:T(8,128)(2,1)S(1)}, bf16[4096,512]{1,0:T(8,128)(2,1)}, u32[]{:S(2)}) copy-start(bf16[4096,512]{1,0:T(8,128)(2,1)} %all-gather.2.cloned.1.call-done.weight) | copy-start | bytes 12582916
  115.9 1.7 copy-start.2
  120.5 22.7 %all-to-all-start.2 = ((bf16[16,128,128]{2,1,0:T(8,128)(2,1)}), bf16[16,128,128]{2,1,0:T(8,128)(2,1)}, u32[]{:S(2)}, u32[]{:S(2)}) async-start(bf16[16,128,128]{2,1,0:T(8,128)(2,1)} %pad_maximum_fusion.1), calls=%async_computation.2 | async-start | bytes 1048576 | tf_op jit(solution)/shard_map/all_to_all | solution.py:79
  127.2 21.2 %copy-start.3 = (bf16[384,4096]{1,0:T(8,128)(2,1)S(1)}, bf16[384,4096]{1,0:T(8,128)(2,1)}, u32[]{:S(2)}) copy-start(bf16[384,4096]{1,0:T(8,128)(2,1)} %copy-done.2) | copy-start | bytes 9437188
  128.9 19.1 %copy-start.11 = (bf16[1,512,32]{1,2,0:T(8,128)(2,1)S(1)}, bf16[1,512,32]{1,2,0:T(8,128)(2,1)}, u32[]{:S(2)}) copy-start(bf16[1,512,32]{1,2,0:T(8,128)(2,1)} %param.13) | copy-start | bytes 98308
  144.9 3.4 %copy-start.1 = (bf16[4096,512]{1,0:T(8,128)(2,1)S(1)}, bf16[4096,512]{1,0:T(8,128)(2,1)}, u32[]{:S(2)}) copy-start(bf16[4096,512]{1,0:T(8,128)(2,1)} %all-gather.2.cloned.1.call-done.weight) | copy-start | bytes 12582916
  152.8 12.8 %copy-start.5 = (bf16[384,1024]{1,0:T(8,128)(2,1)S(1)}, bf16[384,1024]{1,0:T(8,128)(2,1)}, u32[]{:S(2)}) copy-start(bf16[384,1024]{1,0:T(8,128)(2,1)} %copy-done.4) | copy-start | bytes 2359300
  152.8 13.0 %copy-start.8 = (bf16[4,8,32,128]{3,2,1,0:T(8,128)(2,1)S(1)}, bf16[4,8,32,128]{3,2,1,0:T(8,128)(2,1)}, u32[]{:S(2)}) copy-start(bf16[4,8,32,128]{3,2,1,0:T(8,128)(2,1)} %copy-done.7) | copy-start | bytes 786436
  152.8 23.9 %all-to-all-start.3 = ((bf16[32,12,512]{2,1,0:T(8,128)(2,1)}), bf16[32,12,512]{2,1,0:T(8,128)(2,1)S(1)}, u32[]{:S(2)}, u32[]{:S(2)}) async-start(bf16[32,12,512]{2,1,0:T(8,128)(2,1)} %reshape.117), calls=%async_computation.3 | async-start | bytes 1048576 | tf_op jit(solution)/shard_map/all_to_all | solution.py:79
  162.6 14.3 %copy-start.15 = (s32[128]{0:T(128)S(1)}, s32[128]{0:T(128)}, u32[]{:S(2)}) copy-start(s32[128]{0:T(128)} %copy-done.14) | copy-start | bytes 1540
Sparse Core Ops, SparseCore 0:
  20.2 81.5 all-gather.1
